TPU v7x, 32 devices: a whole 2x2x4 slice. The times are simulated.
32 devices in a mesh: pipe: 2 (over core), dp: 16 (over z, y, x).
Axes of the slice: x: 2, y: 2, z: 4, core: 2. Of those that a mesh axis runs over, the one named last changes fastest.
Arguments:
- images: bfloat16 [128, 16, 16, 1024], P('dp'), may hold values from -25 to 25
- extents: int32 [128, 2], P('dp'), may hold values from 8 to 16, as said below
- views: int32 [128], P('dp'), may hold values from 0 to 1, as said below
- params: bfloat16 [2, 6029312], P('pipe'), may hold values from -0.1875 to 0.1875
- norms: float32 [2, 2, 5120], P('pipe'), may hold values from -2 to 2, as said below
- cotangent: bfloat16 [128, 8, 8, 2048], P('dp'), may hold values from -6 to 6
Outputs:
- boundary: bfloat16 [2, 128, 262144], P('pipe', 'dp')
- weight_grads: float32 [2, 6029312], P('pipe')
- norm_grads: float32 [2, 2, 5120], P('pipe')
Inputs may be any that keep to these rules, and one draw needn't show every extreme that they name: `extents`: entry [i, 0] is image i's valid height and [i, 1] its valid width, even numbers from 8 to 16 and from 8 to 16; the valid region is the top-left corner. The first of every dp index's images is whole. Images 2 k and 2 k + 1 have different views. `norms`: gains lie in 0.5 to 1.5.
All inputs are finite; a program needn't handle non-finite values.
Results may differ from a plain program's by a relative error of at most 0.014.
Values may be sent and summed in bfloat16 or wider, within the bound.
No kernel may reach another device: no remote copies, remote signals or barrier semaphores. Data moves between devices by JAX's collectives and lax.ppermute only.
A program may use at most 384 MiB of HBM per device.

v0:
```python
import functools

import jax
import jax.numpy as jnp
from jax import lax
from jax.experimental import pallas as pl
from jax.experimental.pallas import tpu as pltpu
from jax.sharding import PartitionSpec as P

C0 = 1024
M0 = 256
M1 = 512
C1 = 2048
HB = 16
WB = 16
P_SIZE = 6029312
CN = 5120
WORK = 4
PIX0 = 256
PIX1 = 64
ROWS0 = WORK * PIX0
ROWS1 = WORK * PIX1
EPSILON = 1e-05
MIB = 1 << 20

F32 = jnp.float32
BF16 = jnp.bfloat16
CORE, PLANE, LEVEL, HIGH, WIDE = 4, 5, 6, 7, 11


def shape_of(dims, kind):
    return jax.ShapeDtypeStruct(dims, kind)


def hbm_of(dims, kind):
    return pltpu.HBM(dims, kind)


def dot_nn(left, right):
    return lax.dot_general(left, right, (((1,), (0,)), ((), ())), preferred_element_type=F32)


def dot_nt(left, right):
    return lax.dot_general(left, right, (((1,), (1,)), ((), ())), preferred_element_type=F32)


def dot_tn(left, right):
    return lax.dot_general(left, right, (((0,), (0,)), ((), ())), preferred_element_type=F32)


def over_lanes(column, width):
    return jnp.concatenate([column] * (width // 128), axis=1)


def pixel_mask(high, wide, breadth, rows):
    index = lax.broadcasted_iota(jnp.int32, (rows, 128), 0)
    row = (index >> (breadth.bit_length() - 1)).astype(F32)
    col = (index & (breadth - 1)).astype(F32)
    return jnp.where((row < high) & (col < wide), 1.0, 0.0)


def mask0(hw_ref, image):
    return pixel_mask(hw_ref[image : image + 1, :], hw_ref[4 + image : 5 + image, :], WB, PIX0)


def mask1(hw_ref, image):
    high, wide = hw_ref[image : image + 1, :] * 0.5, hw_ref[4 + image : 5 + image, :] * 0.5
    return pixel_mask(high, wide, WB // 2, PIX1)


def mask1_all(hw_ref, width):
    return over_lanes(jnp.concatenate([mask1(hw_ref, k) for k in range(WORK)], axis=0), width)


def sigmoid(values):
    return 1.0 / (1.0 + jnp.exp(-values))


def silu(values):
    return values * sigmoid(values)


def slope(values):
    sig = sigmoid(values)
    return sig * (1.0 + values * (1.0 - sig))


def total_rows(values):
    return jnp.sum(values, axis=0, keepdims=True)


def put_sums(ref, first, second):
    ref[0:1, :] = total_rows(first)
    ref[1:2, :] = total_rows(second)


def plane_total(refs):
    return (refs[0][...] + refs[1][...]) + (refs[2][...] + refs[3][...])


def mean_scale(table, count):
    mean = table[0:1, :] / count
    spread = table[1:2, :] / count - mean * mean
    return mean, lax.rsqrt(spread + EPSILON)


def count_of(tot_ref):
    return tot_ref[0:1, M0 : M0 + 1]


def side_columns(values, breadth):
    rows, width = values.shape
    column = lax.broadcasted_iota(jnp.int32, (rows, width), 0) & (breadth - 1)
    left = jnp.where(column == 0, 0.0, pltpu.roll(values, 1, 0))
    right = jnp.where(column == breadth - 1, 0.0, pltpu.roll(values, rows - 1, 0))
    return left, right


def later_rows(values, step, height, breadth):
    if step == 0:
        return values
    rows, width = values.shape
    images = values.reshape(rows // (height * breadth), height * breadth, width)
    gap = jnp.zeros((images.shape[0], breadth, width), values.dtype)
    if step > 0:
        moved = jnp.concatenate([gap, images[:, :-breadth]], axis=1)
    else:
        moved = jnp.concatenate([images[:, breadth:], gap], axis=1)
    return moved.reshape(rows, width)


def even_picker():
    row = lax.broadcasted_iota(jnp.int32, (PIX1, PIX0), 0)
    col = lax.broadcasted_iota(jnp.int32, (PIX1, PIX0), 1)
    return jnp.where(col == 32 * (row >> 3) + 2 * (row & 7), 1.0, 0.0).astype(BF16)


def even_placer():
    row = lax.broadcasted_iota(jnp.int32, (PIX0, PIX1), 0)
    col = lax.broadcasted_iota(jnp.int32, (PIX0, PIX1), 1)
    return jnp.where(row == 32 * (col >> 3) + 2 * (col & 7), 1.0, 0.0).astype(BF16)


def placed(values):
    placer = even_placer()
    high = values.astype(BF16)
    rest = (values - high.astype(F32)).astype(BF16)
    return dot_nn(placer, high) + dot_nn(placer, rest)


def call(body, outs, grid, in_specs, out_specs, scratch=(), limit=28, aliases={}, micros=5):
    size = int(micros * 3.6e6)
    return pl.pallas_call(
        body,
        out_shape=outs,
        grid_spec=pltpu.PrefetchScalarGridSpec(
            num_scalar_prefetch=1,
            grid=grid,
            in_specs=in_specs,
            out_specs=out_specs,
            scratch_shapes=list(scratch),
        ),
        input_output_aliases=aliases,
        cost_estimate=pl.CostEstimate(flops=0, bytes_accessed=size, transcendentals=0),
        compiler_params=pltpu.CompilerParams(vmem_limit_bytes=limit * MIB),
    )


ANYWHERE = pl.BlockSpec(memory_space=pltpu.HBM)
DMA = pltpu.SemaphoreType.DMA


def in_hbm(array):
    return pltpu.with_memory_space_constraint(array, pltpu.HBM)


def vmem(*dims):
    return pltpu.VMEM(dims, BF16)


def full(*dims):
    return pl.BlockSpec(dims, lambda *_: (0,) * len(dims), pipeline_mode=pl.Buffered(1))


def per_image(*dims):
    return pl.BlockSpec((1,) + dims, lambda s, meta: (s,) + (0,) * len(dims))


def own_image(*dims):
    return pl.BlockSpec((1,) + dims, lambda s, meta: (meta[s],) + (0,) * len(dims))


def single(body, meta, ins, outs, scratch=(), limit=28, micros=5):
    in_specs = [ANYWHERE if whole else full(*array.shape) for array, whole in ins]
    shapes = [(hbm_of if far else shape_of)(dims, kind) for dims, kind, far in outs]
    out_specs = [full(*dims) for dims, _, _ in outs]
    made = call(body, shapes, (1,), in_specs, out_specs, scratch, limit, micros=micros)
    return made(meta, *[array for array, _ in ins])


def near(*arrays):
    return [(array, False) for array in arrays]


def far(*arrays):
    return [(in_hbm(array), False) for array in arrays]


def weight(pair):
    return [(array, True) for array in pair]


W1 = (0, 0, C0, M0)
W2 = (0, 0, 9 * M0, M0)
W3 = (0, 2304, M0, C0)
V1 = (1, 0, C0, M1)
VS = (1, 2048, C0, C1)
V2 = (1, 0, 9 * M1, M1)
V3 = (1, 9216, M1, C1)


def fetch(meta, weight, own_ref, got_ref, here, sem, rows=None, cols=None):
    owner, base, height, width = weight
    first, some = rows or (0, height)
    left, wide = cols or (0, width)

    def start(ref):
        for k in range(wide // 256):
            source = ref.at[pl.ds(base + (left // 256 + k) * height + first, some)]
            pltpu.make_async_copy(source, here.at[:, pl.ds(256 * k, 256)], sem).start()

    pl.when(meta[CORE] == owner)(functools.partial(start, own_ref))
    pl.when(meta[CORE] != owner)(functools.partial(start, got_ref))


def await_copy(here, sem):
    pltpu.make_async_copy(here, here, sem).wait()


def enter(meta, x_ref, cot_ref, wa_ref, wb_ref, *refs):
    pays, evens, cots, w_ref, sem = refs[0:4], refs[4:8], refs[8:12], refs[12], refs[13]
    step = pl.program_id(0)

    @pl.when(step == 0)
    def _():
        fetch(meta, W1, wa_ref, wb_ref, w_ref, sem)
        await_copy(w_ref, sem)

    x = x_ref[0].reshape(PIX0, C0)
    z = dot_nn(x, w_ref[...])
    even = dot_nn(even_picker(), x).astype(BF16)
    row = lax.broadcasted_iota(jnp.int32, (16, M0), 0)
    high, wide = meta[HIGH + step].astype(F32), meta[WIDE + step].astype(F32)
    sizes = jnp.where(row == 0, high, jnp.where(row == 1, wide, 0.0))
    middle = total_rows(z) * (1.0 / PIX0)
    rest = middle
    for k in range(3):
        part = rest.astype(BF16).astype(F32)
        sizes = jnp.where(row == 2 + k, part, sizes)
        rest = rest - part
    z = z - middle
    for k in range(WORK):

        @pl.when(step == k)
        def _(k=k):
            pays[k][0:PIX0, :] = z.astype(BF16)
            pays[k][PIX0 : PIX0 + 16, :] = sizes.astype(BF16)
            evens[k][...] = even
            cots[k][...] = cot_ref[0].reshape(PIX1, C1)


def arrive(meta, *refs):
    pays, z_ref, z_far_ref, hw_ref, st_ref = refs[0:4], *refs[4:]
    first, second, count = 0.0, 0.0, 0.0
    for k in range(WORK):
        rows = pays[k][PIX0 : PIX0 + 16, :].astype(F32)
        sizes = rows[:, 0:128]
        hw_ref[k : k + 1, :] = sizes[0:1, :]
        hw_ref[4 + k : 5 + k, :] = sizes[1:2, :]
        count = count + sizes[0:1, :] * sizes[1:2, :]
        z = pays[k][0:PIX0, :].astype(F32) + ((rows[2:3, :] + rows[3:4, :]) + rows[4:5, :])
        z_ref[k] = z
        z_far_ref[k] = z
        zm = z * over_lanes(pixel_mask(sizes[0:1, :], sizes[1:2, :], WB, PIX0), M0)
        first = first + total_rows(zm)
        second = second + total_rows(zm * z)
    st_ref[0:1, :] = jnp.concatenate([first, count], axis=1)
    st_ref[1:2, :] = jnp.concatenate([second, count], axis=1)


def front_two(meta, *refs):
    stats, (z_ref, hw_ref, n_ref, wa_ref, wb_ref) = refs[0:4], refs[4:9]
    tot_ref, a1_ref, z2_ref, z2b_ref, st_ref, w_ref, act_ref, sem = refs[9:]
    fetch(meta, W2, wa_ref, wb_ref, w_ref, sem)
    table = plane_total(stats)
    tot_ref[...] = table
    mean, scale = mean_scale(table[:, :M0], count_of(tot_ref))
    act_ref[:, 0:WB, :] = jnp.zeros((2, WB, 3 * M0), BF16)
    act_ref[:, WB + PIX0 : 2 * WB + PIX0, :] = jnp.zeros((2, WB, 3 * M0), BF16)
    first, second = 0.0, 0.0
    for k in range(WORK):
        mask = over_lanes(mask0(hw_ref, k), M0)
        pre = (z_ref[k] - mean) * scale * n_ref[0:1, :M0] + n_ref[1:2, :M0]
        act = silu(pre) * mask
        left, right = side_columns(act, WB)
        wide = jnp.concatenate([left, act, right], axis=1).astype(BF16)
        act_ref[k % 2, WB : WB + PIX0, :] = wide
        a1_ref[k] = wide[:, M0 : 2 * M0]
        if k == 0:
            await_copy(w_ref, sem)
        z2 = dot_nn(act_ref[k % 2, 0:PIX0, :], w_ref[0 : 3 * M0, :])
        z2 = z2 + dot_nn(wide, w_ref[3 * M0 : 6 * M0, :])
        z2 = z2 + dot_nn(act_ref[k % 2, 2 * WB : 2 * WB + PIX0, :], w_ref[6 * M0 :, :])
        z2_ref[k] = z2
        z2b_ref[k] = z2
        zm = z2 * mask
        first = first + total_rows(zm)
        second = second + total_rows(zm * z2)
    st_ref[0:1, :] = first
    st_ref[1:2, :] = second


def front_three(meta, *refs):
    stats, (tot_ref, z2_ref, hw_ref, n_ref, wa_ref, wb_ref) = refs[0:4], refs[4:10]
    tot2_ref, a2_ref, a2b_ref, st_ref, w_ref, sem = refs[10:]
    fetch(meta, W3, wa_ref, wb_ref, w_ref, sem)
    table = plane_total(stats)
    tot2_ref[...] = table
    mean, scale = mean_scale(table, count_of(tot_ref))
    first, second = 0.0, 0.0
    for k in range(WORK):
        pre = (z2_ref[k] - mean) * scale * n_ref[0:1, M0 : 2 * M0] + n_ref[1:2, M0 : 2 * M0]
        act = (silu(pre) * over_lanes(mask0(hw_ref, k), M0)).astype(BF16)
        a2_ref[k] = act
        a2b_ref[k] = act
        if k == 0:
            await_copy(w_ref, sem)
        z3 = dot_nn(act, w_ref[...])
        first = first + total_rows(z3)
        second = second + total_rows(z3 * z3)
    st_ref[0:1, :] = first
    st_ref[1:2, :] = second


def even_picker():
    row = lax.broadcasted_iota(jnp.int32, (PIX1, PIX0), 0)
    col = lax.broadcasted_iota(jnp.int32, (PIX1, PIX0), 1)
    return jnp.where(col == 32 * (row >> 3) + 2 * (row & 7), 1.0, 0.0).astype(BF16)


def even_placer():
    row = lax.broadcasted_iota(jnp.int32, (PIX0, PIX1), 0)
    col = lax.broadcasted_iota(jnp.int32, (PIX0, PIX1), 1)
    return jnp.where(row == 32 * (col >> 3) + 2 * (col & 7), 1.0, 0.0).astype(BF16)


def placed(values):
    placer = even_placer()
    high = values.astype(BF16)
    rest = (values - high.astype(F32)).astype(BF16)
    return dot_nn(placer, high) + dot_nn(placer, rest)


SIDE_PART = C1 // 4


def join(meta, *refs):
    stats, (tot_ref, a2_ref), evens, (hw_ref, n_ref) = refs[0:4], refs[4:6], refs[6:10], refs[10:12]
    wa_ref, wb_ref = refs[12:14]
    tot3_ref, s_ref, p_ref, z3_ref, z1_ref, z1b_ref, zs_ref, st_ref, sts_ref = refs[14:23]
    w3_ref, w1_ref, ws_ref, sems = refs[23:]
    step = pl.program_id(0)

    @pl.when(step == 0)
    def _():
        fetch(meta, W3, wa_ref, wb_ref, w3_ref, sems.at[0])
        fetch(meta, V1, wa_ref, wb_ref, w1_ref, sems.at[1])
        for k in range(4):
            cols = (k * SIDE_PART, SIDE_PART)
            fetch(meta, VS, wa_ref, wb_ref, ws_ref.at[k], sems.at[2 + k], cols=cols)
        table = plane_total(stats)
        tot3_ref[...] = table
        mean, scale = mean_scale(table, count_of(tot_ref))
        picker = even_picker()
        await_copy(w3_ref, sems.at[0])
        for k in range(WORK):
            act = dot_nn(picker, a2_ref[k]).astype(BF16)
            z3 = dot_nn(act, w3_ref[...])
            here = slice(k * PIX1, (k + 1) * PIX1)
            z3_ref[here, :] = z3
            pre = (z3 - mean) * scale * n_ref[0:1, 2 * M0 : 2 * M0 + C0]
            pre = pre + n_ref[1:2, 2 * M0 : 2 * M0 + C0]
            pre = pre + evens[k][...].astype(F32)
            p_ref[here, :] = pre
            s_ref[here, :] = (silu(pre) * over_lanes(mask1(hw_ref, k), C0)).astype(BF16)
        await_copy(w1_ref, sems.at[1])
        z1 = dot_nn(s_ref[...], w1_ref[...])
        z1_ref[...] = z1
        z1b_ref[...] = z1
        put_sums(st_ref, z1, z1 * z1)

    for k in range(4):

        @pl.when(step == k)
        def _(k=k):
            await_copy(ws_ref.at[k], sems.at[2 + k])
            zs = dot_nn(s_ref[...], ws_ref[k])
            zs_ref[...] = zs
            put_sums(sts_ref, zs, zs * zs)


def fetch_conv(meta, wa_ref, wb_ref, w_ref, sems):
    for k in range(3):
        rows = (k * 3 * M1, 3 * M1)
        fetch(meta, V2, wa_ref, wb_ref, w_ref.at[pl.ds(*rows)], sems.at[k], rows=rows)


def await_conv(w_ref, sems, k):
    await_copy(w_ref.at[pl.ds(k * 3 * M1, 3 * M1)], sems.at[k])


def mid_one(meta, *refs):
    stats, (tot_ref, z1_ref, hw_ref, n_ref, wa_ref, wb_ref) = refs[0:4], refs[4:10]
    tot4_ref, a1_ref, z2_ref, z2b_ref, st_ref, w_ref, sems = refs[10:]
    fetch_conv(meta, wa_ref, wb_ref, w_ref, sems)
    table = plane_total(stats)
    tot4_ref[...] = table
    mean, scale = mean_scale(table, count_of(tot_ref) * 0.25)
    mask = mask1_all(hw_ref, M1)
    act = silu((z1_ref[...] - mean) * scale * n_ref[0:1, :M1] + n_ref[1:2, :M1]) * mask
    left, right = side_columns(act, WB // 2)
    wide = jnp.concatenate([left, act, right], axis=1).astype(BF16)
    a1_ref[...] = wide[:, M1 : 2 * M1]
    await_conv(w_ref, sems, 0)
    z2 = later_rows(dot_nn(wide, w_ref[0 : 3 * M1, :]), 1, HB // 2, WB // 2)
    await_conv(w_ref, sems, 1)
    z2 = z2 + dot_nn(wide, w_ref[3 * M1 : 6 * M1, :])
    await_conv(w_ref, sems, 2)
    z2 = z2 + later_rows(dot_nn(wide, w_ref[6 * M1 :, :]), -1, HB // 2, WB // 2)
    z2_ref[...] = z2
    z2b_ref[...] = z2
    zm = z2 * mask
    put_sums(st_ref, zm, zm * z2)


def mid_two(meta, *refs):
    stats, (tot_ref, z2_ref, hw_ref, n_ref, wa_ref, wb_ref) = refs[0:4], refs[4:10]
    tot5_ref, a2_ref, z3_ref, st_ref, w_ref, sem = refs[10:]
    fetch(meta, V3, wa_ref, wb_ref, w_ref, sem)
    table = plane_total(stats)
    tot5_ref[...] = table
    mean, scale = mean_scale(table, count_of(tot_ref) * 0.25)
    pre = (z2_ref[...] - mean) * scale * n_ref[0:1, M1 : 2 * M1] + n_ref[1:2, M1 : 2 * M1]
    act = (silu(pre) * mask1_all(hw_ref, M1)).astype(BF16)
    a2_ref[...] = act
    await_copy(w_ref, sem)
    z3 = dot_nn(act, w_ref[...])
    z3_ref[...] = z3
    put_sums(st_ref, z3, z3 * z3)


AT3, ATS = 2 * M1, 2 * M1 + C1


def turn(meta, *refs):
    stats, sides, (tot_ref, z3_ref, zs_ref, hw_ref, n_ref) = refs[0:4], refs[4:8], refs[8:13]
    cots, (tot6_ref, tots_ref), ys, (g_ref, st_ref) = refs[13:17], refs[17:19], refs[19:23], refs[23:]
    step = pl.program_id(0)

    @pl.when(step == 0)
    def _():
        tot6_ref[...] = plane_total(stats)
        tots_ref[...] = plane_total(sides)
        st_ref[...] = jnp.zeros_like(st_ref)

    count = count_of(tot_ref) * 0.25
    mean, scale = mean_scale(tot6_ref[...], count)
    mean_s, scale_s = mean_scale(tots_ref[...], count)
    normed = (z3_ref[0] - mean) * scale
    normed_s = (zs_ref[0] - mean_s) * scale_s
    pre = normed * n_ref[0:1, AT3:ATS] + n_ref[1:2, AT3:ATS]
    pre = pre + (normed_s * n_ref[0:1, ATS : ATS + C1] + n_ref[1:2, ATS : ATS + C1])
    sig = sigmoid(pre)
    value = pre * sig
    change = sig * (1.0 + pre * (1.0 - sig))
    for k in range(WORK):

        @pl.when(step == k)
        def _(k=k):
            mask = over_lanes(mask1(hw_ref, k), C1)
            ys[k][...] = (value * mask).astype(BF16)
            g_ref[0] = cots[k][...].astype(F32) * change * mask

    grad = g_ref[0]
    st_ref[0:1, :] += total_rows(grad)
    st_ref[1:2, :] += total_rows(grad * normed)
    st_ref[2:3, :] += total_rows(grad * normed_s)


def norm_back(grad, normed, scale, gain, first, second, mask):
    return (mask * (scale * gain) * (grad - first - normed * second)).astype(BF16)


def back_one(meta, *refs):
    stats, (tot6_ref, tots_ref, tot5_ref, tot_ref) = refs[0:4], refs[4:8]
    z3_ref, zs_ref, g_ref, z2_ref, hw_ref, n_ref, wa_ref, wb_ref = refs[8:16]
    tot7_ref, er_ref, es_ref, g2_ref, st_ref, w_ref, sem = refs[16:]
    fetch(meta, V3, wa_ref, wb_ref, w_ref, sem)
    table = plane_total(stats)
    tot7_ref[...] = table
    count = count_of(tot_ref) * 0.25
    table = table / count
    mask = mask1_all(hw_ref, C1)
    grad = g_ref[...]
    mean, scale = mean_scale(tot6_ref[...], count)
    normed = (z3_ref[...] - mean) * scale
    d3 = norm_back(grad, normed, scale, n_ref[0:1, AT3:ATS], table[0:1], table[1:2], mask)
    mean2, scale2 = mean_scale(tot5_ref[...], count)
    normed2 = (z2_ref[...] - mean2) * scale2
    pre2 = normed2 * n_ref[0:1, M1 : 2 * M1] + n_ref[1:2, M1 : 2 * M1]
    await_copy(w_ref, sem)
    g2 = dot_nt(d3, w_ref[...]) * mask[:, :M1] * slope(pre2)
    g2_ref[...] = g2
    put_sums(st_ref, g2, g2 * normed2)
    mean_s, scale_s = mean_scale(tots_ref[...], count)
    normed_s = (zs_ref[...] - mean_s) * scale_s
    ds = norm_back(grad, normed_s, scale_s, n_ref[0:1, ATS : ATS + C1], table[0:1], table[2:3], mask)
    es_ref[...] = ds
    half = C1 // 2
    for p in range(2):
        cols = slice(p * half, (p + 1) * half)
        er_ref[meta[CORE] ^ p] = jnp.concatenate([d3[:, cols], ds[:, cols]], axis=1)


def back_two(meta, *refs):
    stats, (tot5_ref, tot4_ref, tot_ref, z2_ref, g2_ref, z1_ref) = refs[0:4], refs[4:10]
    hw_ref, n_ref, wa_ref, wb_ref, tot8_ref, er_ref, g1_ref, st_ref, w_ref, sems = refs[10:]
    fetch_conv(meta, wa_ref, wb_ref, w_ref, sems)
    table = plane_total(stats)
    tot8_ref[...] = table
    count = count_of(tot_ref) * 0.25
    table = table / count
    mask = mask1_all(hw_ref, M1)
    mean, scale = mean_scale(tot5_ref[...], count)
    normed = (z2_ref[...] - mean) * scale
    d2 = norm_back(
        g2_ref[...], normed, scale, n_ref[0:1, M1 : 2 * M1], table[0:1], table[1:2], mask
    )
    for p in range(2):
        er_ref[meta[CORE] ^ p] = d2[:, p * (M1 // 2) : (p + 1) * (M1 // 2)]
    mean1, scale1 = mean_scale(tot4_ref[...], count)
    normed1 = (z1_ref[...] - mean1) * scale1
    pre1 = normed1 * n_ref[0:1, :M1] + n_ref[1:2, :M1]
    await_conv(w_ref, sems, 0)
    wide = later_rows(dot_nt(d2, w_ref[0 : 3 * M1, :]), -1, HB // 2, WB // 2)
    await_conv(w_ref, sems, 1)
    wide = wide + dot_nt(d2, w_ref[3 * M1 : 6 * M1, :])
    await_conv(w_ref, sems, 2)
    wide = wide + later_rows(dot_nt(d2, w_ref[6 * M1 :, :]), 1, HB // 2, WB // 2)
    left, _ = side_columns(wide[:, 2 * M1 :], WB // 2)
    _, right = side_columns(wide[:, :M1], WB // 2)
    g1 = (wide[:, M1 : 2 * M1] + left + right) * mask * slope(pre1)
    g1_ref[...] = g1
    put_sums(st_ref, g1, g1 * normed1)


def back_three(meta, *refs):
    stats, (tot4_ref, tot_ref, z1_ref, g1_ref, es_ref, tot3_ref, p_ref, z3_ref) = refs[0:4], refs[4:12]
    hw_ref, n_ref, wa_ref, wb_ref = refs[12:16]
    tot9_ref, er_ref, g0_ref, st_ref, w1_ref, ws_ref, sems = refs[16:]
    fetch(meta, V1, wa_ref, wb_ref, w1_ref, sems.at[0])
    fetch(meta, VS, wa_ref, wb_ref, ws_ref, sems.at[1])
    table = plane_total(stats)
    tot9_ref[...] = table
    count = count_of(tot_ref) * 0.25
    table = table / count
    mask = mask1_all(hw_ref, C0)
    mean, scale = mean_scale(tot4_ref[...], count)
    normed = (z1_ref[...] - mean) * scale
    d1 = norm_back(
        g1_ref[...], normed, scale, n_ref[0:1, :M1], table[0:1], table[1:2], mask[:, :M1]
    )
    for p in range(2):
        er_ref[meta[CORE] ^ p] = d1[:, p * (M1 // 2) : (p + 1) * (M1 // 2)]
    await_copy(w1_ref, sems.at[0])
    grad = dot_nt(d1, w1_ref[...])
    await_copy(ws_ref, sems.at[1])
    grad = grad + dot_nt(es_ref[...], ws_ref[...])
    grad = grad.astype(BF16).astype(F32)
    g0 = grad * slope(p_ref[...]) * mask
    g0_ref[...] = g0
    mean3, scale3 = mean_scale(tot3_ref[...], count * 4.0)
    put_sums(st_ref, g0, g0 * ((z3_ref[...] - mean3) * scale3))


def last_one(meta, *refs):
    stats, (tot3_ref, tot2_ref, tot_ref, a2_ref, g0_ref, z2_ref, hw_ref, n_ref) = refs[0:4], refs[4:12]
    wa_ref, wb_ref, tot10_ref, d3_ref, g2_ref, st_ref, w_ref, sem = refs[12:]
    step = pl.program_id(0)

    @pl.when(step == 0)
    def _():
        fetch(meta, W3, wa_ref, wb_ref, w_ref, sem)
        tot10_ref[...] = plane_total(stats)
        st_ref[...] = jnp.zeros_like(st_ref)
        await_copy(w_ref, sem)

    count = count_of(tot_ref)
    table = tot10_ref[...] / count
    mean, scale = mean_scale(tot3_ref[...], count)
    mean2, scale2 = mean_scale(tot2_ref[...], count)
    high = pl.ds(step, 1)
    wide = pl.ds(4 + step, 1)
    mask = over_lanes(pixel_mask(hw_ref[high, :], hw_ref[wide, :], WB, PIX0), C0)
    normed = (dot_nn(a2_ref[0], w_ref[...]) - mean) * scale
    grad = placed(g0_ref[0])
    gain = n_ref[0:1, 2 * M0 : 2 * M0 + C0]
    d3 = norm_back(grad, normed, scale, gain, table[0:1], table[1:2], mask)
    d3_ref[0] = d3
    normed2 = (z2_ref[0] - mean2) * scale2
    pre2 = normed2 * n_ref[0:1, M0 : 2 * M0] + n_ref[1:2, M0 : 2 * M0]
    g2 = dot_nt(d3, w_ref[...]) * mask[:, :M0] * slope(pre2)
    g2_ref[0] = g2
    st_ref[0:1, :] += total_rows(g2)
    st_ref[1:2, :] += total_rows(g2 * normed2)


def last_two(meta, *refs):
    stats, (tot2_ref, tot_ref, z2_ref, g2_ref, z1_ref, hw_ref, n_ref) = refs[0:4], refs[4:11]
    wa_ref, wb_ref, tot11_ref, d2_ref, g1_ref, st_ref, w_ref, sem = refs[11:]
    step = pl.program_id(0)

    @pl.when(step == 0)
    def _():
        fetch(meta, W2, wa_ref, wb_ref, w_ref, sem)
        tot11_ref[...] = plane_total(stats)
        st_ref[...] = jnp.zeros_like(st_ref)

    count = count_of(tot_ref)
    table = tot11_ref[...] / count
    mask = pixel_mask(hw_ref[pl.ds(step, 1), :], hw_ref[pl.ds(4 + step, 1), :], WB, PIX0)
    mask = over_lanes(mask, M0)
    mean2, scale2 = mean_scale(tot2_ref[...], count)
    normed2 = (z2_ref[0] - mean2) * scale2
    gain = n_ref[0:1, M0 : 2 * M0]
    d2 = norm_back(g2_ref[0], normed2, scale2, gain, table[0:1], table[1:2], mask)
    d2_ref[0] = d2
    mean1, scale1 = mean_scale(tot_ref[:, :M0], count)
    normed1 = (z1_ref[0] - mean1) * scale1
    pre1 = normed1 * n_ref[0:1, :M0] + n_ref[1:2, :M0]

    @pl.when(step == 0)
    def _():
        await_copy(w_ref, sem)

    wide = dot_nt(d2, w_ref[3 * M0 : 6 * M0, :])
    wide = wide + later_rows(dot_nt(d2, w_ref[0 : 3 * M0, :]), -1, HB, WB)
    wide = wide + later_rows(dot_nt(d2, w_ref[6 * M0 :, :]), 1, HB, WB)
    left, _ = side_columns(wide[:, 2 * M0 :], WB)
    _, right = side_columns(wide[:, :M0], WB)
    g1 = (wide[:, M0 : 2 * M0] + left + right) * mask * slope(pre1)
    g1_ref[0] = g1
    st_ref[0:1, :] += total_rows(g1)
    st_ref[1:2, :] += total_rows(g1 * normed1)


def last_three(meta, *refs):
    stats, (tot_ref, z1_ref, g1_ref, g0_ref, hw_ref, n_ref) = refs[0:4], refs[4:10]
    tot12_ref, backs = refs[10], refs[11:15]
    table = plane_total(stats)
    tot12_ref[...] = table
    count = count_of(tot_ref)
    table = table / count
    mean, scale = mean_scale(tot_ref[:, :M0], count)
    for k in range(WORK):
        mask = over_lanes(mask0(hw_ref, k), M0)
        normed = (z1_ref[k] - mean) * scale
        backs[k][0:PIX0, :] = norm_back(
            g1_ref[k], normed, scale, n_ref[0:1, :M0], table[0:1], table[1:2], mask
        )
        grad = g0_ref[k * PIX1 : (k + 1) * PIX1, :].astype(BF16)
        for part in range(C0 // M0):
            here = slice(PIX0 + part * PIX1, PIX0 + (part + 1) * PIX1)
            backs[k][here, :] = grad[:, part * M0 : (part + 1) * M0]


def leave(meta, x_ref, wa_ref, wb_ref, *refs):
    backs, gx_ref, out_ref = refs[0:4], refs[5], refs[6]
    w_ref, acc_ref, stage_ref, sem, out_sem = refs[7:]
    step = pl.program_id(0)

    @pl.when(step == 0)
    def _():
        fetch(meta, W1, wa_ref, wb_ref, w_ref, sem)
        acc_ref[...] = jnp.zeros_like(acc_ref)
        await_copy(w_ref, sem)

    for k in range(WORK):

        @pl.when(step == k)
        def _(k=k):
            d1 = backs[k][0:PIX0, :]
            grad = jnp.concatenate(
                [backs[k][PIX0 + n * PIX1 : PIX0 + (n + 1) * PIX1, :] for n in range(C0 // M0)], axis=1
            )
            acc_ref[...] += dot_tn(x_ref[0].reshape(PIX0, C0), d1)
            gx_ref[0] = (dot_nt(d1, w_ref[...]) + dot_nn(even_placer(), grad)).astype(BF16)

    @pl.when(step == WORK - 1)
    def _():
        put_tiles(stage_ref, 0, acc_ref[...])
        copy = pltpu.make_async_copy(stage_ref, out_ref.at[pl.ds(0, 2 * C0)], out_sem)
        copy.start()
        copy.wait()


def put_tiles(ref, start, values):
    rows, width = values.shape
    for k in range(width // 128):
        here = slice(start + k * rows, start + (k + 1) * rows)
        ref[here, :] = values[:, 128 * k : 128 * (k + 1)].astype(BF16)


def nine_shifts(delta, height, breadth):
    pieces = []
    left, right = side_columns(delta, breadth)
    for a in range(3):
        for moved in (right, delta, left):
            pieces.append(later_rows(moved, a - 1, height, breadth).astype(BF16))
    return jnp.concatenate(pieces, axis=1)


SIDES, MIDDLE = 768, 704
SWAPPED = (0, 2, 1, 3)


def place_of(core, chip):
    return jnp.where(core == 0, 2 * (chip & 1) + (chip >> 1), chip)


def spot_of(level):
    return 2 * (level & 1) + (level >> 1)


def put_shards(ref, shard, start, core, level_first, values):
    rows = values.shape[0] // 16
    values = values.astype(BF16)
    for chip in range(4):
        place = place_of(core, chip)
        for z in range(4):
            at = (SWAPPED[z] * 4 + place if level_first else place * 4 + SWAPPED[z]) * shard + start
            part = values[(4 * chip + z) * rows : (4 * chip + z + 1) * rows]
            for k in range(values.shape[1] // 128):
                here = pl.ds(pl.multiple_of(at + k * rows, 16), rows)
                ref[here, :] = part[:, 128 * k : 128 * (k + 1)]


def sides_grad(meta, sa_ref, sb_ref, la_ref, lb_ref, ea_ref, eb_ref, out_ref):
    half = C1 // 2
    side = dot_tn(sa_ref[...], ea_ref[0][:, half:]) + dot_tn(sb_ref[...], eb_ref[0][:, half:])
    put_shards(out_ref, SIDES, 0, meta[CORE], True, side)
    last = dot_tn(la_ref[...], ea_ref[0][:, :half]) + dot_tn(lb_ref[...], eb_ref[0][:, :half])
    put_shards(out_ref, SIDES, C0 // 2, meta[CORE], True, last)


def middle_grad(meta, sa_ref, sb_ref, la_ref, lb_ref, ma_ref, mb_ref, fa_ref, fb_ref, out_ref):
    conv = dot_tn(la_ref[...], nine_shifts(ma_ref[0].astype(F32), HB // 2, WB // 2))
    conv = conv + dot_tn(lb_ref[...], nine_shifts(mb_ref[0].astype(F32), HB // 2, WB // 2))
    put_shards(out_ref, MIDDLE, 0, meta[CORE], False, conv)
    first = dot_tn(sa_ref[...], fa_ref[0]) + dot_tn(sb_ref[...], fb_ref[0])
    put_shards(out_ref, MIDDLE, 9 * M1 // 8, meta[CORE], False, first)


def front_grad_two(meta, a1_ref, d2_ref, a2_ref, d3_ref, out_ref, acc2_ref, acc3_ref):
    slot = pl.program_id(0)
    conv = dot_tn(a1_ref[0], nine_shifts(d2_ref[0].astype(F32), HB, WB))
    last = dot_tn(a2_ref[0], d3_ref[0])

    @pl.when(slot == 0)
    def _():
        acc2_ref[...] = conv
        acc3_ref[...] = last

    @pl.when(slot > 0)
    def _():
        acc2_ref[...] += conv
        acc3_ref[...] += last

    @pl.when(slot == WORK - 1)
    def _():
        for tap in range(9):
            for tile in range(2):
                start = 2 * C0 + tile * 9 * M0 + tap * M0
                lanes = tap * M0 + tile * 128
                out_ref[start : start + M0, :] = acc2_ref[:, lanes : lanes + 128].astype(BF16)
        out_ref[0 : 2 * C0, :] = jnp.zeros((2 * C0, 128), BF16)
        put_tiles(out_ref, 2 * C0 + 2 * 9 * M0, acc3_ref[...])


def unpack_kernel(jobs, chunk, meta, raw_ref, out_ref, *refs):
    raws, flat_ref, sem_in, sem_out = refs[0:3], refs[3], refs[4], refs[5]
    stages = dict(zip(sorted({weight[3] for listed in jobs for _, weight in listed}), refs[6:]))

    def run(listed):
        loads, stores, waits, sizes = [], [], [], []
        for offset, (_, base, height, cols) in listed:
            for row in range(0, height, chunk // cols):
                some = min(chunk // cols, height - row)
                k = len(loads)
                source = raw_ref.at[:, pl.ds(offset + row * cols, some * cols)]
                here = raws[k % 3].at[:, pl.ds(0, some * cols)]
                loads.append(pltpu.make_async_copy(source, here, sem_in.at[k % 3]))
                stage = stages[cols].at[k % 2, pl.ds(0, some)]
                panels = []
                for panel in range(cols // 256):
                    there = out_ref.at[pl.ds(base + panel * height + row, some)]
                    lanes = stage.at[:, pl.ds(256 * panel, 256)]
                    panels.append(pltpu.make_async_copy(lanes, there, sem_out.at[k % 2]))
                stores.append(panels)
                waits.append(pltpu.make_async_copy(stage, stage, sem_out.at[k % 2]))
                sizes.append((some, cols))
        for load in loads[:2]:
            load.start()
        for k, (rows, cols) in enumerate(sizes):
            if k + 2 < len(sizes):
                loads[k + 2].start()
            loads[k].wait()
            flat_ref[:, : rows * cols] = raws[k % 3][:, : rows * cols].astype(F32)
            lines = flat_ref.reshape(chunk // 128, 128)
            if k >= 2:
                waits[k - 2].wait()
            for tile in range(cols // 128):
                values = lines[pl.ds(tile, rows, stride=cols // 128), :].astype(BF16)
                stages[cols][k % 2, 0:rows, tile * 128 : (tile + 1) * 128] = values
            for store in stores[k]:
                store.start()
        for wait in waits[-2:]:
            wait.wait()

    for core in range(2):
        if jobs[core]:
            pl.when(meta[CORE] == core)(functools.partial(run, jobs[core]))


def unpack(meta, packed, rows, jobs, micros, chunk=262144):
    widths = sorted({weight[3] for listed in jobs for _, weight in listed})
    return call(
        functools.partial(unpack_kernel, jobs, chunk),
        pltpu.HBM((rows, 256), BF16),
        (1,),
        [ANYWHERE],
        ANYWHERE,
        [pltpu.VMEM((1, chunk), BF16)] * 3
        + [pltpu.VMEM((1, chunk), F32), DMA((3,)), DMA((2,))]
        + [pltpu.VMEM((2, chunk // cols, cols), BF16) for cols in widths],
        micros=micros,
    )(meta, in_hbm(packed))


PACK_ROWS = 2048
GRAD_ROWS = P_SIZE // 128
ARRIVED = ((1, (0, 1)), (0, (0, 2)), (0, (1, 3)), (1, (2, 3)))


def quarters(bufs, target):
    found = []
    for buf, (p, masks) in zip(bufs, ARRIVED):
        if target == 0:
            p, masks = 1 - p, tuple(SWAPPED[m] for m in masks)
        for k, mask in enumerate(masks):
            found.append((p, mask, buf, k * (buf.shape[0] // 2)))
    return found


def pack_sides(meta, *refs):
    bufs, out_ref = refs[:4], refs[4]
    step = pl.program_id(0)
    level, plane = meta[LEVEL], meta[PLANE]

    @pl.when(meta[CORE] == 0)
    def _():
        out_ref[...] = jnp.zeros_like(out_ref)

    for p, mask, buf, start in quarters(bufs, 1):
        here = meta[CORE] == 1

        @pl.when(here & (step < 4) & (step == (plane ^ mask)))
        def _(p=p, buf=buf, start=start):
            for z in range(4):
                for k in range(8):
                    row = start + spot_of(level ^ z) * SIDES + C0 // 2 + 32 * k
                    rows = buf[pl.ds(pl.multiple_of(row, 32), 32), :].astype(F32)
                    out_ref[pl.ds(512 * z + 8 * p + k, 32, stride=16), :] = rows

        @pl.when(here & (step >= 4) & (((step - 4) >> 1) == (plane ^ mask)))
        def _(p=p, buf=buf, start=start):
            for j in range(2):
                z = 2 * (step & 1) + j
                for k in range(8):
                    row = start + spot_of(level ^ z) * SIDES + 64 * k
                    rows = buf[pl.ds(pl.multiple_of(row, 64), 64), :].astype(F32)
                    out_ref[pl.ds(1024 * j + 8 * p + k, 64, stride=16), :] = rows


def pack_middle(first_step, meta, *refs):
    bufs, out_ref = refs[1:5], refs[-1]
    step = pl.program_id(0) + first_step
    plane, level = meta[PLANE], meta[LEVEL]

    for p, mask, buf, start in quarters(bufs, 1):
        chip = plane ^ mask

        @pl.when((meta[CORE] == 1) & (step < 2) & (step == (chip >> 1)))
        def _(p=p, buf=buf, start=start, chip=chip):
            for z in range(4):
                for k in range(2):
                    row = start + spot_of(level ^ z) * MIDDLE + 9 * M1 // 8 + 64 * k
                    rows = buf[pl.ds(pl.multiple_of(row, 64), 64), :].astype(F32)
                    at = 256 * (4 * (chip & 1) + z) + 2 * p + k
                    out_ref[pl.ds(at, 64, stride=4), :] = rows

        @pl.when((meta[CORE] == 1) & (step > 1))
        def _(p=p, buf=buf, start=start, chip=chip):
            for z in range(4):
                for k in range(2):
                    row = start + spot_of(level ^ z) * MIDDLE + 64 * (step - 2) + 32 * k
                    rows = buf[pl.ds(pl.multiple_of(row, 32), 32), :].astype(F32)
                    at = 128 * (4 * chip + z) + 2 * p + k
                    out_ref[pl.ds(at, 32, stride=4), :] = rows


def pack_rest(meta, *refs):
    out_ref = refs[-1]

    @pl.when(meta[CORE] == 0)
    def _():
        out_ref[...] = jnp.zeros_like(out_ref)

    pack_middle(5, meta, *refs)


def pack_front(meta, *refs):
    fronts, out_ref, whole_ref = refs[5:9], refs[9], refs[10]
    step = pl.program_id(0)
    core, plane, level = meta[CORE], meta[PLANE], meta[LEVEL]
    part = fronts[0].shape[0] // 8

    @pl.when((core == 0) & (step == 0))
    def _():
        for p, mask, buf, start in quarters(fronts, 0):
            for z in range(4):
                there = (16 * p + 4 * place_of(p, plane ^ mask) + spot_of(level ^ z)) * part
                at = start + SWAPPED[z] * part
                rows = buf[at : at + part, :]
                whole_ref[pl.ds(pl.multiple_of(there, 16), part), :] = rows

    at2, at3 = 2 * C0, 2 * C0 + 2 * 9 * M0

    def piece(start, rows):
        return whole_ref[start : start + rows, :].astype(F32)

    @pl.when((core == 0) & (step == 0))
    def _():
        for tile in range(2):
            out_ref[pl.ds(tile, C0, stride=2), :] = piece(tile * C0, C0)

    for k in range(2):

        @pl.when((core == 0) & (step == 1 + k))
        def _(k=k):
            for tile in range(2):
                out_ref[pl.ds(tile, C0, stride=2), :] = piece(at2 + tile * 9 * M0 + k * C0, C0)

    @pl.when((core == 0) & (step == 3))
    def _():
        for tile in range(2):
            out_ref[pl.ds(tile, 256, stride=2), :] = piece(at2 + tile * 9 * M0 + 2 * C0, 256)
        for tile in range(8):
            out_ref[pl.ds(512 + tile, 192, stride=8), :] = piece(at3 + tile * 256, 192)

    @pl.when((core == 0) & (step == 4))
    def _():
        out_ref[...] = jnp.zeros_like(out_ref)
        for tile in range(8):
            out_ref[pl.ds(tile, 64, stride=8), :] = piece(at3 + tile * 256 + 192, 64)

    pack_middle(0, meta, *refs[:5], out_ref)


def rows_out(meta, x_ref, xg_ref, y_ref, yg_ref, out_ref):
    step = pl.program_id(0)
    row = lax.broadcasted_iota(jnp.int32, (128, 128), 0)
    col = lax.broadcasted_iota(jnp.int32, (128, 128), 1)

    def put(first, second, source):
        values = jnp.concatenate([first.reshape(-1, C0), second.reshape(-1, C0)], axis=0)
        mover = jnp.where(col == source, 1.0, 0.0).astype(BF16)
        moved = dot_nn(mover, values).astype(BF16)
        for k in range(16):
            out_ref[:, k * C0 : (k + 1) * C0] = moved[8 * k : 8 * (k + 1), :]

    image, stand = row & 7, row * 0
    for k in range(WORK):
        stand = jnp.where(image == meta[k], k, jnp.where(image == (meta[k] ^ 1), WORK + k, stand))

    @pl.when(meta[CORE] == 0)
    def _():
        put(x_ref[...], xg_ref[...], 16 * stand + (row >> 3))

    @pl.when((meta[CORE] == 1) & (step < HB // 2))
    def _():
        def split(ref):
            pieces = []
            for k in range(WORK):
                wide = ref[k].astype(F32)
                pieces += [wide[:, :C0], wide[:, C0:]]
            return jnp.concatenate(pieces, axis=0).astype(BF16)

        put(split(y_ref), split(yg_ref), 16 * stand + 8 * ((row >> 3) & 1) + (row >> 4))

    @pl.when((meta[CORE] == 1) & (step >= HB // 2))
    def _():
        out_ref[...] = jnp.zeros_like(out_ref)


def pin(value, *others):
    return lax.optimization_barrier((value,) + others)[0]


def swap_cores(value):
    return lax.ppermute(value, "pipe", [(0, 1), (1, 0)])


def xor_permute(value, mask):
    count = lax.axis_size("dp")
    return lax.ppermute(value, "dp", [(i, i ^ mask) for i in range(count)])


def upper_bits():
    return [bit for bit in (16, 32, 64, 128, 256, 512) if bit < lax.axis_size("dp")]


def plane_turn(value, turn_no):
    count = lax.axis_size("dp")
    pairs = []
    for p in range(2):
        mask = SWAPPED[turn_no] if p else turn_no
        pairs += [(p * count + i, p * count + (i ^ mask)) for i in range(count)]
    return lax.ppermute(value, ("pipe", "dp"), pairs)


def shared(value):
    for bit in upper_bits():
        value = value + xor_permute(value, bit)
    return [value] + [plane_turn(value, k) for k in (1, 2, 3)]


def over_levels(values):
    return [values[0]] + [xor_permute(values[k], 4 * k) for k in (1, 2, 3)]


def part_at(value, index, parts):
    rows = value.shape[0] // parts
    return lax.optimization_barrier(lax.dynamic_slice_in_dim(value, index * rows, rows, 0))


def added(*parts):
    total = parts[0].astype(F32)
    for part in parts[1:]:
        total = total + part.astype(F32)
    return total.astype(BF16)


def upper_sum(value):
    for bit in upper_bits():
        value = added(value, xor_permute(value, bit))
    return value


def to_core(both, target):
    count = lax.axis_size("dp")
    other = 1 - target
    close, away = (1, 2) if target == 1 else (2, 1)
    arrived = [both]
    for p, mask in ((other, 0), (other, close), (target, away)):
        pairs = [(p * count + i, target * count + (i ^ mask)) for i in range(count)]
        arrived.append(lax.ppermute(both, ("pipe", "dp"), pairs))
    return arrived


def on_device(images, extents, views, params, norms, cotangent):
    images, cotangent, params = in_hbm(images), in_hbm(cotangent), in_hbm(params)
    core = lax.axis_index("pipe")
    first_core = core == 0
    plane = lax.axis_index("dp") % 4
    level = (lax.axis_index("dp") // 4) % 4
    place = place_of(core, plane)

    pair = 2 * (level ^ jnp.arange(WORK, dtype=jnp.int32))
    hot = (pair[:, None] == jnp.arange(2 * WORK, dtype=jnp.int32)[None, :]).astype(jnp.int32)
    view = jnp.sum(hot * views[None, :], axis=1)
    order = pair + (view != core).astype(jnp.int32)
    hot = (order[:, None] == jnp.arange(2 * WORK, dtype=jnp.int32)[None, :]).astype(jnp.int32)
    sizes = jnp.sum(hot[:, :, None] * extents[None], axis=1)
    spot = jnp.stack([core, plane, level]).astype(jnp.int32)
    meta = jnp.concatenate([order, spot, sizes[:, 0], sizes[:, 1]]).astype(jnp.int32)

    w1 = unpack(meta, params, C0, ([(0, W1)], []), 3, 65536)
    w1 = (in_hbm(w1), in_hbm(lax.ppermute(w1, "pipe", [(0, 1)])))
    norms_there = swap_cores(norms[0])
    n0 = jnp.where(first_core, norms[0], norms_there)
    n1 = jnp.where(first_core, norms_there, norms[0])

    some = lambda dims, kind: [shape_of(dims, kind)] * WORK
    made = call(
        enter,
        some((PIX0 + 16, M0), BF16) + some((PIX1, C0), BF16) + some((PIX1, C1), BF16),
        (WORK,),
        [own_image(HB, WB, C0), own_image(HB // 2, WB // 2, C1), ANYWHERE, ANYWHERE],
        [full(PIX0 + 16, M0)] * 4 + [full(PIX1, C0)] * 4 + [full(PIX1, C1)] * 4,
        [vmem(C0, M0), DMA],
    )(meta, images, cotangent, *w1)
    pays, evens, cots = over_levels(made[0:4]), made[4:8], made[8:12]
    first_weights = unpack(
        meta,
        pin(params, made[0]),
        10240,
        ([(262144, W2), (851968, W3)], [(0, V1), (3932160, VS)]),
        8,
    )
    pays[0] = pin(pays[0], first_weights, norms_there)
    z1, z1b, hw, st = single(
        arrive,
        meta,
        near(*pays),
        [
            ((WORK, PIX0, M0), F32, False),
            ((WORK, PIX0, M0), F32, True),
            ((8, 128), F32, False),
            ((2, M0 + 128), F32, False),
        ],
    )

    s1 = shared(st)
    got = swap_cores(first_weights)
    evens = over_levels(evens)
    second_weights = unpack(
        meta, pin(params, st), 13312, ([], [(524288, V2), (2883584, V3)]), 10
    )
    s1[0] = pin(s1[0], got, evens[1], second_weights)
    wa = (in_hbm(first_weights), in_hbm(got))
    tot1, a1, z2, z2b, st = single(
        front_two,
        meta,
        near(*s1, z1, hw, n0) + weight(wa),
        [
            ((2, M0 + 128), F32, False),
            ((WORK, PIX0, M0), BF16, True),
            ((WORK, PIX0, M0), F32, False),
            ((WORK, PIX0, M0), F32, True),
            ((2, M0), F32, False),
        ],
        [vmem(9 * M0, M0), vmem(2, PIX0 + 2 * WB, 3 * M0), DMA],
    )
    s2 = shared(st)
    got = lax.ppermute(second_weights, "pipe", [(1, 0)])
    s2[0] = pin(s2[0], evens[2])
    tot2, a2, a2b, st = single(
        front_three,
        meta,
        near(*s2, tot1, z2, hw, n0) + weight(wa),
        [
            ((2, M0), F32, False),
            ((WORK, PIX0, M0), BF16, False),
            ((WORK, PIX0, M0), BF16, True),
            ((2, C0), F32, False),
        ],
        [vmem(M0, C0), DMA],
    )
    s3 = shared(st)
    cots = over_levels(cots)
    s3[0] = pin(s3[0], evens[3])

    tile = lambda s, meta: (0, s)
    tot3, src, p_even, z3_even, y1, y1b, ys, st, sts = call(
        join,
        [
            shape_of((2, C0), F32),
            hbm_of((ROWS1, C0), BF16),
            hbm_of((ROWS1, C0), F32),
            hbm_of((ROWS1, C0), F32),
            shape_of((ROWS1, M1), F32),
            hbm_of((ROWS1, M1), F32),
            hbm_of((ROWS1, C1), F32),
            shape_of((2, M1), F32),
            shape_of((2, C1), F32),
        ],
        (4,),
        [full(2, C0)] * 4
        + [full(2, M0 + 128), full(WORK, PIX0, M0)]
        + [full(PIX1, C0)] * 4
        + [full(8, 128), full(2, CN)]
        + [ANYWHERE] * 2,
        [
            full(2, C0),
            full(ROWS1, C0),
            full(ROWS1, C0),
            full(ROWS1, C0),
            full(ROWS1, M1),
            full(ROWS1, M1),
            pl.BlockSpec((ROWS1, SIDE_PART), tile),
            full(2, M1),
            pl.BlockSpec((2, SIDE_PART), tile),
        ],
        [vmem(M0, C0), vmem(C0, M1), vmem(4, C0, SIDE_PART), DMA((6,))],
    )(meta, *s3, tot1, a2, *evens, hw, n0, *wa)

    s4 = shared(st)
    src_there = swap_cores(src)
    s4[0] = pin(s4[0], got, src_there)
    wb = (in_hbm(second_weights), in_hbm(got))
    conv_scratch = [vmem(9 * M1, M1), DMA((3,))]
    last_scratch = [vmem(M1, C1), DMA]
    row = ((2, M1), F32, False)
    tot4, b1, y2, y2b, st = single(
        mid_one,
        meta,
        near(*s4, tot1, y1, hw, n1) + weight(wb),
        [row, ((ROWS1, M1), BF16, True), ((ROWS1, M1), F32, False), ((ROWS1, M1), F32, True), row],
        conv_scratch,
    )
    s5 = shared(st)
    b1_there = swap_cores(b1)
    t5 = shared(sts)
    s5[0] = pin(s5[0], cots[1], b1_there, *t5)
    tot5, b2, y3, st = single(
        mid_two,
        meta,
        near(*s5, tot1, y2, hw, n1) + weight(wb),
        [row, ((ROWS1, M1), BF16, True), ((ROWS1, C1), F32, False), ((2, C1), F32, False)],
        last_scratch,
    )
    s6 = shared(st)
    b2_there = swap_cores(b2)
    s6[0] = pin(s6[0], cots[2], cots[3], b2_there)
    made = call(
        turn,
        [shape_of((2, C1), F32)] * 2
        + some((PIX1, C1), BF16)
        + [shape_of((WORK, PIX1, C1), F32), shape_of((3, C1), F32)],
        (WORK,),
        [full(2, C1)] * 8
        + [full(2, M0 + 128), per_image(PIX1, C1), per_image(PIX1, C1), full(8, 128), full(2, CN)]
        + [full(PIX1, C1)] * 4,
        [full(2, C1)] * 2 + [full(PIX1, C1)] * 4 + [per_image(PIX1, C1), full(3, C1)],
    )(
        meta, *s6, *t5, tot1, y3.reshape(WORK, PIX1, C1), in_hbm(ys.reshape(WORK, PIX1, C1)), hw,
        n1, *cots,
    )
    tot6, tots, y_out, grad_y, st = made[0], made[1], made[2:6], made[6], made[7]
    grad_y = grad_y.reshape(ROWS1, C1)

    s7 = shared(st)
    tot7, er, es, g2, st = single(
        back_one,
        meta,
        near(*s7, tot6, tots, tot5, tot1, y3) + far(ys) + near(grad_y) + far(y2b)
        + near(hw, n1) + weight(wb),
        [
            ((3, C1), F32, False),
            ((2, ROWS1, C1), BF16, False),
            ((ROWS1, C1), BF16, False),
            ((ROWS1, M1), F32, False),
            row,
        ],
        last_scratch,
        limit=36,
    )
    s8 = shared(st)
    other = swap_cores(er[1:])
    sides = single(
        sides_grad,
        meta,
        far(src, src_there, b2, b2_there) + near(er, other),
        [((16 * SIDES, 128), BF16, False)],
        limit=40,
    )[0]
    s8[0] = pin(s8[0], sides)
    low, high = level & 1, level >> 1
    sides = added(part_at(sides, low, 2), xor_permute(part_at(sides, 1 - low, 2), 4))
    tot8, e2r, g1, st = single(
        back_two,
        meta,
        near(*s8, tot5, tot4, tot1) + far(y2b) + near(g2) + far(y1b) + near(hw, n1) + weight(wb),
        [row, ((2, ROWS1, M1 // 2), BF16, False), ((ROWS1, M1), F32, False), row],
        conv_scratch,
    )
    s9 = shared(st)
    other2 = swap_cores(e2r[1:])
    s9[0] = pin(s9[0], other2)
    made = single(
        back_three,
        meta,
        near(*s9, tot4, tot1) + far(y1b) + near(g1, es, tot3) + far(p_even, z3_even)
        + near(hw, n1) + weight(wa),
        [row, ((2, ROWS1, M1 // 2), BF16, False), ((ROWS1, C0), F32, False), ((2, C0), F32, False)],
        [vmem(C0, M1), vmem(C0, C1), DMA((2,))],
    )
    tot9, e1r, g0, st = made

    s10 = shared(st)
    other1 = swap_cores(e1r[1:])
    s10[0] = pin(s10[0], other1, sides)
    half_there = xor_permute(part_at(sides, 1 - high, 2), 8)
    tot10, d3, g2, st = call(
        last_one,
        [
            shape_of((2, C0), F32),
            hbm_of((WORK, PIX0, C0), BF16),
            shape_of((WORK, PIX0, M0), F32),
            shape_of((2, M0), F32),
        ],
        (WORK,),
        [full(2, C0)] * 5
        + [
            full(2, M0), full(2, M0 + 128), per_image(PIX0, M0), per_image(PIX1, C0),
            per_image(PIX0, M0), full(8, 128), full(2, CN), ANYWHERE, ANYWHERE,
        ],
        [full(2, C0), per_image(PIX0, C0), per_image(PIX0, M0), full(2, M0)],
        [vmem(M0, C0), DMA],
    )(
        meta, *s10, tot3, tot2, tot1, in_hbm(a2b), g0.reshape(WORK, PIX1, C0), in_hbm(z2b), hw, n0,
        *wa,
    )
    s11 = shared(st)
    middle = single(
        middle_grad,
        meta,
        far(src, src_there, b1, b1_there) + [(pin(e2r, st), False)] + near(other2, e1r, other1),
        [((16 * MIDDLE, 128), BF16, False)],
        limit=40,
    )[0]
    s11[0] = pin(s11[0], middle)
    tot11, d2, g1, st = call(
        last_two,
        [
            shape_of((2, M0), F32),
            hbm_of((WORK, PIX0, M0), BF16),
            shape_of((WORK, PIX0, M0), F32),
            shape_of((2, M0), F32),
        ],
        (WORK,),
        [full(2, M0)] * 5
        + [full(2, M0 + 128)]
        + [per_image(PIX0, M0)] * 3
        + [full(8, 128), full(2, CN), ANYWHERE, ANYWHERE],
        [full(2, M0), per_image(PIX0, M0), per_image(PIX0, M0), full(2, M0)],
        [vmem(9 * M0, M0), DMA],
    )(meta, *s11, tot2, tot1, in_hbm(z2b), g2, in_hbm(z1b), hw, n0, *wa)
    s12 = shared(st)
    front = call(
        front_grad_two,
        hbm_of((2 * C0 + 2 * 9 * M0 + 8 * M0, 128), BF16),
        (WORK,),
        [per_image(PIX0, M0)] * 3 + [per_image(PIX0, C0)],
        full(2 * C0 + 2 * 9 * M0 + 8 * M0, 128),
        [pltpu.VMEM((M0, 9 * M0), F32), pltpu.VMEM((M0, C0), F32)],
    )(meta, in_hbm(a1), in_hbm(d2), in_hbm(a2b), in_hbm(d3))
    sides = upper_sum(added(part_at(sides, high, 2), half_there))
    s12[0] = pin(s12[0], front, sides)
    made = single(
        last_three,
        meta,
        near(*s12, tot1) + far(z1b) + near(g1) + far(g0) + near(hw, n0),
        [((2, M0), F32, False)] + [((PIX0 + C0 // M0 * PIX1, M0), BF16, False)] * 4,
    )
    tot12, backs = made[0], over_levels(made[1:])

    last = [tot12]

    def after(value):
        return pin(value, last[0])

    def step(value):
        last[0] = value
        return value

    def half_sum(value, bit, got):
        return step(added(after(part_at(value, bit, 2)), got))

    def other_half(value, bit):
        return part_at(value, 1 - bit, 2)

    def joined(value, got):
        return step(lax.optimization_barrier(jnp.concatenate([after(value), got], axis=0)))

    one, two = place >> 1, place & 1
    middle = pin(middle, *s12[1:])
    middle_got = plane_turn(other_half(middle, one), 1)
    sides_got = plane_turn(pin(other_half(sides, one), *s12[1:]), 1)
    sides = half_sum(sides, one, sides_got)
    sides_got = plane_turn(other_half(sides, two), 2)
    middle = half_sum(middle, one, middle_got)
    middle_got = plane_turn(other_half(middle, two), 2)
    sides = half_sum(sides, two, sides_got)
    sides_got = xor_permute(sides, 8)
    backs[0] = after(backs[0])
    rows = front.shape[0]
    gx, front = call(
        leave,
        [shape_of((WORK, PIX0, C0), BF16), hbm_of((rows, 128), BF16)],
        (WORK,),
        [own_image(HB, WB, C0), ANYWHERE, ANYWHERE]
        + [full(PIX0 + C0 // M0 * PIX1, M0)] * 4
        + [ANYWHERE],
        [per_image(PIX0, C0), ANYWHERE],
        [vmem(C0, M0), pltpu.VMEM((C0, M0), F32), vmem(2 * C0, 128), DMA, DMA],
        aliases={8: 1},
    )(meta, images, *w1, *backs, front)
    step(front)
    front_got = swap_cores(other_half(front, core))
    middle = half_sum(middle, two, middle_got)
    middle_got = xor_permute(other_half(middle, low), 4)
    x_there = lax.ppermute(gx, "pipe", [(1, 0)])
    middle = half_sum(middle, low, middle_got)
    middle_got = xor_permute(other_half(middle, high), 8)
    front = half_sum(front, core, front_got)
    front_got = plane_turn(other_half(front, one), 1)
    sides = joined(sides, sides_got)
    sides_got = xor_permute(sides, 4)
    middle = upper_sum(half_sum(middle, high, middle_got))
    middle_got = xor_permute(middle, 8)
    front = half_sum(front, one, front_got)
    front_got = plane_turn(other_half(front, two), 2)
    sides = joined(sides, sides_got)
    sides_got = plane_turn(sides, 2)
    front = half_sum(front, two, front_got)
    front_got = xor_permute(other_half(front, low), 4)
    middle = joined(middle, middle_got)
    middle_got = xor_permute(middle, 4)
    sides = to_core(joined(sides, sides_got), 1)
    y_back = [y_out[0]] + [xor_permute(after(y_out[k]), 4 * k) for k in (1, 2, 3)]
    front = half_sum(front, low, front_got)
    front_got = xor_permute(other_half(front, high), 8)
    middle = joined(middle, middle_got)
    middle_got = plane_turn(middle, 2)
    front = upper_sum(half_sum(front, high, front_got))
    front_got = xor_permute(front, 8)
    front = joined(front, front_got)
    front_got = xor_permute(front, 4)

    whole = shape_of((GRAD_ROWS, 128), F32)
    block_at = lambda at: pl.BlockSpec((PACK_ROWS, 128), lambda s, meta: (s + at, 0))
    side_spec, mid_spec = full(8 * SIDES, 128), full(8 * MIDDLE, 128)
    middle = to_core(joined(middle, middle_got), 1)
    sides[0] = after(sides[0])
    steps = GRAD_ROWS // PACK_ROWS - 11
    grads = call(pack_sides, whole, (steps,), [side_spec] * 4, block_at(11), micros=8)(meta, *sides)
    step(grads)
    y_back = step(lax.optimization_barrier(jnp.stack([after(y_back[0])] + y_back[1:])))
    y_there = lax.ppermute(y_back, "pipe", [(0, 1)])
    front = joined(front, front_got)
    front_got = plane_turn(front, 2)
    strip = lambda s, meta: (0, s, 0)
    strip_y = lambda s, meta: (0, jnp.minimum(s, 7), 0)
    boundary = call(
        rows_out,
        shape_of((2 * WORK, HB * WB * C0), BF16),
        (HB,),
        [pl.BlockSpec((WORK, WB, C0), strip)] * 2
        + [pl.BlockSpec((WORK, WB // 2, C1), strip_y)] * 2,
        pl.BlockSpec((2 * WORK, WB * C0), lambda s, meta: (0, s)),
        micros=9,
    )(meta, after(gx), x_there, y_back, y_there)
    step(boundary)
    fronts = to_core(joined(front, front_got), 0)
    middle[0] = after(middle[0])
    grads = call(
        pack_rest, whole, (6,), [ANYWHERE] + [mid_spec] * 4, block_at(5), aliases={1: 0}
    )(meta, grads, *middle)
    front_rows = fronts[0].shape[0]
    grads = call(
        pack_front,
        whole,
        (5,),
        [ANYWHERE] + [mid_spec] * 4 + [full(front_rows, 128)] * 4,
        block_at(0),
        [pltpu.VMEM((4 * front_rows, 128), BF16)],
        aliases={1: 0},
    )(meta, grads, *middle, *fronts)
    weight_grads = grads.reshape(1, P_SIZE)

    def gain_shift(table, second=1):
        return jnp.concatenate([table[second : second + 1], table[0:1]], axis=0)

    line0 = jnp.concatenate(
        [gain_shift(tot12), gain_shift(tot11), gain_shift(tot10), jnp.zeros((2, CN - 1536), F32)],
        axis=1,
    )
    line1 = jnp.concatenate(
        [gain_shift(tot9), gain_shift(tot8), gain_shift(tot7), gain_shift(tot7, 2)], axis=1
    )
    line = jnp.where(first_core, line0, line1) + swap_cores(jnp.where(first_core, line1, line0))
    for bit in (4, 8):
        line = line + xor_permute(line, bit)

    return boundary[None], weight_grads, line[None]


def solution(mesh):
    placed_as = (
        P("dp", None, None, None),
        P("dp", None),
        P("dp"),
        P("pipe", None),
        P("pipe", None, None),
        P("dp", None, None, None),
    )
    return jax.shard_map(
        on_device,
        mesh=mesh,
        in_specs=placed_as,
        out_specs=(P("pipe", "dp", None), P("pipe", None), P("pipe", None, None)),
        check_vma=False,
    )
```

profile of v0, /device:TPU:0, one launch (start us, length us, event | category | flops | bytes accessed | tf_op | source)
XLA Modules:
  0.0 420.8 jit_solution(2400292240869692790)
XLA Ops:
  9.6 6.1 %shard_map.86 = (bf16[272,256]{1,0:T(8,128)(2,1)S(1)}, bf16[272,256]{1,0:T(8,128)(2,1)S(1)}, bf16[272,256]{1,0:T(8,128)(2,1)S(1)}, bf16[272,256]{1,0:T(8,128)(2,...) custom-call(s32[15]{0:T(128)S(1)} %concatenate.57.meta, ...), custom_call_target="tpu_custom_call" | custom-call | bytes 18000000 | tf_op jit(solution)/shard_map/pallas_call | solution.py:1115
  21.4 4.6 %shard_map.87.refs_7_.refs_8_.refs_12_.refs_14_.refs_11_ = bf16[10240,256]{1,0:T(8,128)(2,1)} custom-call(s32[15]{0:T(128)S(1)} %concatenate.57.meta, bf16[1,6029312]{1,0:T(2,128)(2,1)} %raw_ref.3), custom_call_target="tpu_custom_call" | custom-call | bytes 28800000 | tf_op jit(solution)/shard_map/pallas_call | solution.py:847
  30.0 5.7 %collective-permute-done.1 = f32[2,5120]{1,0:T(2,128)S(1)} collective-permute-done((f32[2,5120]{1,0:T(2,128)S(1)}, f32[2,5120]{1,0:T(2,128)S(1)}, u32[]{:S(2)}, u32[]{:S(2)}) %collective-permute-start.1) | collective-permute-done | bytes 40992 | tf_op jit(solution)/shard_map/ppermute | solution.py:1031
  53.4 4.5 %shard_map.90 = (f32[2,384]{1,0:T(2,128)S(1)}, bf16[4,256,256]{2,1,0:T(8,128)(2,1)}, f32[4,256,256]{2,1,0:T(8,128)S(1)}, f32[4,256,256]{2,1,0:T(8,128)}, f32[2,256]{1,0:T(2,128)S(1)}) custom-call(s32[15]{0:T(128)S(1)} %concatenate.57.meta, f32[2,384]{1,0:T(2,128)S(1)} %get-tuple-element.136.refs_0_, f32[2,384]{1,0:T(2,128)S(1)} %collective-permute-done.7.refs_1_, ...), custom_call_target="tpu_custom_call" | custom-call | bytes 18000000 | tf_op jit(solution)/shard_map/pallas_call | solution.py:198
  73.6 7.4 %shard_map.92 = (f32[2,1024]{1,0:T(2,128)S(1)}, bf16[256,1024]{1,0:T(8,128)(2,1)}, f32[256,1024]{1,0:T(8,128)}, f32[256,1024]{1,0:T(8,128)}, f32[256,512]{1,0:T(...) custom-call(s32[15]{0:T(128)S(1)} %concatenate.57.meta, ...), custom_call_target="tpu_custom_call" | custom-call | bytes 18000000 | tf_op jit(solution)/shard_map/pallas_call | solution.py:1185
  81.0 6.4 %collective-permute-start.19 = (bf16[256,1024]{1,0:T(8,128)(2,1)}, bf16[256,1024]{1,0:T(8,128)(2,1)S(1)}, u32[]{:S(2)}, u32[]{:S(2)}) collective-permute-start(bf16[256,1024]{1,0:T(8,128)(2,1)} %get-tuple-element.150.sa_ref), channel_id=1, source_target_pairs={{0,16},{16,0},{1,17},{17,1},{2,18},{18,2},{3,19},{19,3},{4,20},{20... | collective-permute-start | bytes 1572872 | tf_op jit(solution)/shard_map/ppermute | solution.py:1031
  93.3 4.5 %shard_map.93 = (f32[2,512]{1,0:T(2,128)S(1)}, bf16[256,512]{1,0:T(8,128)(2,1)}, f32[256,512]{1,0:T(8,128)S(1)}, f32[256,512]{1,0:T(8,128)}, f32[2,512]{1,0:T(2,128)S(1)}) custom-call(s32[15]{0:T(128)S(1)} %concatenate.57.meta, f32[2,512]{1,0:T(2,128)S(1)} %get-tuple-element.151.refs_0_, f32[2,512]{1,0:T(2,128)S(1)} %collective-permute-done.20.refs_1_, ...), custom_call_target="tpu_custom_call" | custom-call | bytes 18000000 | tf_op jit(solution)/shard_map/pallas_call | solution.py:198
  115.7 7.1 %collective-permute-done.31.refs_15_ = bf16[64,2048]{1,0:T(8,128)(2,1)S(1)} collective-permute-done((bf16[64,2048]{1,0:T(8,128)(2,1)S(1)}, bf16[64,2048]{1,0:T(8,128)(2,1)S(1)}, u32[]{:S(2)}, u32[]{:S(2)}) %collective-permute-start.31) | collective-permute-done | bytes 262176 | tf_op jit(solution)/shard_map/ppermute | solution.py:1036
  126.5 14.2 %shard_map.95 = (f32[2,2048]{1,0:T(2,128)S(1)}, f32[2,2048]{1,0:T(2,128)S(1)}, bf16[64,2048]{1,0:T(8,128)(2,1)S(1)}, bf16[64,2048]{1,0:T(8,128)(2,1)S(1)}, bf16[...) custom-call(s32[15]{0:T(128)S(1)} %concatenate.57.meta, ...), custom_call_target="tpu_custom_call" | custom-call | bytes 18000000 | tf_op jit(solution)/shard_map/pallas_call | solution.py:1246
  149.5 5.8 %shard_map.96 = (f32[3,2048]{1,0:T(4,128)S(1)}, bf16[2,256,2048]{2,1,0:T(8,128)(2,1)S(1)}, bf16[256,2048]{1,0:T(8,128)(2,1)S(1)}, f32[256,512]{1,0:T(8,128)S(1)}, f32[2,512]{1,0:T(2,128)S(1)}) custom-call(s32[15]{0:T(128)S(1)} %concatenate.57.meta, f32[3,2048]{1,0:T(4,128)S(1)} %get-tuple-element.167.refs_0_, f32[3,2048]{1,0:T(4,128)S(1)} %collective-permute-done.37.refs_1_, ...), custom_call_target="tpu_custom_call" | custom-call | bytes 18000000 | tf_op jit(solution)/shard_map/pallas_call | solution.py:198
  174.4 5.3 %shard_map.98 = (f32[2,512]{1,0:T(2,128)S(1)}, bf16[2,256,256]{2,1,0:T(8,128)(2,1)S(1)}, f32[256,512]{1,0:T(8,128)S(1)}, f32[2,512]{1,0:T(2,128)S(1)}) custom-call(s32[15]{0:T(128)S(1)} %concatenate.57.meta, f32[2,512]{1,0:T(2,128)S(1)} %copy-done.4, f32[2,512]{1,0:T(2,128)S(1)} %collective-permute-done.41.refs_1_, ...), custom_call_target="tpu_custom_call" | custom-call | bytes 18000000 | tf_op jit(solution)/shard_map/pallas_call | solution.py:198
  186.0 6.6 %shard_map.99 = (f32[2,512]{1,0:T(2,128)S(1)}, bf16[2,256,256]{2,1,0:T(8,128)(2,1)S(1)}, f32[256,1024]{1,0:T(8,128)S(1)}, f32[2,1024]{1,0:T(2,128)S(1)}) custom-call(s32[15]{0:T(128)S(1)} %concatenate.57.meta, f32[2,512]{1,0:T(2,128)S(1)} %get-tuple-element.181.refs_0_, f32[2,512]{1,0:T(2,128)S(1)} %collective-permute-done.45.refs_1_, ...), custom_call_target="tpu_custom_call" | custom-call | bytes 18000000 | tf_op jit(solution)/shard_map/pallas_call | solution.py:198
  196.3 7.1 %collective-permute-done.49 = bf16[6144,128]{1,0:T(8,128)(2,1)} collective-permute-done((bf16[6144,128]{1,0:T(8,128)(2,1)}, bf16[6144,128]{1,0:T(8,128)(2,1)}, u32[]{:S(2)}, u32[]{:S(2)}) %collective-permute-start.49) | collective-permute-done | bytes 1572896 | tf_op jit(solution)/shard_map/ppermute | solution.py:1036
  205.3 7.3 %shard_map.100 = (f32[2,1024]{1,0:T(2,128)S(1)}, bf16[4,256,1024]{2,1,0:T(8,128)(2,1)}, f32[4,256,256]{2,1,0:T(8,128)S(1)}, f32[2,256]{1,0:T(2,128)S(1)}) custom-call(s32[15]{0:T(128)S(1)} %concatenate.57.meta, f32[2,1024]{1,0:T(2,128)S(1)} %get-tuple-element.189.refs_0_, f32[2,1024]{1,0:T(2,128)S(1)} %collective-permute-done.50.refs_1_, ...), custom_call_target="tpu_custom_call" | custom-call | bytes 18000000 | tf_op jit(solution)/shard_map/pallas_call | solution.py:1315
  222.1 6.4 %shard_map.102 = (f32[2,256]{1,0:T(2,128)S(1)}, bf16[4,256,256]{2,1,0:T(8,128)(2,1)}, f32[4,256,256]{2,1,0:T(8,128)S(1)}, f32[2,256]{1,0:T(2,128)S(1)}) custom-call(s32[15]{0:T(128)S(1)} %concatenate.57.meta, f32[2,256]{1,0:T(2,128)S(1)} %get-tuple-element.196.refs_0_, f32[2,256]{1,0:T(2,128)S(1)} %collective-permute-done.53.refs_1_, ...), custom_call_target="tpu_custom_call" | custom-call | bytes 18000000 | tf_op jit(solution)/shard_map/pallas_call | solution.py:1344
  232.1 7.5 %shard_map.103.refs_4_ = bf16[8704,128]{1,0:T(8,128)(2,1)} custom-call(s32[15]{0:T(128)S(1)} %concatenate.57.meta, bf16[4,256,256]{2,1,0:T(8,128)(2,1)} %get-tuple-element.200.a1_ref, bf16[4,256,256]{2,1,0:T(8,128)(2,1)} %get-tuple-element.201.d2_ref, bf16[4,256,256]{2,1,0:T(8,128)(2,1)} %get-tuple-element.191.refs_7_.a2_ref, ...), custom_call_target="tpu_custom_call" | custom-call | bytes 18000000 | tf_op jit(solution)/shard_map/pallas_call | solution.py:1361
  241.0 11.1 %collective-permute-done.56 = bf16[3072,128]{1,0:T(8,128)(2,1)S(1)} collective-permute-done((bf16[3072,128]{1,0:T(8,128)(2,1)S(1)}, bf16[3072,128]{1,0:T(8,128)(2,1)S(1)}, u32[]{:S(2)}, u32[]{:S(2)}) %collective-permute-start.56) | collective-permute-done | bytes 786464 | tf_op jit(solution)/shard_map/ppermute | solution.py:1036
  269.7 7.8 %collective-permute-done.64.refs_2_ = bf16[512,256]{1,0:T(8,128)(2,1)S(1)} collective-permute-done((bf16[512,256]{1,0:T(8,128)(2,1)S(1)}, bf16[512,256]{1,0:T(8,128)(2,1)S(1)}, u32[]{:S(2)}, u32[]{:S(2)}) %collective-permute-start.64) | collective-permute-done | bytes 262176 | tf_op jit(solution)/shard_map/ppermute | solution.py:1036
  277.4 6.5 %shard_map.105 = (bf16[4,256,1024]{2,1,0:T(8,128)(2,1)S(1)}, bf16[8704,128]{1,0:T(8,128)(2,1)}) custom-call(s32[15]{0:T(128)S(1)} %concatenate.57.meta, bf16[8,16,16,1024]{3,2,1,0:T(8,128)(2,1)} %x_ref.3, bf16[1024,256]{1,0:T(8,128)(2,1)} %shard_map.85.wa_ref, bf16[1024,256]{1,0:T(8,128)(2,1)} %copy-done.14, ...), custom_call_target="tpu_custom_call", output_to_operand_aliasing={{1}: (8, {})} | custom-call | bytes 18000000 | tf_op jit(solution)/shard_map/pallas_call | solution.py:1409
  286.0 4.5 %collective-permute-start.67 = (bf16[1408,128]{1,0:T(8,128)(2,1)S(1)}, bf16[1408,128]{1,0:T(8,128)(2,1)S(1)}, u32[]{:S(2)}, u32[]{:S(2)}) collective-permute-start(bf16[1408,128]{1,0:T(8,128)(2,1)S(1)} %get-tuple-element.266), channel_id=1, source_target_pairs={{0,4},{1,5},{2,6},{3,7},{4,0},{5,1},{6,2},{7,3},{8,12},{9,13},{10,... | collective-permute-start | bytes 1081352 | tf_op jit(solution)/shard_map/ppermute | solution.py:1036
  292.0 11.8 %collective-permute-done.67 = bf16[1408,128]{1,0:T(8,128)(2,1)S(1)} collective-permute-done((bf16[1408,128]{1,0:T(8,128)(2,1)S(1)}, bf16[1408,128]{1,0:T(8,128)(2,1)S(1)}, u32[]{:S(2)}, u32[]{:S(2)}) %collective-permute-start.67) | collective-permute-done | bytes 360480 | tf_op jit(solution)/shard_map/ppermute | solution.py:1036
  307.8 7.6 %collective-permute-done.70 = bf16[704,128]{1,0:T(8,128)(2,1)S(1)} collective-permute-done((bf16[704,128]{1,0:T(8,128)(2,1)S(1)}, bf16[704,128]{1,0:T(8,128)(2,1)S(1)}, u32[]{:S(2)}, u32[]{:S(2)}) %collective-permute-start.70) | collective-permute-done | bytes 180256 | tf_op jit(solution)/shard_map/ppermute | solution.py:1036
  328.8 4.7 %collective-permute-done.75 = bf16[3072,128]{1,0:T(8,128)(2,1)S(1)} collective-permute-done((bf16[3072,128]{1,0:T(8,128)(2,1)S(1)}, bf16[3072,128]{1,0:T(8,128)(2,1)S(1)}, u32[]{:S(2)}, u32[]{:S(2)}) %collective-permute-start.75) | collective-permute-done | bytes 786464 | tf_op jit(solution)/shard_map/ppermute | solution.py:1049
  347.0 5.2 %collective-permute-done.79 = bf16[272,128]{1,0:T(8,128)(2,1)S(1)} collective-permute-done((bf16[272,128]{1,0:T(8,128)(2,1)S(1)}, bf16[272,128]{1,0:T(8,128)(2,1)S(1)}, u32[]{:S(2)}, u32[]{:S(2)}) %collective-permute-start.79) | collective-permute-done | bytes 69664 | tf_op jit(solution)/shard_map/ppermute | solution.py:1036
  353.5 5.8 %collective-permute-done.80 = bf16[2816,128]{1,0:T(8,128)(2,1)S(1)} collective-permute-done((bf16[2816,128]{1,0:T(8,128)(2,1)S(1)}, bf16[2816,128]{1,0:T(8,128)(2,1)S(1)}, u32[]{:S(2)}, u32[]{:S(2)}) %collective-permute-start.80) | collective-permute-done | bytes 720928 | tf_op jit(solution)/shard_map/ppermute | solution.py:1049
  364.7 8.0 %shard_map.106.refs_0_ = f32[47104,128]{1,0:T(8,128)} custom-call(s32[15]{0:T(128)S(1)} %concatenate.57.meta, bf16[6144,128]{1,0:T(8,128)(2,1)S(1)} %pad_maximum_fusion.refs_0_, bf16[6144,128]{1,0:T(8,128)(2,1)S(1)} %collective-permute-done.81.refs_1_, bf16[6144,128]{1,0:T(8,128)(2,1)S(1)} %collective-permute-done.82.refs_2_, ...), custom_call_target="tpu_custom_call" | custom-call | bytes 28800000 | tf_op jit(solution)/shard_map/pallas_call | solution.py:1458
  374.7 6.7 %collective-permute-done.85 = bf16[64,2048]{1,0:T(8,128)(2,1)S(1)} collective-permute-done((bf16[64,2048]{1,0:T(8,128)(2,1)S(1)}, bf16[64,2048]{1,0:T(8,128)(2,1)S(1)}, u32[]{:S(2)}, u32[]{:S(2)}) %collective-permute-start.85) | collective-permute-done | bytes 262176 | tf_op jit(solution)/shard_map/ppermute | solution.py:1036
  382.3 4.1 collective-permute-start.89
  386.9 4.3 %collective-permute-start.99 = (f32[2,5120]{1,0:T(2,128)S(1)}, f32[2,5120]{1,0:T(2,128)S(1)}, u32[]{:S(2)}, u32[]{:S(2)}) collective-permute-start(f32[2,5120]{1,0:T(2,128)S(1)} %fusion.8), channel_id=1, source_target_pairs={{0,8},{1,9},{2,10},{3,11},{4,12},{5,13},{6,14},{7,15},{8,0},{9,1},... | collective-permute-start | bytes 122888 | tf_op jit(solution)/shard_map/ppermute | solution.py:1036
  394.0 8.9 %shard_map.107 = bf16[8,262144]{1,0:T(8,128)(2,1)} custom-call(s32[15]{0:T(128)S(1)} %concatenate.57.meta, bf16[4,256,1024]{2,1,0:T(8,128)(2,1)S(1)} %get-tuple-element.243.x_ref, bf16[4,256,1024]{2,1,0:T(8,128)(2,1)S(1)} %collective-permute-done.88.xg_ref, bf16[4,64,2048]{2,1,0:T(8,128)(2,1)S(1)} %pad_maximum_fusion.2.y_ref, ...), custom_call_target="tpu_custom_call" | custom-call | bytes 32400000 | tf_op jit(solution)/shard_map/pallas_call | solution.py:1466
  409.1 4.5 %shard_map.108.refs_0_ = f32[47104,128]{1,0:T(8,128)} custom-call(s32[15]{0:T(128)S(1)} %concatenate.57.meta, f32[47104,128]{1,0:T(8,128)} %shard_map.106.refs_0_, bf16[5632,128]{1,0:T(8,128)(2,1)S(1)} %pad_maximum_fusion.1.refs_1_, bf16[5632,128]{1,0:T(8,128)(2,1)S(1)} %collective-permute-done.91.refs_2_, ...), custom_call_target="tpu_custom_call", output_to_operand_aliasing={{}: (1, {})} | custom-call | bytes 18000000 | tf_op jit(solution)/shard_map/pallas_call | solution.py:1478
  415.9 4.4 %shard_map.109 = f32[47104,128]{1,0:T(8,128)} custom-call(s32[15]{0:T(128)S(1)} %concatenate.57.meta, f32[47104,128]{1,0:T(8,128)} %shard_map.108.refs_0_, bf16[5632,128]{1,0:T(8,128)(2,1)S(1)} %pad_maximum_fusion.1.refs_1_, bf16[5632,128]{1,0:T(8,128)(2,1)S(1)} %collective-permute-done.91.refs_2_, ...), custom_call_target="tpu_custom_call", output_to_operand_aliasing={{}: (1, {})} | custom-call | bytes 18000000 | tf_op jit(solution)/shard_map/pallas_call | solution.py:1482
  (290 shorter events, 206.4 us)
Async XLA Ops:
  15.7 20.0 %collective-permute-start.2 = (bf16[272,256]{1,0:T(8,128)(2,1)S(1)}, bf16[272,256]{1,0:T(8,128)(2,1)S(1)}, u32[]{:S(2)}, u32[]{:S(2)}) collective-permute-start(bf16[272,256]{1,0:T(8,128)(2,1)S(1)} %get-tuple-element.130), channel_id=1, source_target_pairs={{0,4},{1,5},{2,6},{3,7},{4,0},{5,1},{6,2},{7,3},{8,12},{9,13},{10,... | collective-permute-start | bytes 417800 | tf_op jit(solution)/shard_map/ppermute | solution.py:1036
  18.9 16.9 %collective-permute-start.3 = (bf16[272,256]{1,0:T(8,128)(2,1)S(1)}, bf16[272,256]{1,0:T(8,128)(2,1)S(1)}, u32[]{:S(2)}, u32[]{:S(2)}) collective-permute-start(bf16[272,256]{1,0:T(8,128)(2,1)S(1)} %get-tuple-element.131), channel_id=1, source_target_pairs={{0,8},{1,9},{2,10},{3,11},{4,12},{5,13},{6,14},{7,15},{8,0},{9,1},... | collective-permute-start | bytes 417800 | tf_op jit(solution)/shard_map/ppermute | solution.py:1036
  26.1 23.7 %collective-permute-start.5 = (bf16[10240,256]{1,0:T(8,128)(2,1)}, bf16[10240,256]{1,0:T(8,128)(2,1)}, u32[]{:S(2)}, u32[]{:S(2)}) collective-permute-start(bf16[10240,256]{1,0:T(8,128)(2,1)} %shard_map.87.refs_7_.refs_8_.refs_12_.refs_14_.refs_11_), channel_id=1, source_target_pairs={{0,16},{16,0},{1,17},{17,1},{2,18},{18,2},{3,19},{19,3},{4,20},{20... | collective-permute-start | bytes 15728648 | tf_op jit(solution)/shard_map/ppermute | solution.py:1031
  38.4 52.5 %collective-permute-start.18 = (bf16[13312,256]{1,0:T(8,128)(2,1)}, bf16[13312,256]{1,0:T(8,128)(2,1)}, u32[]{:S(2)}, u32[]{:S(2)}) collective-permute-start(bf16[13312,256]{1,0:T(8,128)(2,1)} %shard_map.89.refs_8_.refs_14_.refs_12_), channel_id=1, source_target_pairs={{16,0},{17,1},{18,2},{19,3},{20,4},{21,5},{22,6},{23,7},{24,8},{25... | collective-permute-start | bytes 20447240 | tf_op jit(solution)/shard_map/ppermute | solution.py:1166
  42.9 18.1 %collective-permute-start.10 = (bf16[64,1024]{1,0:T(8,128)(2,1)}, bf16[64,1024]{1,0:T(8,128)(2,1)S(1)}, u32[]{:S(2)}, u32[]{:S(2)}) collective-permute-start(bf16[64,1024]{1,0:T(8,128)(2,1)} %get-tuple-element.140), channel_id=1, source_target_pairs={{0,8},{1,9},{2,10},{3,11},{4,12},{5,13},{6,14},{7,15},{8,0},{9,1},... | collective-permute-start | bytes 393224 | tf_op jit(solution)/shard_map/ppermute | solution.py:1036
  46.4 25.1 %collective-permute-start.14 = (bf16[64,1024]{1,0:T(8,128)(2,1)}, bf16[64,1024]{1,0:T(8,128)(2,1)S(1)}, u32[]{:S(2)}, u32[]{:S(2)}) collective-permute-start(bf16[64,1024]{1,0:T(8,128)(2,1)} %get-tuple-element.145), channel_id=1, source_target_pairs={{0,12},{1,13},{2,14},{3,15},{4,8},{5,9},{6,10},{7,11},{8,4},{9,5},... | collective-permute-start | bytes 393224 | tf_op jit(solution)/shard_map/ppermute | solution.py:1036
  101.4 21.4 %collective-permute-start.31 = (bf16[64,2048]{1,0:T(8,128)(2,1)S(1)}, bf16[64,2048]{1,0:T(8,128)(2,1)S(1)}, u32[]{:S(2)}, u32[]{:S(2)}) collective-permute-start(bf16[64,2048]{1,0:T(8,128)(2,1)S(1)} %get-tuple-element.160), channel_id=1, source_target_pairs={{0,8},{1,9},{2,10},{3,11},{4,12},{5,13},{6,14},{7,15},{8,0},{9,1},... | collective-permute-start | bytes 786440 | tf_op jit(solution)/shard_map/ppermute | solution.py:1036
  108.2 15.8 %collective-permute-start.32 = (bf16[64,2048]{1,0:T(8,128)(2,1)S(1)}, bf16[64,2048]{1,0:T(8,128)(2,1)S(1)}, u32[]{:S(2)}, u32[]{:S(2)}) collective-permute-start(bf16[64,2048]{1,0:T(8,128)(2,1)S(1)} %get-tuple-element.161), channel_id=1, source_target_pairs={{0,12},{1,13},{2,14},{3,15},{4,8},{5,9},{6,10},{7,11},{8,4},{9,5},... | collective-permute-start | bytes 786440 | tf_op jit(solution)/shard_map/ppermute | solution.py:1036
  166.7 36.8 %collective-permute-start.49 = (bf16[6144,128]{1,0:T(8,128)(2,1)}, bf16[6144,128]{1,0:T(8,128)(2,1)}, u32[]{:S(2)}, u32[]{:S(2)}) collective-permute-start(bf16[6144,128]{1,0:T(8,128)(2,1)} %get-tuple-element.252), channel_id=1, source_target_pairs={{0,4},{1,5},{2,6},{3,7},{4,0},{5,1},{6,2},{7,3},{8,12},{9,13},{10,... | collective-permute-start | bytes 4718600 | tf_op jit(solution)/shard_map/ppermute | solution.py:1036
  216.3 35.7 %collective-permute-start.56 = (bf16[3072,128]{1,0:T(8,128)(2,1)S(1)}, bf16[3072,128]{1,0:T(8,128)(2,1)S(1)}, u32[]{:S(2)}, u32[]{:S(2)}) collective-permute-start(bf16[3072,128]{1,0:T(8,128)(2,1)S(1)} %get-tuple-element.258), channel_id=1, source_target_pairs={{0,8},{1,9},{2,10},{3,11},{4,12},{5,13},{6,14},{7,15},{8,0},{9,1},... | collective-permute-start | bytes 2359304 | tf_op jit(solution)/shard_map/ppermute | solution.py:1036
  239.8 25.6 %collective-permute-start.61 = (bf16[5632,128]{1,0:T(8,128)(2,1)S(1)}, bf16[5632,128]{1,0:T(8,128)(2,1)S(1)}, u32[]{:S(2)}, u32[]{:S(2)}) collective-permute-start(bf16[5632,128]{1,0:T(8,128)(2,1)S(1)} %get-tuple-element.254), channel_id=1, source_target_pairs={{0,1},{1,0},{2,3},{3,2},{4,5},{5,4},{6,7},{7,6},{8,9},{9,8},{10,11... | collective-permute-start | bytes 4325384 | tf_op jit(solution)/shard_map/ppermute | solution.py:1049
  256.0 21.4 %collective-permute-start.64 = (bf16[512,256]{1,0:T(8,128)(2,1)S(1)}, bf16[512,256]{1,0:T(8,128)(2,1)S(1)}, u32[]{:S(2)}, u32[]{:S(2)}) collective-permute-start(bf16[512,256]{1,0:T(8,128)(2,1)S(1)} %get-tuple-element.214), channel_id=1, source_target_pairs={{0,8},{1,9},{2,10},{3,11},{4,12},{5,13},{6,14},{7,15},{8,0},{9,1},... | collective-permute-start | bytes 786440 | tf_op jit(solution)/shard_map/ppermute | solution.py:1036
  258.6 18.8 %collective-permute-start.65 = (bf16[512,256]{1,0:T(8,128)(2,1)S(1)}, bf16[512,256]{1,0:T(8,128)(2,1)S(1)}, u32[]{:S(2)}, u32[]{:S(2)}) collective-permute-start(bf16[512,256]{1,0:T(8,128)(2,1)S(1)} %get-tuple-element.215), channel_id=1, source_target_pairs={{0,12},{1,13},{2,14},{3,15},{4,8},{5,9},{6,10},{7,11},{8,4},{9,5},... | collective-permute-start | bytes 786440 | tf_op jit(solution)/shard_map/ppermute | solution.py:1036
  265.9 19.8 %collective-permute-start.66 = (bf16[2816,128]{1,0:T(8,128)(2,1)S(1)}, bf16[2816,128]{1,0:T(8,128)(2,1)S(1)}, u32[]{:S(2)}, u32[]{:S(2)}) collective-permute-start(bf16[2816,128]{1,0:T(8,128)(2,1)S(1)} %get-tuple-element.260), channel_id=1, source_target_pairs={{0,2},{1,3},{2,0},{3,1},{4,6},{5,7},{6,4},{7,5},{8,10},{9,11},{10,... | collective-permute-start | bytes 2162696 | tf_op jit(solution)/shard_map/ppermute | solution.py:1049
  285.6 18.2 %collective-permute-start.68 = (bf16[4352,128]{1,0:T(8,128)(2,1)S(1)}, bf16[4352,128]{1,0:T(8,128)(2,1)S(1)}, u32[]{:S(2)}, u32[]{:S(2)}) collective-permute-start(bf16[4352,128]{1,0:T(8,128)(2,1)S(1)} %get-tuple-element.256), channel_id=1, source_target_pairs={{0,16},{16,0},{1,17},{17,1},{2,18},{18,2},{3,19},{19,3},{4,20},{20... | collective-permute-start | bytes 3342344 | tf_op jit(solution)/shard_map/ppermute | solution.py:1031
  286.0 17.7 %collective-permute-start.67 = (bf16[1408,128]{1,0:T(8,128)(2,1)S(1)}, bf16[1408,128]{1,0:T(8,128)(2,1)S(1)}, u32[]{:S(2)}, u32[]{:S(2)}) collective-permute-start(bf16[1408,128]{1,0:T(8,128)(2,1)S(1)} %get-tuple-element.266), channel_id=1, source_target_pairs={{0,4},{1,5},{2,6},{3,7},{4,0},{5,1},{6,2},{7,3},{8,12},{9,13},{10,... | collective-permute-start | bytes 1081352 | tf_op jit(solution)/shard_map/ppermute | solution.py:1036
  290.5 56.3 %collective-permute-start.97 = (f32[2,5120]{1,0:T(2,128)S(1)}, f32[2,5120]{1,0:T(2,128)S(1)}, u32[]{:S(2)}, u32[]{:S(2)}) collective-permute-start(f32[2,5120]{1,0:T(2,128)S(1)} %broadcast_select_fusion), channel_id=1, source_target_pairs={{0,16},{16,0},{1,17},{17,1},{2,18},{18,2},{3,19},{19,3},{4,20},{20... | collective-permute-start | bytes 122888 | tf_op jit(solution)/shard_map/ppermute | solution.py:1031
  290.8 14.5 %collective-permute-start.69 = (bf16[768,128]{1,0:T(8,128)(2,1)S(1)}, bf16[768,128]{1,0:T(8,128)(2,1)S(1)}, u32[]{:S(2)}, u32[]{:S(2)}) collective-permute-start(bf16[768,128]{1,0:T(8,128)(2,1)S(1)} %add_convert_fusion.9), channel_id=1, source_target_pairs={{0,8},{1,9},{2,10},{3,11},{4,12},{5,13},{6,14},{7,15},{8,0},{9,1},... | collective-permute-start | bytes 589832 | tf_op jit(solution)/shard_map/ppermute | solution.py:1036
  305.3 16.1 %collective-permute-start.72 = (bf16[1536,128]{1,0:T(8,128)(2,1)S(1)}, bf16[1536,128]{1,0:T(8,128)(2,1)S(1)}, u32[]{:S(2)}, u32[]{:S(2)}) collective-permute-start(bf16[1536,128]{1,0:T(8,128)(2,1)S(1)} %pad_maximum_fusion.6), channel_id=1, source_target_pairs={{0,4},{1,5},{2,6},{3,7},{4,0},{5,1},{6,2},{7,3},{8,12},{9,13},{10,... | collective-permute-start | bytes 1179656 | tf_op jit(solution)/shard_map/ppermute | solution.py:1036
  333.6 27.4 %collective-permute-start.83 = (bf16[6144,128]{1,0:T(8,128)(2,1)S(1)}, bf16[6144,128]{1,0:T(8,128)(2,1)S(1)}, u32[]{:S(2)}, u32[]{:S(2)}) collective-permute-start(bf16[6144,128]{1,0:T(8,128)(2,1)S(1)} %pad_maximum_fusion.refs_0_), channel_id=1, source_target_pairs={{16,18},{17,19},{18,16},{19,17},{20,22},{21,23},{22,20},{23,21},{2... | collective-permute-start | bytes 4718600 | tf_op jit(solution)/shard_map/ppermute | solution.py:1087
  334.5 28.8 %collective-permute-start.82 = (bf16[6144,128]{1,0:T(8,128)(2,1)S(1)}, bf16[6144,128]{1,0:T(8,128)(2,1)S(1)}, u32[]{:S(2)}, u32[]{:S(2)}) collective-permute-start(bf16[6144,128]{1,0:T(8,128)(2,1)S(1)} %pad_maximum_fusion.refs_0_), channel_id=1, source_target_pairs={{0,17},{1,16},{2,19},{3,18},{4,21},{5,20},{6,23},{7,22},{8,25},{9,... | collective-permute-start | bytes 4718600 | tf_op jit(solution)/shard_map/ppermute | solution.py:1087
  340.2 19.1 %collective-permute-start.80 = (bf16[2816,128]{1,0:T(8,128)(2,1)S(1)}, bf16[2816,128]{1,0:T(8,128)(2,1)S(1)}, u32[]{:S(2)}, u32[]{:S(2)}) collective-permute-start(bf16[2816,128]{1,0:T(8,128)(2,1)S(1)} %pad_maximum_fusion.4), channel_id=1, source_target_pairs={{0,2},{1,3},{2,0},{3,1},{4,6},{5,7},{6,4},{7,5},{8,10},{9,11},{10,... | collective-permute-start | bytes 2162696 | tf_op jit(solution)/shard_map/ppermute | solution.py:1049
  345.4 19.2 %collective-permute-start.81 = (bf16[6144,128]{1,0:T(8,128)(2,1)S(1)}, bf16[6144,128]{1,0:T(8,128)(2,1)S(1)}, u32[]{:S(2)}, u32[]{:S(2)}) collective-permute-start(bf16[6144,128]{1,0:T(8,128)(2,1)S(1)} %pad_maximum_fusion.refs_0_), channel_id=1, source_target_pairs={{0,16},{1,17},{2,18},{3,19},{4,20},{5,21},{6,22},{7,23},{8,24},{9,... | collective-permute-start | bytes 4718600 | tf_op jit(solution)/shard_map/ppermute | solution.py:1087
  352.2 39.1 %collective-permute-start.88 = (bf16[4,256,1024]{2,1,0:T(8,128)(2,1)S(1)}, bf16[4,256,1024]{2,1,0:T(8,128)(2,1)S(1)}, u32[]{:S(2)}, u32[]{:S(2)}) collective-permute-start(bf16[4,256,1024]{2,1,0:T(8,128)(2,1)S(1)} %get-tuple-element.243.x_ref), channel_id=1, source_target_pairs={{16,0},{17,1},{18,2},{19,3},{20,4},{21,5},{22,6},{23,7},{24,8},{25... | collective-permute-start | bytes 6291464 | tf_op jit(solution)/shard_map/ppermute | solution.py:1424
  361.1 20.4 %collective-permute-start.85 = (bf16[64,2048]{1,0:T(8,128)(2,1)S(1)}, bf16[64,2048]{1,0:T(8,128)(2,1)S(1)}, u32[]{:S(2)}, u32[]{:S(2)}) collective-permute-start(bf16[64,2048]{1,0:T(8,128)(2,1)S(1)} %copy-done.8), channel_id=1, source_target_pairs={{0,8},{1,9},{2,10},{3,11},{4,12},{5,13},{6,14},{7,15},{8,0},{9,1},... | collective-permute-start | bytes 786440 | tf_op jit(solution)/shard_map/ppermute | solution.py:1036
  363.3 18.8 %collective-permute-start.86 = (bf16[64,2048]{1,0:T(8,128)(2,1)S(1)}, bf16[64,2048]{1,0:T(8,128)(2,1)S(1)}, u32[]{:S(2)}, u32[]{:S(2)}) collective-permute-start(bf16[64,2048]{1,0:T(8,128)(2,1)S(1)} %copy-done.6), channel_id=1, source_target_pairs={{0,12},{1,13},{2,14},{3,15},{4,8},{5,9},{6,10},{7,11},{8,4},{9,5},... | collective-permute-start | bytes 786440 | tf_op jit(solution)/shard_map/ppermute | solution.py:1036
  364.7 22.2 %collective-permute-start.98 = (f32[2,5120]{1,0:T(2,128)S(1)}, f32[2,5120]{1,0:T(2,128)S(1)}, u32[]{:S(2)}, u32[]{:S(2)}) collective-permute-start(f32[2,5120]{1,0:T(2,128)S(1)} %select_add_fusion), channel_id=1, source_target_pairs={{0,4},{1,5},{2,6},{3,7},{4,0},{5,1},{6,2},{7,3},{8,12},{9,13},{10,... | collective-permute-start | bytes 122888 | tf_op jit(solution)/shard_map/ppermute | solution.py:1036
  381.4 25.0 %collective-permute-start.93 = (bf16[5632,128]{1,0:T(8,128)(2,1)S(1)}, bf16[5632,128]{1,0:T(8,128)(2,1)S(1)}, u32[]{:S(2)}, u32[]{:S(2)}) collective-permute-start(bf16[5632,128]{1,0:T(8,128)(2,1)S(1)} %pad_maximum_fusion.1.refs_1_), channel_id=1, source_target_pairs={{16,18},{17,19},{18,16},{19,17},{20,22},{21,23},{22,20},{23,21},{2... | collective-permute-start | bytes 4325384 | tf_op jit(solution)/shard_map/ppermute | solution.py:1087
  386.5 16.4 %collective-permute-start.90 = (bf16[1088,128]{1,0:T(8,128)(2,1)S(1)}, bf16[1088,128]{1,0:T(8,128)(2,1)S(1)}, u32[]{:S(2)}, u32[]{:S(2)}) collective-permute-start(bf16[1088,128]{1,0:T(8,128)(2,1)S(1)} %pad_maximum_fusion.8), channel_id=1, source_target_pairs={{0,2},{1,3},{2,0},{3,1},{4,6},{5,7},{6,4},{7,5},{8,10},{9,11},{10,... | collective-permute-start | bytes 835592 | tf_op jit(solution)/shard_map/ppermute | solution.py:1049
  386.9 18.2 %collective-permute-start.99 = (f32[2,5120]{1,0:T(2,128)S(1)}, f32[2,5120]{1,0:T(2,128)S(1)}, u32[]{:S(2)}, u32[]{:S(2)}) collective-permute-start(f32[2,5120]{1,0:T(2,128)S(1)} %fusion.8), channel_id=1, source_target_pairs={{0,8},{1,9},{2,10},{3,11},{4,12},{5,13},{6,14},{7,15},{8,0},{9,1},... | collective-permute-start | bytes 122888 | tf_op jit(solution)/shard_map/ppermute | solution.py:1036
  391.3 17.8 %collective-permute-start.92 = (bf16[5632,128]{1,0:T(8,128)(2,1)S(1)}, bf16[5632,128]{1,0:T(8,128)(2,1)S(1)}, u32[]{:S(2)}, u32[]{:S(2)}) collective-permute-start(bf16[5632,128]{1,0:T(8,128)(2,1)S(1)} %pad_maximum_fusion.1.refs_1_), channel_id=1, source_target_pairs={{0,17},{1,16},{2,19},{3,18},{4,21},{5,20},{6,23},{7,22},{8,25},{9,... | collective-permute-start | bytes 4325384 | tf_op jit(solution)/shard_map/ppermute | solution.py:1087
  392.7 16.4 %collective-permute-start.91 = (bf16[5632,128]{1,0:T(8,128)(2,1)S(1)}, bf16[5632,128]{1,0:T(8,128)(2,1)S(1)}, u32[]{:S(2)}, u32[]{:S(2)}) collective-permute-start(bf16[5632,128]{1,0:T(8,128)(2,1)S(1)} %pad_maximum_fusion.1.refs_1_), channel_id=1, source_target_pairs={{0,16},{1,17},{2,18},{3,19},{4,20},{5,21},{6,22},{7,23},{8,24},{9,... | collective-permute-start | bytes 4325384 | tf_op jit(solution)/shard_map/ppermute | solution.py:1087
  (87 other events, 677.6 us)
where the time goes:
time: 428 us; the launch traced here: 421 us
  starting transfers between devices  137 us (32%)
  Pallas kernels  135 us (32%)
  waiting for transfers between devices  129 us (30%)
  local copies, waits for them, and re-layouts  10.6 us (2%)
  other arithmetic  6.62 us (2%)
    ppermute x29, waiting for transfers between devices, xor_permute(): return lax.ppermute(value, 'dp', [(i, i ^ mask) for i in range(count)])  77 us
    ppermute x48, starting transfers between devices, plane_turn(): return lax.ppermute(value, ('pipe', 'dp'), pairs)  58.5 us
    ppermute x29, starting transfers between devices, xor_permute(): return lax.ppermute(value, 'dp', [(i, i ^ mask) for i in range(count)])  46.2 us
    pallas_call x11, Pallas kernels, single(): return made(meta, *[array for array, _ in ins])  45.1 us
    ppermute x48, waiting for transfers between devices, plane_turn(): return lax.ppermute(value, ('pipe', 'dp'), pairs)  36 us
    pallas_call x1, Pallas kernels, on_device(): call(turn, [shape_of((2, C1), F32)] * 2 + some((PIX1, C1), BF16) + [shape...  14.2 us
    ppermute x9, starting transfers between devices, to_core(): arrived.append(lax.ppermute(both, ('pipe', 'dp'), pairs))  13.7 us
    ppermute x10, starting transfers between devices, swap_cores(): return lax.ppermute(value, 'pipe', [(0, 1), (1, 0)])  10.9 us
  transfers between devices with their start and end apart: 100, of which 43 were waited for; matrix products, arithmetic and copies ran while one was open for 2% of the time, Pallas kernels for 21%

commit v1 on v0

--- a/solution.py
+++ b/solution.py
@@ -758,9 +758,9 @@
 def sides_grad(meta, sa_ref, sb_ref, la_ref, lb_ref, ea_ref, eb_ref, out_ref):
     half = C1 // 2
     side = dot_tn(sa_ref[...], ea_ref[0][:, half:]) + dot_tn(sb_ref[...], eb_ref[0][:, half:])
-    put_shards(out_ref, SIDES, 0, meta[CORE], True, side)
+    put_shards(out_ref, SIDES, 0, meta[CORE], False, side)
     last = dot_tn(la_ref[...], ea_ref[0][:, :half]) + dot_tn(lb_ref[...], eb_ref[0][:, :half])
-    put_shards(out_ref, SIDES, C0 // 2, meta[CORE], True, last)
+    put_shards(out_ref, SIDES, C0 // 2, meta[CORE], False, last)
 
 
 def middle_grad(meta, sa_ref, sb_ref, la_ref, lb_ref, ma_ref, mb_ref, fa_ref, fb_ref, out_ref):
@@ -1278,16 +1278,8 @@
     )
     s8 = shared(st)
     other = swap_cores(er[1:])
-    sides = single(
-        sides_grad,
-        meta,
-        far(src, src_there, b2, b2_there) + near(er, other),
-        [((16 * SIDES, 128), BF16, False)],
-        limit=40,
-    )[0]
-    s8[0] = pin(s8[0], sides)
+    s8[0] = pin(s8[0], other)
     low, high = level & 1, level >> 1
-    sides = added(part_at(sides, low, 2), xor_permute(part_at(sides, 1 - low, 2), 4))
     tot8, e2r, g1, st = single(
         back_two,
         meta,
@@ -1297,7 +1289,14 @@
     )
     s9 = shared(st)
     other2 = swap_cores(e2r[1:])
-    s9[0] = pin(s9[0], other2)
+    sides = single(
+        sides_grad,
+        meta,
+        far(src, src_there, b2, b2_there) + [(pin(er, st), False), (other, False)],
+        [((16 * SIDES, 128), BF16, False)],
+        limit=40,
+    )[0]
+    s9[0] = pin(s9[0], other2, sides)
     made = single(
         back_three,
         meta,
@@ -1310,8 +1309,8 @@
 
     s10 = shared(st)
     other1 = swap_cores(e1r[1:])
-    s10[0] = pin(s10[0], other1, sides)
-    half_there = xor_permute(part_at(sides, 1 - high, 2), 8)
+    y_back = [y_out[0], xor_permute(y_out[1], 4), xor_permute(y_out[2], 8)]
+    s10[0] = pin(s10[0], other1, y_back[1])
     tot10, d3, g2, st = call(
         last_one,
         [
@@ -1340,7 +1339,8 @@
         [((16 * MIDDLE, 128), BF16, False)],
         limit=40,
     )[0]
-    s11[0] = pin(s11[0], middle)
+    y_back.append(xor_permute(pin(y_out[3], tot9), 12))
+    s11[0] = pin(s11[0], middle, y_back[2])
     tot11, d2, g1, st = call(
         last_two,
         [
@@ -1366,8 +1366,9 @@
         full(2 * C0 + 2 * 9 * M0 + 8 * M0, 128),
         [pltpu.VMEM((M0, 9 * M0), F32), pltpu.VMEM((M0, C0), F32)],
     )(meta, in_hbm(a1), in_hbm(d2), in_hbm(a2b), in_hbm(d3))
-    sides = upper_sum(added(part_at(sides, high, 2), half_there))
-    s12[0] = pin(s12[0], front, sides)
+    one, two = place >> 1, place & 1
+    kept, sent = part_at(middle, one, 2), part_at(middle, 1 - one, 2)
+    s12[0] = pin(s12[0], front, y_back[3], kept, sent)
     made = single(
         last_three,
         meta,
@@ -1394,16 +1395,15 @@
     def joined(value, got):
         return step(lax.optimization_barrier(jnp.concatenate([after(value), got], axis=0)))
 
-    one, two = place >> 1, place & 1
-    middle = pin(middle, *s12[1:])
-    middle_got = plane_turn(other_half(middle, one), 1)
-    sides_got = plane_turn(pin(other_half(sides, one), *s12[1:]), 1)
+    sides = pin(sides, *s12[1:])
+    sides_got = plane_turn(other_half(sides, one), 1)
     sides = half_sum(sides, one, sides_got)
     sides_got = plane_turn(other_half(sides, two), 2)
-    middle = half_sum(middle, one, middle_got)
-    middle_got = plane_turn(other_half(middle, two), 2)
+    middle_got = plane_turn(after(sent), 1)
+    y_back = step(lax.optimization_barrier(jnp.stack([after(y_back[0])] + y_back[1:])))
+    y_there = lax.ppermute(y_back, "pipe", [(0, 1)])
     sides = half_sum(sides, two, sides_got)
-    sides_got = xor_permute(sides, 8)
+    sides_got = xor_permute(other_half(sides, low), 4)
     backs[0] = after(backs[0])
     rows = front.shape[0]
     gx, front = call(
@@ -1419,48 +1419,40 @@
     )(meta, images, *w1, *backs, front)
     step(front)
     front_got = swap_cores(other_half(front, core))
+    x_there = lax.ppermute(gx, "pipe", [(1, 0)])
+    sides = half_sum(sides, low, sides_got)
+    sides_got = xor_permute(other_half(sides, high), 8)
+    middle = step(added(after(kept), middle_got))
+    middle_got = plane_turn(other_half(middle, two), 2)
+    front = half_sum(front, core, front_got)
+    front_got = plane_turn(other_half(front, one), 1)
+    sides = upper_sum(half_sum(sides, high, sides_got))
+    sides_got = xor_permute(sides, 8)
     middle = half_sum(middle, two, middle_got)
     middle_got = xor_permute(other_half(middle, low), 4)
-    x_there = lax.ppermute(gx, "pipe", [(1, 0)])
+    sides = joined(sides, sides_got)
+    sides_got = xor_permute(sides, 4)
+    front = half_sum(front, one, front_got)
+    front_got = plane_turn(other_half(front, two), 2)
     middle = half_sum(middle, low, middle_got)
     middle_got = xor_permute(other_half(middle, high), 8)
-    front = half_sum(front, core, front_got)
-    front_got = plane_turn(other_half(front, one), 1)
+    front = half_sum(front, two, front_got)
+    front_got = xor_permute(other_half(front, low), 4)
     sides = joined(sides, sides_got)
-    sides_got = xor_permute(sides, 4)
+    sides_got = plane_turn(sides, 2)
     middle = upper_sum(half_sum(middle, high, middle_got))
     middle_got = xor_permute(middle, 8)
-    front = half_sum(front, one, front_got)
-    front_got = plane_turn(other_half(front, two), 2)
-    sides = joined(sides, sides_got)
-    sides_got = plane_turn(sides, 2)
-    front = half_sum(front, two, front_got)
-    front_got = xor_permute(other_half(front, low), 4)
+    front = half_sum(front, low, front_got)
+    front_got = xor_permute(other_half(front, high), 8)
+    sides = to_core(joined(sides, sides_got), 1)
     middle = joined(middle, middle_got)
     middle_got = xor_permute(middle, 4)
-    sides = to_core(joined(sides, sides_got), 1)
-    y_back = [y_out[0]] + [xor_permute(after(y_out[k]), 4 * k) for k in (1, 2, 3)]
-    front = half_sum(front, low, front_got)
-    front_got = xor_permute(other_half(front, high), 8)
+    front = upper_sum(half_sum(front, high, front_got))
+    front_got = xor_permute(front, 8)
     middle = joined(middle, middle_got)
     middle_got = plane_turn(middle, 2)
-    front = upper_sum(half_sum(front, high, front_got))
-    front_got = xor_permute(front, 8)
     front = joined(front, front_got)
     front_got = xor_permute(front, 4)
-
-    whole = shape_of((GRAD_ROWS, 128), F32)
-    block_at = lambda at: pl.BlockSpec((PACK_ROWS, 128), lambda s, meta: (s + at, 0))
-    side_spec, mid_spec = full(8 * SIDES, 128), full(8 * MIDDLE, 128)
-    middle = to_core(joined(middle, middle_got), 1)
-    sides[0] = after(sides[0])
-    steps = GRAD_ROWS // PACK_ROWS - 11
-    grads = call(pack_sides, whole, (steps,), [side_spec] * 4, block_at(11), micros=8)(meta, *sides)
-    step(grads)
-    y_back = step(lax.optimization_barrier(jnp.stack([after(y_back[0])] + y_back[1:])))
-    y_there = lax.ppermute(y_back, "pipe", [(0, 1)])
-    front = joined(front, front_got)
-    front_got = plane_turn(front, 2)
     strip = lambda s, meta: (0, s, 0)
     strip_y = lambda s, meta: (0, jnp.minimum(s, 7), 0)
     boundary = call(
@@ -1473,6 +1465,18 @@
         micros=9,
     )(meta, after(gx), x_there, y_back, y_there)
     step(boundary)
+    middle = joined(middle, middle_got)
+    front = joined(front, front_got)
+    front_got = plane_turn(front, 2)
+    middle = to_core(middle, 1)
+
+    whole = shape_of((GRAD_ROWS, 128), F32)
+    block_at = lambda at: pl.BlockSpec((PACK_ROWS, 128), lambda s, meta: (s + at, 0))
+    side_spec, mid_spec = full(8 * SIDES, 128), full(8 * MIDDLE, 128)
+    steps = GRAD_ROWS // PACK_ROWS - 11
+    sides[0] = after(sides[0])
+    grads = call(pack_sides, whole, (steps,), [side_spec] * 4, block_at(11), micros=8)(meta, *sides)
+    step(grads)
     fronts = to_core(joined(front, front_got), 0)
     middle[0] = after(middle[0])
     grads = call(

time: 428 us -> 409 us (0.956)
  waiting for transfers between devices: 129 us -> 115 us
    ppermute x29, waiting for transfers between devices: 77 us -> 51.3 us  [xor_permute(): return lax.ppermute(value, 'dp', [(i, i ^ mask) for i in range(count)])]
    ppermute x48, waiting for transfers between devices: 36 us -> 52.7 us  [plane_turn(): return lax.ppermute(value, ('pipe', 'dp'), pairs)]
    ppermute x29, starting transfers between devices: 46.2 us -> 41.3 us  [xor_permute(): return lax.ppermute(value, 'dp', [(i, i ^ mask) for i in range(count)])]
    ppermute x10, waiting for transfers between devices: 10.1 us -> 5.77 us  [swap_cores(): return lax.ppermute(value, 'pipe', [(0, 1), (1, 0)])]
  transfers between devices with their start and end apart: 100 -> 100, of which waited for: 43 -> 39; matrix products, arithmetic and copies ran while one was open for 2% -> 2% of each run, Pallas kernels for 21% -> 24%
where the time goes in v1:
time: 409 us; the launch traced here: 402 us
  starting transfers between devices  136 us (33%)
  Pallas kernels  134 us (33%)
  waiting for transfers between devices  115 us (28%)
  local copies, waits for them, and re-layouts  8.28 us (2%)
  other arithmetic  5.21 us (1%)
    ppermute x48, starting transfers between devices, plane_turn(): return lax.ppermute(value, ('pipe', 'dp'), pairs)  62.6 us
    ppermute x48, waiting for transfers between devices, plane_turn(): return lax.ppermute(value, ('pipe', 'dp'), pairs)  52.7 us
    ppermute x29, waiting for transfers between devices, xor_permute(): return lax.ppermute(value, 'dp', [(i, i ^ mask) for i in range(count)])  51.3 us
    pallas_call x11, Pallas kernels, single(): return made(meta, *[array for array, _ in ins])  44.9 us
    ppermute x29, starting transfers between devices, xor_permute(): return lax.ppermute(value, 'dp', [(i, i ^ mask) for i in range(count)])  41.3 us
    pallas_call x1, Pallas kernels, on_device(): call(turn, [shape_of((2, C1), F32)] * 2 + some((PIX1, C1), BF16) + [shape...  14.3 us
    ppermute x9, starting transfers between devices, to_core(): arrived.append(lax.ppermute(both, ('pipe', 'dp'), pairs))  14 us
    ppermute x10, starting transfers between devices, swap_cores(): return lax.ppermute(value, 'pipe', [(0, 1), (1, 0)])  12.1 us
  transfers between devices with their start and end apart: 100, of which 39 were waited for; matrix products, arithmetic and copies ran while one was open for 2% of the time, Pallas kernels for 24%

profile of v1, /device:TPU:0, one launch (start us, length us, event | category | flops | bytes accessed | tf_op | source)
XLA Modules:
  0.0 401.5 jit_solution(3323452268787168379)
XLA Ops:
  9.6 5.4 %shard_map.86 = (bf16[272,256]{1,0:T(8,128)(2,1)S(1)}, bf16[272,256]{1,0:T(8,128)(2,1)S(1)}, bf16[272,256]{1,0:T(8,128)(2,1)S(1)}, bf16[272,256]{1,0:T(8,128)(2,...) custom-call(s32[15]{0:T(128)S(1)} %concatenate.57.meta, ...), custom_call_target="tpu_custom_call" | custom-call | bytes 18000000 | tf_op jit(solution)/shard_map/pallas_call | solution.py:1115
  20.7 4.6 %shard_map.87.refs_7_.refs_8_.refs_12_.refs_14_.refs_11_ = bf16[10240,256]{1,0:T(8,128)(2,1)} custom-call(s32[15]{0:T(128)S(1)} %concatenate.57.meta, bf16[1,6029312]{1,0:T(2,128)(2,1)} %raw_ref.3), custom_call_target="tpu_custom_call" | custom-call | bytes 28800000 | tf_op jit(solution)/shard_map/pallas_call | solution.py:847
  25.4 3.8 collective-permute-start.5
  29.3 5.7 %collective-permute-done.1 = f32[2,5120]{1,0:T(2,128)S(1)} collective-permute-done((f32[2,5120]{1,0:T(2,128)S(1)}, f32[2,5120]{1,0:T(2,128)S(1)}, u32[]{:S(2)}, u32[]{:S(2)}) %collective-permute-start.1) | collective-permute-done | bytes 40992 | tf_op jit(solution)/shard_map/ppermute | solution.py:1031
  52.7 4.5 %shard_map.90 = (f32[2,384]{1,0:T(2,128)S(1)}, bf16[4,256,256]{2,1,0:T(8,128)(2,1)}, f32[4,256,256]{2,1,0:T(8,128)S(1)}, f32[4,256,256]{2,1,0:T(8,128)}, f32[2,256]{1,0:T(2,128)S(1)}) custom-call(s32[15]{0:T(128)S(1)} %concatenate.57.meta, f32[2,384]{1,0:T(2,128)S(1)} %get-tuple-element.137.refs_0_, f32[2,384]{1,0:T(2,128)S(1)} %collective-permute-done.7.refs_1_, ...), custom_call_target="tpu_custom_call" | custom-call | bytes 18000000 | tf_op jit(solution)/shard_map/pallas_call | solution.py:198
  72.9 7.4 %shard_map.92 = (f32[2,1024]{1,0:T(2,128)S(1)}, bf16[256,1024]{1,0:T(8,128)(2,1)}, f32[256,1024]{1,0:T(8,128)}, f32[256,1024]{1,0:T(8,128)}, f32[256,512]{1,0:T(...) custom-call(s32[15]{0:T(128)S(1)} %concatenate.57.meta, ...), custom_call_target="tpu_custom_call" | custom-call | bytes 18000000 | tf_op jit(solution)/shard_map/pallas_call | solution.py:1185
  80.3 7.6 %collective-permute-start.19 = (bf16[256,1024]{1,0:T(8,128)(2,1)}, bf16[256,1024]{1,0:T(8,128)(2,1)S(1)}, u32[]{:S(2)}, u32[]{:S(2)}) collective-permute-start(bf16[256,1024]{1,0:T(8,128)(2,1)} %get-tuple-element.151.sa_ref), channel_id=1, source_target_pairs={{0,16},{16,0},{1,17},{17,1},{2,18},{18,2},{3,19},{19,3},{4,20},{20... | collective-permute-start | bytes 1572872 | tf_op jit(solution)/shard_map/ppermute | solution.py:1031
  93.4 4.5 %shard_map.93 = (f32[2,512]{1,0:T(2,128)S(1)}, bf16[256,512]{1,0:T(8,128)(2,1)}, f32[256,512]{1,0:T(8,128)S(1)}, f32[256,512]{1,0:T(8,128)}, f32[2,512]{1,0:T(2,128)S(1)}) custom-call(s32[15]{0:T(128)S(1)} %concatenate.57.meta, f32[2,512]{1,0:T(2,128)S(1)} %get-tuple-element.152.refs_0_, f32[2,512]{1,0:T(2,128)S(1)} %collective-permute-done.20.refs_1_, ...), custom_call_target="tpu_custom_call" | custom-call | bytes 18000000 | tf_op jit(solution)/shard_map/pallas_call | solution.py:198
  115.5 7.4 %collective-permute-done.31.refs_15_ = bf16[64,2048]{1,0:T(8,128)(2,1)S(1)} collective-permute-done((bf16[64,2048]{1,0:T(8,128)(2,1)S(1)}, bf16[64,2048]{1,0:T(8,128)(2,1)S(1)}, u32[]{:S(2)}, u32[]{:S(2)}) %collective-permute-start.31) | collective-permute-done | bytes 262176 | tf_op jit(solution)/shard_map/ppermute | solution.py:1036
  126.7 14.3 %shard_map.95 = (f32[2,2048]{1,0:T(2,128)S(1)}, f32[2,2048]{1,0:T(2,128)S(1)}, bf16[64,2048]{1,0:T(8,128)(2,1)S(1)}, bf16[64,2048]{1,0:T(8,128)(2,1)S(1)}, bf16[...) custom-call(s32[15]{0:T(128)S(1)} %concatenate.57.meta, ...), custom_call_target="tpu_custom_call" | custom-call | bytes 18000000 | tf_op jit(solution)/shard_map/pallas_call | solution.py:1246
  148.0 5.8 %shard_map.96 = (f32[3,2048]{1,0:T(4,128)S(1)}, bf16[2,256,2048]{2,1,0:T(8,128)(2,1)S(1)}, bf16[256,2048]{1,0:T(8,128)(2,1)S(1)}, f32[256,512]{1,0:T(8,128)S(1)}, f32[2,512]{1,0:T(2,128)S(1)}) custom-call(s32[15]{0:T(128)S(1)} %concatenate.57.meta, f32[3,2048]{1,0:T(4,128)S(1)} %get-tuple-element.168.refs_0_, f32[3,2048]{1,0:T(4,128)S(1)} %collective-permute-done.37.refs_1_, ...), custom_call_target="tpu_custom_call" | custom-call | bytes 18000000 | tf_op jit(solution)/shard_map/pallas_call | solution.py:198
  159.6 5.3 %shard_map.97 = (f32[2,512]{1,0:T(2,128)S(1)}, bf16[2,256,256]{2,1,0:T(8,128)(2,1)S(1)}, f32[256,512]{1,0:T(8,128)S(1)}, f32[2,512]{1,0:T(2,128)S(1)}) custom-call(s32[15]{0:T(128)S(1)} %concatenate.57.meta, f32[2,512]{1,0:T(2,128)S(1)} %get-tuple-element.176.refs_0_, f32[2,512]{1,0:T(2,128)S(1)} %collective-permute-done.41.refs_1_, ...), custom_call_target="tpu_custom_call" | custom-call | bytes 18000000 | tf_op jit(solution)/shard_map/pallas_call | solution.py:198
  173.7 6.7 %shard_map.99 = (f32[2,512]{1,0:T(2,128)S(1)}, bf16[2,256,256]{2,1,0:T(8,128)(2,1)S(1)}, f32[256,1024]{1,0:T(8,128)S(1)}, f32[2,1024]{1,0:T(2,128)S(1)}) custom-call(s32[15]{0:T(128)S(1)} %concatenate.57.meta, f32[2,512]{1,0:T(2,128)S(1)} %get-tuple-element.183.refs_0_, f32[2,512]{1,0:T(2,128)S(1)} %collective-permute-done.45.refs_1_, ...), custom_call_target="tpu_custom_call" | custom-call | bytes 18000000 | tf_op jit(solution)/shard_map/pallas_call | solution.py:198
  187.2 7.3 %shard_map.100 = (f32[2,1024]{1,0:T(2,128)S(1)}, bf16[4,256,1024]{2,1,0:T(8,128)(2,1)}, f32[4,256,256]{2,1,0:T(8,128)S(1)}, f32[2,256]{1,0:T(2,128)S(1)}) custom-call(s32[15]{0:T(128)S(1)} %concatenate.57.meta, f32[2,1024]{1,0:T(2,128)S(1)} %get-tuple-element.192.refs_0_, f32[2,1024]{1,0:T(2,128)S(1)} %collective-permute-done.50.refs_1_, ...), custom_call_target="tpu_custom_call" | custom-call | bytes 18000000 | tf_op jit(solution)/shard_map/pallas_call | solution.py:1314
  201.9 6.8 %shard_map.102 = (f32[2,256]{1,0:T(2,128)S(1)}, bf16[4,256,256]{2,1,0:T(8,128)(2,1)}, f32[4,256,256]{2,1,0:T(8,128)S(1)}, f32[2,256]{1,0:T(2,128)S(1)}) custom-call(s32[15]{0:T(128)S(1)} %concatenate.57.meta, f32[2,256]{1,0:T(2,128)S(1)} %get-tuple-element.200.refs_0_, f32[2,256]{1,0:T(2,128)S(1)} %collective-permute-done.54.refs_1_, ...), custom_call_target="tpu_custom_call" | custom-call | bytes 18000000 | tf_op jit(solution)/shard_map/pallas_call | solution.py:1344
  222.8 7.4 %shard_map.103.refs_4_ = bf16[8704,128]{1,0:T(8,128)(2,1)} custom-call(s32[15]{0:T(128)S(1)} %concatenate.57.meta, bf16[4,256,256]{2,1,0:T(8,128)(2,1)} %get-tuple-element.204.a1_ref, bf16[4,256,256]{2,1,0:T(8,128)(2,1)} %get-tuple-element.205.d2_ref, bf16[4,256,256]{2,1,0:T(8,128)(2,1)} %get-tuple-element.194.refs_7_.a2_ref, ...), custom_call_target="tpu_custom_call" | custom-call | bytes 18000000 | tf_op jit(solution)/shard_map/pallas_call | solution.py:1361
  233.0 5.8 %collective-permute-done.61 = bf16[6144,128]{1,0:T(8,128)(2,1)S(1)} collective-permute-done((bf16[6144,128]{1,0:T(8,128)(2,1)}, bf16[6144,128]{1,0:T(8,128)(2,1)S(1)}, u32[]{:S(2)}, u32[]{:S(2)}) %collective-permute-start.61) | collective-permute-done | bytes 1572896 | tf_op jit(solution)/shard_map/ppermute | solution.py:1049
  247.2 12.7 %collective-permute-done.62 = bf16[3072,128]{1,0:T(8,128)(2,1)S(1)} collective-permute-done((bf16[3072,128]{1,0:T(8,128)(2,1)S(1)}, bf16[3072,128]{1,0:T(8,128)(2,1)S(1)}, u32[]{:S(2)}, u32[]{:S(2)}) %collective-permute-start.62) | collective-permute-done | bytes 786464 | tf_op jit(solution)/shard_map/ppermute | solution.py:1049
  260.2 6.5 %shard_map.105 = (bf16[4,256,1024]{2,1,0:T(8,128)(2,1)S(1)}, bf16[8704,128]{1,0:T(8,128)(2,1)}) custom-call(s32[15]{0:T(128)S(1)} %concatenate.57.meta, bf16[8,16,16,1024]{3,2,1,0:T(8,128)(2,1)} %x_ref.3, bf16[1024,256]{1,0:T(8,128)(2,1)} %shard_map.85.wa_ref, bf16[1024,256]{1,0:T(8,128)(2,1)} %copy-done.6, ...), custom_call_target="tpu_custom_call", output_to_operand_aliasing={{1}: (8, {})} | custom-call | bytes 18000000 | tf_op jit(solution)/shard_map/pallas_call | solution.py:1409
  270.3 4.8 %collective-permute-done.66 = bf16[1536,128]{1,0:T(8,128)(2,1)S(1)} collective-permute-done((bf16[1536,128]{1,0:T(8,128)(2,1)S(1)}, bf16[1536,128]{1,0:T(8,128)(2,1)S(1)}, u32[]{:S(2)}, u32[]{:S(2)}) %collective-permute-start.66) | collective-permute-done | bytes 393248 | tf_op jit(solution)/shard_map/ppermute | solution.py:1036
  275.3 4.9 %collective-permute-start.69 = (bf16[768,128]{1,0:T(8,128)(2,1)S(1)}, bf16[768,128]{1,0:T(8,128)(2,1)S(1)}, u32[]{:S(2)}, u32[]{:S(2)}) collective-permute-start(bf16[768,128]{1,0:T(8,128)(2,1)S(1)} %get-tuple-element.272), channel_id=1, source_target_pairs={{0,8},{1,9},{2,10},{3,11},{4,12},{5,13},{6,14},{7,15},{8,0},{9,1},... | collective-permute-start | bytes 589832 | tf_op jit(solution)/shard_map/ppermute | solution.py:1036
  282.6 5.1 %collective-permute-done.69 = bf16[768,128]{1,0:T(8,128)(2,1)S(1)} collective-permute-done((bf16[768,128]{1,0:T(8,128)(2,1)S(1)}, bf16[768,128]{1,0:T(8,128)(2,1)S(1)}, u32[]{:S(2)}, u32[]{:S(2)}) %collective-permute-start.69) | collective-permute-done | bytes 196640 | tf_op jit(solution)/shard_map/ppermute | solution.py:1036
  289.6 7.9 %collective-permute-done.70 = bf16[2816,128]{1,0:T(8,128)(2,1)S(1)} collective-permute-done((bf16[2816,128]{1,0:T(8,128)(2,1)S(1)}, bf16[2816,128]{1,0:T(8,128)(2,1)S(1)}, u32[]{:S(2)}, u32[]{:S(2)}) %collective-permute-start.70) | collective-permute-done | bytes 720928 | tf_op jit(solution)/shard_map/ppermute | solution.py:1049
  301.5 10.7 %collective-permute-done.73 = bf16[1408,128]{1,0:T(8,128)(2,1)S(1)} collective-permute-done((bf16[1408,128]{1,0:T(8,128)(2,1)S(1)}, bf16[1408,128]{1,0:T(8,128)(2,1)S(1)}, u32[]{:S(2)}, u32[]{:S(2)}) %collective-permute-start.73) | collective-permute-done | bytes 360480 | tf_op jit(solution)/shard_map/ppermute | solution.py:1036
  324.9 7.2 %collective-permute-done.79 = bf16[704,128]{1,0:T(8,128)(2,1)S(1)} collective-permute-done((bf16[704,128]{1,0:T(8,128)(2,1)S(1)}, bf16[704,128]{1,0:T(8,128)(2,1)S(1)}, u32[]{:S(2)}, u32[]{:S(2)}) %collective-permute-start.79) | collective-permute-done | bytes 180256 | tf_op jit(solution)/shard_map/ppermute | solution.py:1036
  337.4 4.9 %collective-permute-done.81 = bf16[1408,128]{1,0:T(8,128)(2,1)S(1)} collective-permute-done((bf16[1408,128]{1,0:T(8,128)(2,1)S(1)}, bf16[1408,128]{1,0:T(8,128)(2,1)S(1)}, u32[]{:S(2)}, u32[]{:S(2)}) %collective-permute-start.81) | collective-permute-done | bytes 360480 | tf_op jit(solution)/shard_map/ppermute | solution.py:1036
  347.3 8.9 %shard_map.106 = bf16[8,262144]{1,0:T(8,128)(2,1)} custom-call(s32[15]{0:T(128)S(1)} %concatenate.57.meta, bf16[4,256,1024]{2,1,0:T(8,128)(2,1)S(1)} %get-tuple-element.243.x_ref, bf16[4,256,1024]{2,1,0:T(8,128)(2,1)S(1)} %collective-permute-done.83.xg_ref, bf16[4,64,2048]{2,1,0:T(8,128)(2,1)S(1)} %pad_maximum_fusion.2.y_ref, ...), custom_call_target="tpu_custom_call" | custom-call | bytes 32400000 | tf_op jit(solution)/shard_map/pallas_call | solution.py:1458
  356.2 5.2 %collective-permute-done.85 = bf16[2816,128]{1,0:T(8,128)(2,1)S(1)} collective-permute-done((bf16[2816,128]{1,0:T(8,128)(2,1)S(1)}, bf16[2816,128]{1,0:T(8,128)(2,1)S(1)}, u32[]{:S(2)}, u32[]{:S(2)}) %collective-permute-start.85) | collective-permute-done | bytes 720928 | tf_op jit(solution)/shard_map/ppermute | solution.py:1049
  361.5 5.0 %collective-permute-done.86 = bf16[544,128]{1,0:T(8,128)(2,1)S(1)} collective-permute-done((bf16[544,128]{1,0:T(8,128)(2,1)S(1)}, bf16[544,128]{1,0:T(8,128)(2,1)S(1)}, u32[]{:S(2)}, u32[]{:S(2)}) %collective-permute-start.86) | collective-permute-done | bytes 139296 | tf_op jit(solution)/shard_map/ppermute | solution.py:1036
  374.6 8.0 %shard_map.107.refs_0_ = f32[47104,128]{1,0:T(8,128)} custom-call(s32[15]{0:T(128)S(1)} %concatenate.57.meta, bf16[6144,128]{1,0:T(8,128)(2,1)S(1)} %pad_maximum_fusion.refs_0_, bf16[6144,128]{1,0:T(8,128)(2,1)S(1)} %collective-permute-done.87.refs_1_, bf16[6144,128]{1,0:T(8,128)(2,1)S(1)} %collective-permute-done.88.refs_2_, ...), custom_call_target="tpu_custom_call" | custom-call | bytes 28800000 | tf_op jit(solution)/shard_map/pallas_call | solution.py:1478
  389.6 4.5 %shard_map.108.refs_0_ = f32[47104,128]{1,0:T(8,128)} custom-call(s32[15]{0:T(128)S(1)} %concatenate.57.meta, f32[47104,128]{1,0:T(8,128)} %shard_map.107.refs_0_, bf16[5632,128]{1,0:T(8,128)(2,1)S(1)} %pad_maximum_fusion.1.refs_1_, bf16[5632,128]{1,0:T(8,128)(2,1)S(1)} %collective-permute-done.91.refs_2_, ...), custom_call_target="tpu_custom_call", output_to_operand_aliasing={{}: (1, {})} | custom-call | bytes 18000000 | tf_op jit(solution)/shard_map/pallas_call | solution.py:1482
  396.7 4.4 %shard_map.109 = f32[47104,128]{1,0:T(8,128)} custom-call(s32[15]{0:T(128)S(1)} %concatenate.57.meta, f32[47104,128]{1,0:T(8,128)} %shard_map.108.refs_0_, bf16[5632,128]{1,0:T(8,128)(2,1)S(1)} %pad_maximum_fusion.1.refs_1_, bf16[5632,128]{1,0:T(8,128)(2,1)S(1)} %collective-permute-done.91.refs_2_, ...), custom_call_target="tpu_custom_call", output_to_operand_aliasing={{}: (1, {})} | custom-call | bytes 18000000 | tf_op jit(solution)/shard_map/pallas_call | solution.py:1486
  (282 shorter events, 188.3 us)
Async XLA Ops:
  15.0 20.0 %collective-permute-start.2 = (bf16[272,256]{1,0:T(8,128)(2,1)S(1)}, bf16[272,256]{1,0:T(8,128)(2,1)S(1)}, u32[]{:S(2)}, u32[]{:S(2)}) collective-permute-start(bf16[272,256]{1,0:T(8,128)(2,1)S(1)} %get-tuple-element.131), channel_id=1, source_target_pairs={{0,4},{1,5},{2,6},{3,7},{4,0},{5,1},{6,2},{7,3},{8,12},{9,13},{10,... | collective-permute-start | bytes 417800 | tf_op jit(solution)/shard_map/ppermute | solution.py:1036
  18.1 16.9 %collective-permute-start.3 = (bf16[272,256]{1,0:T(8,128)(2,1)S(1)}, bf16[272,256]{1,0:T(8,128)(2,1)S(1)}, u32[]{:S(2)}, u32[]{:S(2)}) collective-permute-start(bf16[272,256]{1,0:T(8,128)(2,1)S(1)} %get-tuple-element.132), channel_id=1, source_target_pairs={{0,8},{1,9},{2,10},{3,11},{4,12},{5,13},{6,14},{7,15},{8,0},{9,1},... | collective-permute-start | bytes 417800 | tf_op jit(solution)/shard_map/ppermute | solution.py:1036
  20.7 14.3 %collective-permute-start.4 = (bf16[272,256]{1,0:T(8,128)(2,1)S(1)}, bf16[272,256]{1,0:T(8,128)(2,1)S(1)}, u32[]{:S(2)}, u32[]{:S(2)}) collective-permute-start(bf16[272,256]{1,0:T(8,128)(2,1)S(1)} %get-tuple-element.133), channel_id=1, source_target_pairs={{0,12},{1,13},{2,14},{3,15},{4,8},{5,9},{6,10},{7,11},{8,4},{9,5},... | collective-permute-start | bytes 417800 | tf_op jit(solution)/shard_map/ppermute | solution.py:1036
  25.4 23.7 %collective-permute-start.5 = (bf16[10240,256]{1,0:T(8,128)(2,1)}, bf16[10240,256]{1,0:T(8,128)(2,1)}, u32[]{:S(2)}, u32[]{:S(2)}) collective-permute-start(bf16[10240,256]{1,0:T(8,128)(2,1)} %shard_map.87.refs_7_.refs_8_.refs_12_.refs_14_.refs_11_), channel_id=1, source_target_pairs={{0,16},{16,0},{1,17},{17,1},{2,18},{18,2},{3,19},{19,3},{4,20},{20... | collective-permute-start | bytes 15728648 | tf_op jit(solution)/shard_map/ppermute | solution.py:1031
  37.7 53.7 %collective-permute-start.18 = (bf16[13312,256]{1,0:T(8,128)(2,1)}, bf16[13312,256]{1,0:T(8,128)(2,1)}, u32[]{:S(2)}, u32[]{:S(2)}) collective-permute-start(bf16[13312,256]{1,0:T(8,128)(2,1)} %shard_map.89.refs_8_.refs_14_.refs_12_), channel_id=1, source_target_pairs={{16,0},{17,1},{18,2},{19,3},{20,4},{21,5},{22,6},{23,7},{24,8},{25... | collective-permute-start | bytes 20447240 | tf_op jit(solution)/shard_map/ppermute | solution.py:1166
  42.1 18.1 %collective-permute-start.10 = (bf16[64,1024]{1,0:T(8,128)(2,1)S(1)}, bf16[64,1024]{1,0:T(8,128)(2,1)S(1)}, u32[]{:S(2)}, u32[]{:S(2)}) collective-permute-start(bf16[64,1024]{1,0:T(8,128)(2,1)S(1)} %get-tuple-element.141), channel_id=1, source_target_pairs={{0,8},{1,9},{2,10},{3,11},{4,12},{5,13},{6,14},{7,15},{8,0},{9,1},... | collective-permute-start | bytes 393224 | tf_op jit(solution)/shard_map/ppermute | solution.py:1036
  45.6 25.1 %collective-permute-start.14 = (bf16[64,1024]{1,0:T(8,128)(2,1)S(1)}, bf16[64,1024]{1,0:T(8,128)(2,1)S(1)}, u32[]{:S(2)}, u32[]{:S(2)}) collective-permute-start(bf16[64,1024]{1,0:T(8,128)(2,1)S(1)} %get-tuple-element.146), channel_id=1, source_target_pairs={{0,12},{1,13},{2,14},{3,15},{4,8},{5,9},{6,10},{7,11},{8,4},{9,5},... | collective-permute-start | bytes 393224 | tf_op jit(solution)/shard_map/ppermute | solution.py:1036
  101.6 21.4 %collective-permute-start.31 = (bf16[64,2048]{1,0:T(8,128)(2,1)S(1)}, bf16[64,2048]{1,0:T(8,128)(2,1)S(1)}, u32[]{:S(2)}, u32[]{:S(2)}) collective-permute-start(bf16[64,2048]{1,0:T(8,128)(2,1)S(1)} %get-tuple-element.161), channel_id=1, source_target_pairs={{0,8},{1,9},{2,10},{3,11},{4,12},{5,13},{6,14},{7,15},{8,0},{9,1},... | collective-permute-start | bytes 786440 | tf_op jit(solution)/shard_map/ppermute | solution.py:1036
  106.9 17.6 %collective-permute-start.32 = (bf16[64,2048]{1,0:T(8,128)(2,1)S(1)}, bf16[64,2048]{1,0:T(8,128)(2,1)S(1)}, u32[]{:S(2)}, u32[]{:S(2)}) collective-permute-start(bf16[64,2048]{1,0:T(8,128)(2,1)S(1)} %get-tuple-element.162), channel_id=1, source_target_pairs={{0,12},{1,13},{2,14},{3,15},{4,8},{5,9},{6,10},{7,11},{8,4},{9,5},... | collective-permute-start | bytes 786440 | tf_op jit(solution)/shard_map/ppermute | solution.py:1036
  157.6 26.0 %collective-permute-start.49 = (bf16[64,2048]{1,0:T(8,128)(2,1)S(1)}, bf16[64,2048]{1,0:T(8,128)(2,1)S(1)}, u32[]{:S(2)}, u32[]{:S(2)}) collective-permute-start(bf16[64,2048]{1,0:T(8,128)(2,1)S(1)} %get-tuple-element.191), channel_id=1, source_target_pairs={{0,4},{1,5},{2,6},{3,7},{4,0},{5,1},{6,2},{7,3},{8,12},{9,13},{10,... | collective-permute-start | bytes 786440 | tf_op jit(solution)/shard_map/ppermute | solution.py:1036
  165.1 36.7 %collective-permute-start.53 = (bf16[64,2048]{1,0:T(8,128)(2,1)S(1)}, bf16[64,2048]{1,0:T(8,128)(2,1)S(1)}, u32[]{:S(2)}, u32[]{:S(2)}) collective-permute-start(bf16[64,2048]{1,0:T(8,128)(2,1)S(1)} %get-tuple-element.199), channel_id=1, source_target_pairs={{0,8},{1,9},{2,10},{3,11},{4,12},{5,13},{6,14},{7,15},{8,0},{9,1},... | collective-permute-start | bytes 786440 | tf_op jit(solution)/shard_map/ppermute | solution.py:1036
  217.1 21.7 %collective-permute-start.61 = (bf16[6144,128]{1,0:T(8,128)(2,1)}, bf16[6144,128]{1,0:T(8,128)(2,1)S(1)}, u32[]{:S(2)}, u32[]{:S(2)}) collective-permute-start(bf16[6144,128]{1,0:T(8,128)(2,1)} %get-tuple-element.254), channel_id=1, source_target_pairs={{0,1},{1,0},{2,3},{3,2},{4,5},{5,4},{6,7},{7,6},{8,9},{9,8},{10,11... | collective-permute-start | bytes 4718600 | tf_op jit(solution)/shard_map/ppermute | solution.py:1049
  239.4 20.5 %collective-permute-start.62 = (bf16[3072,128]{1,0:T(8,128)(2,1)S(1)}, bf16[3072,128]{1,0:T(8,128)(2,1)S(1)}, u32[]{:S(2)}, u32[]{:S(2)}) collective-permute-start(bf16[3072,128]{1,0:T(8,128)(2,1)S(1)} %get-tuple-element.260), channel_id=1, source_target_pairs={{0,2},{1,3},{2,0},{3,1},{4,6},{5,7},{6,4},{7,5},{8,10},{9,11},{10,... | collective-permute-start | bytes 2359304 | tf_op jit(solution)/shard_map/ppermute | solution.py:1049
  240.9 19.2 %collective-permute-start.63 = (bf16[512,256]{1,0:T(8,128)(2,1)S(1)}, bf16[512,256]{1,0:T(8,128)(2,1)S(1)}, u32[]{:S(2)}, u32[]{:S(2)}) collective-permute-start(bf16[512,256]{1,0:T(8,128)(2,1)S(1)} %get-tuple-element.220), channel_id=1, source_target_pairs={{0,4},{1,5},{2,6},{3,7},{4,0},{5,1},{6,2},{7,3},{8,12},{9,13},{10,... | collective-permute-start | bytes 786440 | tf_op jit(solution)/shard_map/ppermute | solution.py:1036
  241.3 18.8 %collective-permute-start.64 = (bf16[512,256]{1,0:T(8,128)(2,1)S(1)}, bf16[512,256]{1,0:T(8,128)(2,1)S(1)}, u32[]{:S(2)}, u32[]{:S(2)}) collective-permute-start(bf16[512,256]{1,0:T(8,128)(2,1)S(1)} %get-tuple-element.221), channel_id=1, source_target_pairs={{0,8},{1,9},{2,10},{3,11},{4,12},{5,13},{6,14},{7,15},{8,0},{9,1},... | collective-permute-start | bytes 786440 | tf_op jit(solution)/shard_map/ppermute | solution.py:1036
  243.6 16.6 %collective-permute-start.65 = (bf16[512,256]{1,0:T(8,128)(2,1)S(1)}, bf16[512,256]{1,0:T(8,128)(2,1)S(1)}, u32[]{:S(2)}, u32[]{:S(2)}) collective-permute-start(bf16[512,256]{1,0:T(8,128)(2,1)S(1)} %get-tuple-element.222), channel_id=1, source_target_pairs={{0,12},{1,13},{2,14},{3,15},{4,8},{5,9},{6,10},{7,11},{8,4},{9,5},... | collective-permute-start | bytes 786440 | tf_op jit(solution)/shard_map/ppermute | solution.py:1036
  245.5 34.7 %collective-permute-start.67 = (bf16[5632,128]{1,0:T(8,128)(2,1)S(1)}, bf16[5632,128]{1,0:T(8,128)(2,1)S(1)}, u32[]{:S(2)}, u32[]{:S(2)}) collective-permute-start(bf16[5632,128]{1,0:T(8,128)(2,1)S(1)} %get-tuple-element.227), channel_id=1, source_target_pairs={{0,1},{1,0},{2,3},{3,2},{4,5},{5,4},{6,7},{7,6},{8,9},{9,8},{10,11... | collective-permute-start | bytes 4325384 | tf_op jit(solution)/shard_map/ppermute | solution.py:1049
  280.7 16.8 %collective-permute-start.70 = (bf16[2816,128]{1,0:T(8,128)(2,1)S(1)}, bf16[2816,128]{1,0:T(8,128)(2,1)S(1)}, u32[]{:S(2)}, u32[]{:S(2)}) collective-permute-start(bf16[2816,128]{1,0:T(8,128)(2,1)S(1)} %get-tuple-element.262), channel_id=1, source_target_pairs={{0,2},{1,3},{2,0},{3,1},{4,6},{5,7},{6,4},{7,5},{8,10},{9,11},{10,... | collective-permute-start | bytes 2162696 | tf_op jit(solution)/shard_map/ppermute | solution.py:1049
  297.8 14.8 %collective-permute-start.75 = (bf16[1536,128]{1,0:T(8,128)(2,1)S(1)}, bf16[1536,128]{1,0:T(8,128)(2,1)S(1)}, u32[]{:S(2)}, u32[]{:S(2)}) collective-permute-start(bf16[1536,128]{1,0:T(8,128)(2,1)S(1)} %pad_maximum_fusion.6), channel_id=1, source_target_pairs={{0,4},{1,5},{2,6},{3,7},{4,0},{5,1},{6,2},{7,3},{8,12},{9,13},{10,... | collective-permute-start | bytes 1179656 | tf_op jit(solution)/shard_map/ppermute | solution.py:1036
  297.9 14.4 %collective-permute-start.73 = (bf16[1408,128]{1,0:T(8,128)(2,1)S(1)}, bf16[1408,128]{1,0:T(8,128)(2,1)S(1)}, u32[]{:S(2)}, u32[]{:S(2)}) collective-permute-start(bf16[1408,128]{1,0:T(8,128)(2,1)S(1)} %get-tuple-element.268), channel_id=1, source_target_pairs={{0,4},{1,5},{2,6},{3,7},{4,0},{5,1},{6,2},{7,3},{8,12},{9,13},{10,... | collective-permute-start | bytes 1081352 | tf_op jit(solution)/shard_map/ppermute | solution.py:1036
  314.5 31.5 %collective-permute-start.83 = (bf16[4,256,1024]{2,1,0:T(8,128)(2,1)S(1)}, bf16[4,256,1024]{2,1,0:T(8,128)(2,1)S(1)}, u32[]{:S(2)}, u32[]{:S(2)}) collective-permute-start(bf16[4,256,1024]{2,1,0:T(8,128)(2,1)S(1)} %get-tuple-element.243.x_ref), channel_id=1, source_target_pairs={{16,0},{17,1},{18,2},{19,3},{20,4},{21,5},{22,6},{23,7},{24,8},{25... | collective-permute-start | bytes 6291464 | tf_op jit(solution)/shard_map/ppermute | solution.py:1422
  342.4 19.0 %collective-permute-start.85 = (bf16[2816,128]{1,0:T(8,128)(2,1)S(1)}, bf16[2816,128]{1,0:T(8,128)(2,1)S(1)}, u32[]{:S(2)}, u32[]{:S(2)}) collective-permute-start(bf16[2816,128]{1,0:T(8,128)(2,1)S(1)} %pad_maximum_fusion.4), channel_id=1, source_target_pairs={{0,2},{1,3},{2,0},{3,1},{4,6},{5,7},{6,4},{7,5},{8,10},{9,11},{10,... | collective-permute-start | bytes 2162696 | tf_op jit(solution)/shard_map/ppermute | solution.py:1049
  343.6 23.6 %collective-permute-start.98 = (f32[2,5120]{1,0:T(2,128)S(1)}, f32[2,5120]{1,0:T(2,128)S(1)}, u32[]{:S(2)}, u32[]{:S(2)}) collective-permute-start(f32[2,5120]{1,0:T(2,128)S(1)} %select_add_fusion), channel_id=1, source_target_pairs={{0,4},{1,5},{2,6},{3,7},{4,0},{5,1},{6,2},{7,3},{8,12},{9,13},{10,... | collective-permute-start | bytes 122888 | tf_op jit(solution)/shard_map/ppermute | solution.py:1036
  343.7 24.9 %collective-permute-start.89 = (bf16[6144,128]{1,0:T(8,128)(2,1)S(1)}, bf16[6144,128]{1,0:T(8,128)(2,1)S(1)}, u32[]{:S(2)}, u32[]{:S(2)}) collective-permute-start(bf16[6144,128]{1,0:T(8,128)(2,1)S(1)} %pad_maximum_fusion.refs_0_), channel_id=1, source_target_pairs={{16,18},{17,19},{18,16},{19,17},{20,22},{21,23},{22,20},{23,21},{2... | collective-permute-start | bytes 4718600 | tf_op jit(solution)/shard_map/ppermute | solution.py:1087
  344.5 25.5 %collective-permute-start.88 = (bf16[6144,128]{1,0:T(8,128)(2,1)S(1)}, bf16[6144,128]{1,0:T(8,128)(2,1)S(1)}, u32[]{:S(2)}, u32[]{:S(2)}) collective-permute-start(bf16[6144,128]{1,0:T(8,128)(2,1)S(1)} %pad_maximum_fusion.refs_0_), channel_id=1, source_target_pairs={{0,17},{1,16},{2,19},{3,18},{4,21},{5,20},{6,23},{7,22},{8,25},{9,... | collective-permute-start | bytes 4718600 | tf_op jit(solution)/shard_map/ppermute | solution.py:1087
  345.9 27.3 %collective-permute-start.87 = (bf16[6144,128]{1,0:T(8,128)(2,1)S(1)}, bf16[6144,128]{1,0:T(8,128)(2,1)S(1)}, u32[]{:S(2)}, u32[]{:S(2)}) collective-permute-start(bf16[6144,128]{1,0:T(8,128)(2,1)S(1)} %pad_maximum_fusion.refs_0_), channel_id=1, source_target_pairs={{0,16},{1,17},{2,18},{3,19},{4,20},{5,21},{6,22},{7,23},{8,24},{9,... | collective-permute-start | bytes 4718600 | tf_op jit(solution)/shard_map/ppermute | solution.py:1087
  366.5 20.0 %collective-permute-start.93 = (bf16[5632,128]{1,0:T(8,128)(2,1)S(1)}, bf16[5632,128]{1,0:T(8,128)(2,1)S(1)}, u32[]{:S(2)}, u32[]{:S(2)}) collective-permute-start(bf16[5632,128]{1,0:T(8,128)(2,1)S(1)} %pad_maximum_fusion.1.refs_1_), channel_id=1, source_target_pairs={{16,18},{17,19},{18,16},{19,17},{20,22},{21,23},{22,20},{23,21},{2... | collective-permute-start | bytes 4325384 | tf_op jit(solution)/shard_map/ppermute | solution.py:1087
  367.2 15.3 %collective-permute-start.90 = (bf16[1088,128]{1,0:T(8,128)(2,1)S(1)}, bf16[1088,128]{1,0:T(8,128)(2,1)S(1)}, u32[]{:S(2)}, u32[]{:S(2)}) collective-permute-start(bf16[1088,128]{1,0:T(8,128)(2,1)S(1)} %pad_maximum_fusion.8), channel_id=1, source_target_pairs={{0,2},{1,3},{2,0},{3,1},{4,6},{5,7},{6,4},{7,5},{8,10},{9,11},{10,... | collective-permute-start | bytes 835592 | tf_op jit(solution)/shard_map/ppermute | solution.py:1049
  368.6 16.6 %collective-permute-start.99 = (f32[2,5120]{1,0:T(2,128)S(1)}, f32[2,5120]{1,0:T(2,128)S(1)}, u32[]{:S(2)}, u32[]{:S(2)}) collective-permute-start(f32[2,5120]{1,0:T(2,128)S(1)} %fusion.8), channel_id=1, source_target_pairs={{0,8},{1,9},{2,10},{3,11},{4,12},{5,13},{6,14},{7,15},{8,0},{9,1},... | collective-permute-start | bytes 122888 | tf_op jit(solution)/shard_map/ppermute | solution.py:1036
  370.0 19.6 %collective-permute-start.92 = (bf16[5632,128]{1,0:T(8,128)(2,1)S(1)}, bf16[5632,128]{1,0:T(8,128)(2,1)S(1)}, u32[]{:S(2)}, u32[]{:S(2)}) collective-permute-start(bf16[5632,128]{1,0:T(8,128)(2,1)S(1)} %pad_maximum_fusion.1.refs_1_), channel_id=1, source_target_pairs={{0,17},{1,16},{2,19},{3,18},{4,21},{5,20},{6,23},{7,22},{8,25},{9,... | collective-permute-start | bytes 4325384 | tf_op jit(solution)/shard_map/ppermute | solution.py:1087
  373.2 16.4 %collective-permute-start.91 = (bf16[5632,128]{1,0:T(8,128)(2,1)S(1)}, bf16[5632,128]{1,0:T(8,128)(2,1)S(1)}, u32[]{:S(2)}, u32[]{:S(2)}) collective-permute-start(bf16[5632,128]{1,0:T(8,128)(2,1)S(1)} %pad_maximum_fusion.1.refs_1_), channel_id=1, source_target_pairs={{0,16},{1,17},{2,18},{3,19},{4,20},{5,21},{6,22},{7,23},{8,24},{9,... | collective-permute-start | bytes 4325384 | tf_op jit(solution)/shard_map/ppermute | solution.py:1087
  382.6 14.1 %collective-permute-start.96 = (bf16[2176,128]{1,0:T(8,128)(2,1)S(1)}, bf16[2176,128]{1,0:T(8,128)(2,1)S(1)}, u32[]{:S(2)}, u32[]{:S(2)}) collective-permute-start(bf16[2176,128]{1,0:T(8,128)(2,1)S(1)} %pad_maximum_fusion.5.refs_5_), channel_id=1, source_target_pairs={{0,1},{1,0},{2,3},{3,2},{4,5},{5,4},{6,7},{7,6},{8,9},{9,8},{10,11... | collective-permute-start | bytes 1671176 | tf_op jit(solution)/shard_map/ppermute | solution.py:1087
  (83 other events, 579.6 us)

commit v2 on v1

--- a/solution.py
+++ b/solution.py
@@ -464,7 +464,8 @@
 
 def turn(meta, *refs):
     stats, sides, (tot_ref, z3_ref, zs_ref, hw_ref, n_ref) = refs[0:4], refs[4:8], refs[8:13]
-    cots, (tot6_ref, tots_ref), ys, (g_ref, st_ref) = refs[13:17], refs[17:19], refs[19:23], refs[23:]
+    cots, (tot6_ref, tots_ref), ys = refs[13:17], refs[17:19], refs[19:23]
+    g_ref, st_ref, cot_ref, y_ref = refs[23:]
     step = pl.program_id(0)
 
     @pl.when(step == 0)
@@ -481,15 +482,21 @@
     pre = normed * n_ref[0:1, AT3:ATS] + n_ref[1:2, AT3:ATS]
     pre = pre + (normed_s * n_ref[0:1, ATS : ATS + C1] + n_ref[1:2, ATS : ATS + C1])
     sig = sigmoid(pre)
-    value = pre * sig
-    change = sig * (1.0 + pre * (1.0 - sig))
     for k in range(WORK):
 
         @pl.when(step == k)
         def _(k=k):
-            mask = over_lanes(mask1(hw_ref, k), C1)
-            ys[k][...] = (value * mask).astype(BF16)
-            g_ref[0] = cots[k][...].astype(F32) * change * mask
+            cot_ref[...] = cots[k][...]
+
+    high, wide = hw_ref[pl.ds(step, 1), :] * 0.5, hw_ref[pl.ds(4 + step, 1), :] * 0.5
+    mask = over_lanes(pixel_mask(high, wide, WB // 2, PIX1), C1)
+    y_ref[...] = (pre * sig * mask).astype(BF16)
+    g_ref[0] = cot_ref[...].astype(F32) * (sig * (1.0 + pre * (1.0 - sig))) * mask
+    for k in range(WORK):
+
+        @pl.when(step == k)
+        def _(k=k):
+            ys[k][...] = y_ref[...]
 
     grad = g_ref[0]
     st_ref[0:1, :] += total_rows(grad)
@@ -842,7 +849,7 @@
             pl.when(meta[CORE] == core)(functools.partial(run, jobs[core]))
 
 
-def unpack(meta, packed, rows, jobs, micros, chunk=262144):
+def unpack(meta, packed, rows, jobs, micros, chunk=524288):
     widths = sorted({weight[3] for listed in jobs for _, weight in listed})
     return call(
         functools.partial(unpack_kernel, jobs, chunk),
@@ -1105,7 +1112,7 @@
     spot = jnp.stack([core, plane, level]).astype(jnp.int32)
     meta = jnp.concatenate([order, spot, sizes[:, 0], sizes[:, 1]]).astype(jnp.int32)
 
-    w1 = unpack(meta, params, C0, ([(0, W1)], []), 3, 65536)
+    w1 = unpack(meta, params, C0, ([(0, W1)], []), 3, 131072)
     w1 = (in_hbm(w1), in_hbm(lax.ppermute(w1, "pipe", [(0, 1)])))
     norms_there = swap_cores(norms[0])
     n0 = jnp.where(first_core, norms[0], norms_there)
@@ -1253,6 +1260,7 @@
         + [full(2, M0 + 128), per_image(PIX1, C1), per_image(PIX1, C1), full(8, 128), full(2, CN)]
         + [full(PIX1, C1)] * 4,
         [full(2, C1)] * 2 + [full(PIX1, C1)] * 4 + [per_image(PIX1, C1), full(3, C1)],
+        [vmem(PIX1, C1), vmem(PIX1, C1)],
     )(
         meta, *s6, *t5, tot1, y3.reshape(WORK, PIX1, C1), in_hbm(ys.reshape(WORK, PIX1, C1)), hw,
         n1, *cots,
@@ -1465,10 +1473,9 @@
         micros=9,
     )(meta, after(gx), x_there, y_back, y_there)
     step(boundary)
-    middle = joined(middle, middle_got)
+    middle = to_core(joined(middle, middle_got), 1)
     front = joined(front, front_got)
     front_got = plane_turn(front, 2)
-    middle = to_core(middle, 1)
 
     whole = shape_of((GRAD_ROWS, 128), F32)
     block_at = lambda at: pl.BlockSpec((PACK_ROWS, 128), lambda s, meta: (s + at, 0))

time: 409 us -> 401 us (0.980)
  starting transfers between devices: 136 us -> 127 us
  waiting for transfers between devices: 115 us -> 124 us
  Pallas kernels: 134 us -> 126 us
    pallas_call x1, Pallas kernels: 14.3 us -> 5.85 us  [on_device(): call(turn, [shape_of((2, C1), F32)] * 2 + some((PIX1, C1), BF16) + [shape...]
    ppermute x48, starting transfers between devices: 62.6 us -> 54.4 us  [plane_turn(): return lax.ppermute(value, ('pipe', 'dp'), pairs)]
    ppermute x10, starting transfers between devices: 12.1 us -> 4.76 us  [swap_cores(): return lax.ppermute(value, 'pipe', [(0, 1), (1, 0)])]
    ppermute x1, starting transfers between devices: 1.29 us -> 8.28 us  [on_device(): got = lax.ppermute(second_weights, 'pipe', [(1, 0)])]
    ppermute x29, waiting for transfers between devices: 51.3 us -> 56.3 us  [xor_permute(): return lax.ppermute(value, 'dp', [(i, i ^ mask) for i in range(count)])]
  transfers between devices with their start and end apart: 100 -> 100, of which waited for: 39 -> 40; matrix products, arithmetic and copies ran while one was open for 2% -> 2% of each run, Pallas kernels for 24% -> 24%
where the time goes in v2:
time: 401 us; the launch traced here: 393 us
  starting transfers between devices  127 us (32%)
  Pallas kernels  126 us (31%)
  waiting for transfers between devices  124 us (31%)
  local copies, waits for them, and re-layouts  8.26 us (2%)
  other arithmetic  5.21 us (1%)
    ppermute x48, waiting for transfers between devices, plane_turn(): return lax.ppermute(value, ('pipe', 'dp'), pairs)  56.6 us
    ppermute x29, waiting for transfers between devices, xor_permute(): return lax.ppermute(value, 'dp', [(i, i ^ mask) for i in range(count)])  56.3 us
    ppermute x48, starting transfers between devices, plane_turn(): return lax.ppermute(value, ('pipe', 'dp'), pairs)  54.4 us
    pallas_call x11, Pallas kernels, single(): return made(meta, *[array for array, _ in ins])  44.8 us
    ppermute x29, starting transfers between devices, xor_permute(): return lax.ppermute(value, 'dp', [(i, i ^ mask) for i in range(count)])  39.6 us
    ppermute x9, starting transfers between devices, to_core(): arrived.append(lax.ppermute(both, ('pipe', 'dp'), pairs))  15.4 us
    pallas_call x1, Pallas kernels, on_device(): call(rows_out, shape_of((2 * WORK, HB * WB * C0), BF16), (HB,), [pl.Block...  8.88 us
    pallas_call x3, Pallas kernels, unpack(): call(functools.partial(unpack_kernel, jobs, chunk), pltpu.HBM((rows, 256)...  8.29 us
  transfers between devices with their start and end apart: 100, of which 40 were waited for; matrix products, arithmetic and copies ran while one was open for 2% of the time, Pallas kernels for 24%

profile of v2, /device:TPU:0, one launch (start us, length us, event | category | flops | bytes accessed | tf_op | source)
XLA Modules:
  0.0 392.9 jit_solution(4200406042377766025)
XLA Ops:
  9.0 5.4 %shard_map.86 = (bf16[272,256]{1,0:T(8,128)(2,1)S(1)}, bf16[272,256]{1,0:T(8,128)(2,1)S(1)}, bf16[272,256]{1,0:T(8,128)(2,1)S(1)}, bf16[272,256]{1,0:T(8,128)(2,...) custom-call(s32[15]{0:T(128)S(1)} %concatenate.57.meta, ...), custom_call_target="tpu_custom_call" | custom-call | bytes 18000000 | tf_op jit(solution)/shard_map/pallas_call | solution.py:1122
  20.1 4.8 %shard_map.87.refs_7_.refs_8_.refs_12_.refs_14_.refs_11_ = bf16[10240,256]{1,0:T(8,128)(2,1)} custom-call(s32[15]{0:T(128)S(1)} %concatenate.57.meta, bf16[1,6029312]{1,0:T(2,128)(2,1)} %raw_ref.3), custom_call_target="tpu_custom_call" | custom-call | bytes 28800000 | tf_op jit(solution)/shard_map/pallas_call | solution.py:854
  25.0 4.1 %collective-permute-start.5 = (bf16[10240,256]{1,0:T(8,128)(2,1)}, bf16[10240,256]{1,0:T(8,128)(2,1)}, u32[]{:S(2)}, u32[]{:S(2)}) collective-permute-start(bf16[10240,256]{1,0:T(8,128)(2,1)} %shard_map.87.refs_7_.refs_8_.refs_12_.refs_14_.refs_11_), channel_id=1, source_target_pairs={{0,16},{16,0},{1,17},{17,1},{2,18},{18,2},{3,19},{19,3},{4,20},{20... | collective-permute-start | bytes 15728648 | tf_op jit(solution)/shard_map/ppermute | solution.py:1038
  29.2 5.7 %collective-permute-done.1 = f32[2,5120]{1,0:T(2,128)S(1)} collective-permute-done((f32[2,5120]{1,0:T(2,128)S(1)}, f32[2,5120]{1,0:T(2,128)S(1)}, u32[]{:S(2)}, u32[]{:S(2)}) %collective-permute-start.1) | collective-permute-done | bytes 40992 | tf_op jit(solution)/shard_map/ppermute | solution.py:1038
  37.5 8.3 %collective-permute-start.18 = (bf16[13312,256]{1,0:T(8,128)(2,1)}, bf16[13312,256]{1,0:T(8,128)(2,1)}, u32[]{:S(2)}, u32[]{:S(2)}) collective-permute-start(bf16[13312,256]{1,0:T(8,128)(2,1)} %shard_map.89.refs_8_.refs_14_.refs_12_), channel_id=1, source_target_pairs={{16,0},{17,1},{18,2},{19,3},{20,4},{21,5},{22,6},{23,7},{24,8},{25... | collective-permute-start | bytes 20447240 | tf_op jit(solution)/shard_map/ppermute | solution.py:1173
  59.5 4.5 %shard_map.90 = (f32[2,384]{1,0:T(2,128)S(1)}, bf16[4,256,256]{2,1,0:T(8,128)(2,1)}, f32[4,256,256]{2,1,0:T(8,128)S(1)}, f32[4,256,256]{2,1,0:T(8,128)}, f32[2,256]{1,0:T(2,128)S(1)}) custom-call(s32[15]{0:T(128)S(1)} %concatenate.57.meta, f32[2,384]{1,0:T(2,128)S(1)} %get-tuple-element.137.refs_0_, f32[2,384]{1,0:T(2,128)S(1)} %collective-permute-done.7.refs_1_, ...), custom_call_target="tpu_custom_call" | custom-call | bytes 18000000 | tf_op jit(solution)/shard_map/pallas_call | solution.py:198
  79.7 7.4 %shard_map.92 = (f32[2,1024]{1,0:T(2,128)S(1)}, bf16[256,1024]{1,0:T(8,128)(2,1)}, f32[256,1024]{1,0:T(8,128)}, f32[256,1024]{1,0:T(8,128)}, f32[256,512]{1,0:T(...) custom-call(s32[15]{0:T(128)S(1)} %concatenate.57.meta, ...), custom_call_target="tpu_custom_call" | custom-call | bytes 18000000 | tf_op jit(solution)/shard_map/pallas_call | solution.py:1192
  94.0 4.5 %shard_map.93 = (f32[2,512]{1,0:T(2,128)S(1)}, bf16[256,512]{1,0:T(8,128)(2,1)}, f32[256,512]{1,0:T(8,128)S(1)}, f32[256,512]{1,0:T(8,128)}, f32[2,512]{1,0:T(2,128)S(1)}) custom-call(s32[15]{0:T(128)S(1)} %concatenate.57.meta, f32[2,512]{1,0:T(2,128)S(1)} %get-tuple-element.152.refs_0_, f32[2,512]{1,0:T(2,128)S(1)} %collective-permute-done.20.refs_1_, ...), custom_call_target="tpu_custom_call" | custom-call | bytes 18000000 | tf_op jit(solution)/shard_map/pallas_call | solution.py:198
  114.9 8.6 %collective-permute-done.31.refs_15_ = bf16[64,2048]{1,0:T(8,128)(2,1)S(1)} collective-permute-done((bf16[64,2048]{1,0:T(8,128)(2,1)S(1)}, bf16[64,2048]{1,0:T(8,128)(2,1)S(1)}, u32[]{:S(2)}, u32[]{:S(2)}) %collective-permute-start.31) | collective-permute-done | bytes 262176 | tf_op jit(solution)/shard_map/ppermute | solution.py:1043
  127.2 5.8 %shard_map.95 = (f32[2,2048]{1,0:T(2,128)S(1)}, f32[2,2048]{1,0:T(2,128)S(1)}, bf16[64,2048]{1,0:T(8,128)(2,1)S(1)}, bf16[64,2048]{1,0:T(8,128)(2,1)S(1)}, bf16[...) custom-call(s32[15]{0:T(128)S(1)} %concatenate.57.meta, ...), custom_call_target="tpu_custom_call" | custom-call | bytes 18000000 | tf_op jit(solution)/shard_map/pallas_call | solution.py:1253
  139.1 5.8 %shard_map.96 = (f32[3,2048]{1,0:T(4,128)S(1)}, bf16[2,256,2048]{2,1,0:T(8,128)(2,1)S(1)}, bf16[256,2048]{1,0:T(8,128)(2,1)S(1)}, f32[256,512]{1,0:T(8,128)S(1)}, f32[2,512]{1,0:T(2,128)S(1)}) custom-call(s32[15]{0:T(128)S(1)} %concatenate.57.meta, f32[3,2048]{1,0:T(4,128)S(1)} %get-tuple-element.168.refs_0_, f32[3,2048]{1,0:T(4,128)S(1)} %collective-permute-done.37.refs_1_, ...), custom_call_target="tpu_custom_call" | custom-call | bytes 18000000 | tf_op jit(solution)/shard_map/pallas_call | solution.py:198
  151.7 5.3 %shard_map.97 = (f32[2,512]{1,0:T(2,128)S(1)}, bf16[2,256,256]{2,1,0:T(8,128)(2,1)S(1)}, f32[256,512]{1,0:T(8,128)S(1)}, f32[2,512]{1,0:T(2,128)S(1)}) custom-call(s32[15]{0:T(128)S(1)} %concatenate.57.meta, f32[2,512]{1,0:T(2,128)S(1)} %get-tuple-element.176.refs_0_, f32[2,512]{1,0:T(2,128)S(1)} %collective-permute-done.41.refs_1_, ...), custom_call_target="tpu_custom_call" | custom-call | bytes 18000000 | tf_op jit(solution)/shard_map/pallas_call | solution.py:198
  165.7 6.7 %shard_map.99 = (f32[2,512]{1,0:T(2,128)S(1)}, bf16[2,256,256]{2,1,0:T(8,128)(2,1)S(1)}, f32[256,1024]{1,0:T(8,128)S(1)}, f32[2,1024]{1,0:T(2,128)S(1)}) custom-call(s32[15]{0:T(128)S(1)} %concatenate.57.meta, f32[2,512]{1,0:T(2,128)S(1)} %get-tuple-element.183.refs_0_, f32[2,512]{1,0:T(2,128)S(1)} %collective-permute-done.45.refs_1_, ...), custom_call_target="tpu_custom_call" | custom-call | bytes 18000000 | tf_op jit(solution)/shard_map/pallas_call | solution.py:198
  178.2 7.3 %shard_map.100 = (f32[2,1024]{1,0:T(2,128)S(1)}, bf16[4,256,1024]{2,1,0:T(8,128)(2,1)}, f32[4,256,256]{2,1,0:T(8,128)S(1)}, f32[2,256]{1,0:T(2,128)S(1)}) custom-call(s32[15]{0:T(128)S(1)} %concatenate.57.meta, f32[2,1024]{1,0:T(2,128)S(1)} %get-tuple-element.192.refs_0_, f32[2,1024]{1,0:T(2,128)S(1)} %collective-permute-done.50.refs_1_, ...), custom_call_target="tpu_custom_call" | custom-call | bytes 18000000 | tf_op jit(solution)/shard_map/pallas_call | solution.py:1322
  192.8 6.8 %shard_map.102 = (f32[2,256]{1,0:T(2,128)S(1)}, bf16[4,256,256]{2,1,0:T(8,128)(2,1)}, f32[4,256,256]{2,1,0:T(8,128)S(1)}, f32[2,256]{1,0:T(2,128)S(1)}) custom-call(s32[15]{0:T(128)S(1)} %concatenate.57.meta, f32[2,256]{1,0:T(2,128)S(1)} %get-tuple-element.200.refs_0_, f32[2,256]{1,0:T(2,128)S(1)} %collective-permute-done.54.refs_1_, ...), custom_call_target="tpu_custom_call" | custom-call | bytes 18000000 | tf_op jit(solution)/shard_map/pallas_call | solution.py:1352
  213.9 7.4 %shard_map.103.refs_4_ = bf16[8704,128]{1,0:T(8,128)(2,1)} custom-call(s32[15]{0:T(128)S(1)} %concatenate.57.meta, bf16[4,256,256]{2,1,0:T(8,128)(2,1)} %get-tuple-element.204.a1_ref, bf16[4,256,256]{2,1,0:T(8,128)(2,1)} %get-tuple-element.205.d2_ref, bf16[4,256,256]{2,1,0:T(8,128)(2,1)} %get-tuple-element.194.refs_7_.a2_ref, ...), custom_call_target="tpu_custom_call" | custom-call | bytes 18000000 | tf_op jit(solution)/shard_map/pallas_call | solution.py:1369
  224.1 7.0 %collective-permute-done.61 = bf16[6144,128]{1,0:T(8,128)(2,1)S(1)} collective-permute-done((bf16[6144,128]{1,0:T(8,128)(2,1)}, bf16[6144,128]{1,0:T(8,128)(2,1)S(1)}, u32[]{:S(2)}, u32[]{:S(2)}) %collective-permute-start.61) | collective-permute-done | bytes 1572896 | tf_op jit(solution)/shard_map/ppermute | solution.py:1056
  237.7 14.4 %collective-permute-done.62 = bf16[3072,128]{1,0:T(8,128)(2,1)S(1)} collective-permute-done((bf16[3072,128]{1,0:T(8,128)(2,1)S(1)}, bf16[3072,128]{1,0:T(8,128)(2,1)S(1)}, u32[]{:S(2)}, u32[]{:S(2)}) %collective-permute-start.62) | collective-permute-done | bytes 786464 | tf_op jit(solution)/shard_map/ppermute | solution.py:1056
  252.5 6.5 %shard_map.105 = (bf16[4,256,1024]{2,1,0:T(8,128)(2,1)S(1)}, bf16[8704,128]{1,0:T(8,128)(2,1)}) custom-call(s32[15]{0:T(128)S(1)} %concatenate.57.meta, bf16[8,16,16,1024]{3,2,1,0:T(8,128)(2,1)} %x_ref.3, bf16[1024,256]{1,0:T(8,128)(2,1)} %shard_map.85.wa_ref, bf16[1024,256]{1,0:T(8,128)(2,1)} %copy-done.6, ...), custom_call_target="tpu_custom_call", output_to_operand_aliasing={{1}: (8, {})} | custom-call | bytes 18000000 | tf_op jit(solution)/shard_map/pallas_call | solution.py:1417
  261.1 5.7 %collective-permute-done.66 = bf16[1536,128]{1,0:T(8,128)(2,1)S(1)} collective-permute-done((bf16[1536,128]{1,0:T(8,128)(2,1)S(1)}, bf16[1536,128]{1,0:T(8,128)(2,1)S(1)}, u32[]{:S(2)}, u32[]{:S(2)}) %collective-permute-start.66) | collective-permute-done | bytes 393248 | tf_op jit(solution)/shard_map/ppermute | solution.py:1043
  266.9 4.5 %collective-permute-start.69 = (bf16[768,128]{1,0:T(8,128)(2,1)S(1)}, bf16[768,128]{1,0:T(8,128)(2,1)S(1)}, u32[]{:S(2)}, u32[]{:S(2)}) collective-permute-start(bf16[768,128]{1,0:T(8,128)(2,1)S(1)} %get-tuple-element.272), channel_id=1, source_target_pairs={{0,8},{1,9},{2,10},{3,11},{4,12},{5,13},{6,14},{7,15},{8,0},{9,1},... | collective-permute-start | bytes 589832 | tf_op jit(solution)/shard_map/ppermute | solution.py:1043
  272.4 7.3 %collective-permute-done.69 = bf16[768,128]{1,0:T(8,128)(2,1)S(1)} collective-permute-done((bf16[768,128]{1,0:T(8,128)(2,1)S(1)}, bf16[768,128]{1,0:T(8,128)(2,1)S(1)}, u32[]{:S(2)}, u32[]{:S(2)}) %collective-permute-start.69) | collective-permute-done | bytes 196640 | tf_op jit(solution)/shard_map/ppermute | solution.py:1043
  280.6 8.1 %collective-permute-done.70 = bf16[2816,128]{1,0:T(8,128)(2,1)S(1)} collective-permute-done((bf16[2816,128]{1,0:T(8,128)(2,1)S(1)}, bf16[2816,128]{1,0:T(8,128)(2,1)S(1)}, u32[]{:S(2)}, u32[]{:S(2)}) %collective-permute-start.70) | collective-permute-done | bytes 720928 | tf_op jit(solution)/shard_map/ppermute | solution.py:1056
  291.7 11.5 %collective-permute-done.73 = bf16[1408,128]{1,0:T(8,128)(2,1)S(1)} collective-permute-done((bf16[1408,128]{1,0:T(8,128)(2,1)S(1)}, bf16[1408,128]{1,0:T(8,128)(2,1)S(1)}, u32[]{:S(2)}, u32[]{:S(2)}) %collective-permute-start.73) | collective-permute-done | bytes 360480 | tf_op jit(solution)/shard_map/ppermute | solution.py:1043
  316.7 6.3 %collective-permute-done.79 = bf16[704,128]{1,0:T(8,128)(2,1)S(1)} collective-permute-done((bf16[704,128]{1,0:T(8,128)(2,1)S(1)}, bf16[704,128]{1,0:T(8,128)(2,1)S(1)}, u32[]{:S(2)}, u32[]{:S(2)}) %collective-permute-start.79) | collective-permute-done | bytes 180256 | tf_op jit(solution)/shard_map/ppermute | solution.py:1043
  328.3 5.0 %collective-permute-done.81 = bf16[1408,128]{1,0:T(8,128)(2,1)S(1)} collective-permute-done((bf16[1408,128]{1,0:T(8,128)(2,1)S(1)}, bf16[1408,128]{1,0:T(8,128)(2,1)S(1)}, u32[]{:S(2)}, u32[]{:S(2)}) %collective-permute-start.81) | collective-permute-done | bytes 360480 | tf_op jit(solution)/shard_map/ppermute | solution.py:1043
  340.8 8.9 %shard_map.106 = bf16[8,262144]{1,0:T(8,128)(2,1)} custom-call(s32[15]{0:T(128)S(1)} %concatenate.57.meta, bf16[4,256,1024]{2,1,0:T(8,128)(2,1)S(1)} %get-tuple-element.243.x_ref, bf16[4,256,1024]{2,1,0:T(8,128)(2,1)S(1)} %collective-permute-done.83.xg_ref, bf16[4,64,2048]{2,1,0:T(8,128)(2,1)S(1)} %pad_maximum_fusion.2.y_ref, ...), custom_call_target="tpu_custom_call" | custom-call | bytes 32400000 | tf_op jit(solution)/shard_map/pallas_call | solution.py:1466
  353.0 5.0 %collective-permute-done.86 = bf16[544,128]{1,0:T(8,128)(2,1)S(1)} collective-permute-done((bf16[544,128]{1,0:T(8,128)(2,1)S(1)}, bf16[544,128]{1,0:T(8,128)(2,1)S(1)}, u32[]{:S(2)}, u32[]{:S(2)}) %collective-permute-start.86) | collective-permute-done | bytes 139296 | tf_op jit(solution)/shard_map/ppermute | solution.py:1043
  361.0 3.9 collective-permute-start.92
  366.3 8.0 %shard_map.107.refs_0_ = f32[47104,128]{1,0:T(8,128)} custom-call(s32[15]{0:T(128)S(1)} %concatenate.57.meta, bf16[6144,128]{1,0:T(8,128)(2,1)S(1)} %pad_maximum_fusion.refs_0_, bf16[6144,128]{1,0:T(8,128)(2,1)S(1)} %collective-permute-done.87.refs_1_, bf16[6144,128]{1,0:T(8,128)(2,1)S(1)} %collective-permute-done.88.refs_2_, ...), custom_call_target="tpu_custom_call" | custom-call | bytes 28800000 | tf_op jit(solution)/shard_map/pallas_call | solution.py:1485
  381.3 4.5 %shard_map.108.refs_0_ = f32[47104,128]{1,0:T(8,128)} custom-call(s32[15]{0:T(128)S(1)} %concatenate.57.meta, f32[47104,128]{1,0:T(8,128)} %shard_map.107.refs_0_, bf16[5632,128]{1,0:T(8,128)(2,1)S(1)} %pad_maximum_fusion.1.refs_1_, bf16[5632,128]{1,0:T(8,128)(2,1)S(1)} %collective-permute-done.91.refs_2_, ...), custom_call_target="tpu_custom_call", output_to_operand_aliasing={{}: (1, {})} | custom-call | bytes 18000000 | tf_op jit(solution)/shard_map/pallas_call | solution.py:1489
  388.0 4.4 %shard_map.109 = f32[47104,128]{1,0:T(8,128)} custom-call(s32[15]{0:T(128)S(1)} %concatenate.57.meta, f32[47104,128]{1,0:T(8,128)} %shard_map.108.refs_0_, bf16[5632,128]{1,0:T(8,128)(2,1)S(1)} %pad_maximum_fusion.1.refs_1_, bf16[5632,128]{1,0:T(8,128)(2,1)S(1)} %collective-permute-done.91.refs_2_, ...), custom_call_target="tpu_custom_call", output_to_operand_aliasing={{}: (1, {})} | custom-call | bytes 18000000 | tf_op jit(solution)/shard_map/pallas_call | solution.py:1493
  (282 shorter events, 181.4 us)
Async XLA Ops:
  14.4 20.5 %collective-permute-start.2 = (bf16[272,256]{1,0:T(8,128)(2,1)S(1)}, bf16[272,256]{1,0:T(8,128)(2,1)S(1)}, u32[]{:S(2)}, u32[]{:S(2)}) collective-permute-start(bf16[272,256]{1,0:T(8,128)(2,1)S(1)} %get-tuple-element.131), channel_id=1, source_target_pairs={{0,4},{1,5},{2,6},{3,7},{4,0},{5,1},{6,2},{7,3},{8,12},{9,13},{10,... | collective-permute-start | bytes 417800 | tf_op jit(solution)/shard_map/ppermute | solution.py:1043
  17.5 17.4 %collective-permute-start.3 = (bf16[272,256]{1,0:T(8,128)(2,1)S(1)}, bf16[272,256]{1,0:T(8,128)(2,1)S(1)}, u32[]{:S(2)}, u32[]{:S(2)}) collective-permute-start(bf16[272,256]{1,0:T(8,128)(2,1)S(1)} %get-tuple-element.132), channel_id=1, source_target_pairs={{0,8},{1,9},{2,10},{3,11},{4,12},{5,13},{6,14},{7,15},{8,0},{9,1},... | collective-permute-start | bytes 417800 | tf_op jit(solution)/shard_map/ppermute | solution.py:1043
  20.1 14.8 %collective-permute-start.4 = (bf16[272,256]{1,0:T(8,128)(2,1)S(1)}, bf16[272,256]{1,0:T(8,128)(2,1)S(1)}, u32[]{:S(2)}, u32[]{:S(2)}) collective-permute-start(bf16[272,256]{1,0:T(8,128)(2,1)S(1)} %get-tuple-element.133), channel_id=1, source_target_pairs={{0,12},{1,13},{2,14},{3,15},{4,8},{5,9},{6,10},{7,11},{8,4},{9,5},... | collective-permute-start | bytes 417800 | tf_op jit(solution)/shard_map/ppermute | solution.py:1043
  25.0 31.0 %collective-permute-start.5 = (bf16[10240,256]{1,0:T(8,128)(2,1)}, bf16[10240,256]{1,0:T(8,128)(2,1)}, u32[]{:S(2)}, u32[]{:S(2)}) collective-permute-start(bf16[10240,256]{1,0:T(8,128)(2,1)} %shard_map.87.refs_7_.refs_8_.refs_12_.refs_14_.refs_11_), channel_id=1, source_target_pairs={{0,16},{16,0},{1,17},{17,1},{2,18},{18,2},{3,19},{19,3},{4,20},{20... | collective-permute-start | bytes 15728648 | tf_op jit(solution)/shard_map/ppermute | solution.py:1038
  37.5 53.4 %collective-permute-start.18 = (bf16[13312,256]{1,0:T(8,128)(2,1)}, bf16[13312,256]{1,0:T(8,128)(2,1)}, u32[]{:S(2)}, u32[]{:S(2)}) collective-permute-start(bf16[13312,256]{1,0:T(8,128)(2,1)} %shard_map.89.refs_8_.refs_14_.refs_12_), channel_id=1, source_target_pairs={{16,0},{17,1},{18,2},{19,3},{20,4},{21,5},{22,6},{23,7},{24,8},{25... | collective-permute-start | bytes 20447240 | tf_op jit(solution)/shard_map/ppermute | solution.py:1173
  49.0 18.1 %collective-permute-start.10 = (bf16[64,1024]{1,0:T(8,128)(2,1)S(1)}, bf16[64,1024]{1,0:T(8,128)(2,1)S(1)}, u32[]{:S(2)}, u32[]{:S(2)}) collective-permute-start(bf16[64,1024]{1,0:T(8,128)(2,1)S(1)} %get-tuple-element.141), channel_id=1, source_target_pairs={{0,8},{1,9},{2,10},{3,11},{4,12},{5,13},{6,14},{7,15},{8,0},{9,1},... | collective-permute-start | bytes 393224 | tf_op jit(solution)/shard_map/ppermute | solution.py:1043
  52.4 25.1 %collective-permute-start.14 = (bf16[64,1024]{1,0:T(8,128)(2,1)S(1)}, bf16[64,1024]{1,0:T(8,128)(2,1)S(1)}, u32[]{:S(2)}, u32[]{:S(2)}) collective-permute-start(bf16[64,1024]{1,0:T(8,128)(2,1)S(1)} %get-tuple-element.146), channel_id=1, source_target_pairs={{0,12},{1,13},{2,14},{3,15},{4,8},{5,9},{6,10},{7,11},{8,4},{9,5},... | collective-permute-start | bytes 393224 | tf_op jit(solution)/shard_map/ppermute | solution.py:1043
  87.2 14.9 %collective-permute-start.23 = (bf16[64,2048]{1,0:T(8,128)(2,1)S(1)}, bf16[64,2048]{1,0:T(8,128)(2,1)S(1)}, u32[]{:S(2)}, u32[]{:S(2)}) collective-permute-start(bf16[64,2048]{1,0:T(8,128)(2,1)S(1)} %get-tuple-element.155), channel_id=1, source_target_pairs={{0,4},{1,5},{2,6},{3,7},{4,0},{5,1},{6,2},{7,3},{8,12},{9,13},{10,... | collective-permute-start | bytes 786440 | tf_op jit(solution)/shard_map/ppermute | solution.py:1043
  102.1 21.4 %collective-permute-start.31 = (bf16[64,2048]{1,0:T(8,128)(2,1)S(1)}, bf16[64,2048]{1,0:T(8,128)(2,1)S(1)}, u32[]{:S(2)}, u32[]{:S(2)}) collective-permute-start(bf16[64,2048]{1,0:T(8,128)(2,1)S(1)} %get-tuple-element.161), channel_id=1, source_target_pairs={{0,8},{1,9},{2,10},{3,11},{4,12},{5,13},{6,14},{7,15},{8,0},{9,1},... | collective-permute-start | bytes 786440 | tf_op jit(solution)/shard_map/ppermute | solution.py:1043
  106.9 17.1 %collective-permute-start.32 = (bf16[64,2048]{1,0:T(8,128)(2,1)S(1)}, bf16[64,2048]{1,0:T(8,128)(2,1)S(1)}, u32[]{:S(2)}, u32[]{:S(2)}) collective-permute-start(bf16[64,2048]{1,0:T(8,128)(2,1)S(1)} %get-tuple-element.162), channel_id=1, source_target_pairs={{0,12},{1,13},{2,14},{3,15},{4,8},{5,9},{6,10},{7,11},{8,4},{9,5},... | collective-permute-start | bytes 786440 | tf_op jit(solution)/shard_map/ppermute | solution.py:1043
  148.6 25.9 %collective-permute-start.49 = (bf16[64,2048]{1,0:T(8,128)(2,1)S(1)}, bf16[64,2048]{1,0:T(8,128)(2,1)S(1)}, u32[]{:S(2)}, u32[]{:S(2)}) collective-permute-start(bf16[64,2048]{1,0:T(8,128)(2,1)S(1)} %get-tuple-element.191), channel_id=1, source_target_pairs={{0,4},{1,5},{2,6},{3,7},{4,0},{5,1},{6,2},{7,3},{8,12},{9,13},{10,... | collective-permute-start | bytes 786440 | tf_op jit(solution)/shard_map/ppermute | solution.py:1043
  157.1 35.7 %collective-permute-start.53 = (bf16[64,2048]{1,0:T(8,128)(2,1)S(1)}, bf16[64,2048]{1,0:T(8,128)(2,1)S(1)}, u32[]{:S(2)}, u32[]{:S(2)}) collective-permute-start(bf16[64,2048]{1,0:T(8,128)(2,1)S(1)} %get-tuple-element.199), channel_id=1, source_target_pairs={{0,8},{1,9},{2,10},{3,11},{4,12},{5,13},{6,14},{7,15},{8,0},{9,1},... | collective-permute-start | bytes 786440 | tf_op jit(solution)/shard_map/ppermute | solution.py:1043
  209.1 22.0 %collective-permute-start.61 = (bf16[6144,128]{1,0:T(8,128)(2,1)}, bf16[6144,128]{1,0:T(8,128)(2,1)S(1)}, u32[]{:S(2)}, u32[]{:S(2)}) collective-permute-start(bf16[6144,128]{1,0:T(8,128)(2,1)} %get-tuple-element.254), channel_id=1, source_target_pairs={{0,1},{1,0},{2,3},{3,2},{4,5},{5,4},{6,7},{7,6},{8,9},{9,8},{10,11... | collective-permute-start | bytes 4718600 | tf_op jit(solution)/shard_map/ppermute | solution.py:1056
  231.6 20.5 %collective-permute-start.62 = (bf16[3072,128]{1,0:T(8,128)(2,1)S(1)}, bf16[3072,128]{1,0:T(8,128)(2,1)S(1)}, u32[]{:S(2)}, u32[]{:S(2)}) collective-permute-start(bf16[3072,128]{1,0:T(8,128)(2,1)S(1)} %get-tuple-element.260), channel_id=1, source_target_pairs={{0,2},{1,3},{2,0},{3,1},{4,6},{5,7},{6,4},{7,5},{8,10},{9,11},{10,... | collective-permute-start | bytes 2359304 | tf_op jit(solution)/shard_map/ppermute | solution.py:1056
  231.9 20.5 %collective-permute-start.63 = (bf16[512,256]{1,0:T(8,128)(2,1)S(1)}, bf16[512,256]{1,0:T(8,128)(2,1)S(1)}, u32[]{:S(2)}, u32[]{:S(2)}) collective-permute-start(bf16[512,256]{1,0:T(8,128)(2,1)S(1)} %get-tuple-element.220), channel_id=1, source_target_pairs={{0,4},{1,5},{2,6},{3,7},{4,0},{5,1},{6,2},{7,3},{8,12},{9,13},{10,... | collective-permute-start | bytes 786440 | tf_op jit(solution)/shard_map/ppermute | solution.py:1043
  232.7 19.8 %collective-permute-start.64 = (bf16[512,256]{1,0:T(8,128)(2,1)S(1)}, bf16[512,256]{1,0:T(8,128)(2,1)S(1)}, u32[]{:S(2)}, u32[]{:S(2)}) collective-permute-start(bf16[512,256]{1,0:T(8,128)(2,1)S(1)} %get-tuple-element.221), channel_id=1, source_target_pairs={{0,8},{1,9},{2,10},{3,11},{4,12},{5,13},{6,14},{7,15},{8,0},{9,1},... | collective-permute-start | bytes 786440 | tf_op jit(solution)/shard_map/ppermute | solution.py:1043
  234.7 17.8 %collective-permute-start.65 = (bf16[512,256]{1,0:T(8,128)(2,1)S(1)}, bf16[512,256]{1,0:T(8,128)(2,1)S(1)}, u32[]{:S(2)}, u32[]{:S(2)}) collective-permute-start(bf16[512,256]{1,0:T(8,128)(2,1)S(1)} %get-tuple-element.222), channel_id=1, source_target_pairs={{0,12},{1,13},{2,14},{3,15},{4,8},{5,9},{6,10},{7,11},{8,4},{9,5},... | collective-permute-start | bytes 786440 | tf_op jit(solution)/shard_map/ppermute | solution.py:1043
  236.5 35.0 %collective-permute-start.67 = (bf16[5632,128]{1,0:T(8,128)(2,1)S(1)}, bf16[5632,128]{1,0:T(8,128)(2,1)S(1)}, u32[]{:S(2)}, u32[]{:S(2)}) collective-permute-start(bf16[5632,128]{1,0:T(8,128)(2,1)S(1)} %get-tuple-element.227), channel_id=1, source_target_pairs={{0,1},{1,0},{2,3},{3,2},{4,5},{5,4},{6,7},{7,6},{8,9},{9,8},{10,11... | collective-permute-start | bytes 4325384 | tf_op jit(solution)/shard_map/ppermute | solution.py:1056
  272.0 16.7 %collective-permute-start.70 = (bf16[2816,128]{1,0:T(8,128)(2,1)S(1)}, bf16[2816,128]{1,0:T(8,128)(2,1)S(1)}, u32[]{:S(2)}, u32[]{:S(2)}) collective-permute-start(bf16[2816,128]{1,0:T(8,128)(2,1)S(1)} %get-tuple-element.262), channel_id=1, source_target_pairs={{0,2},{1,3},{2,0},{3,1},{4,6},{5,7},{6,4},{7,5},{8,10},{9,11},{10,... | collective-permute-start | bytes 2162696 | tf_op jit(solution)/shard_map/ppermute | solution.py:1056
  288.9 15.6 %collective-permute-start.75 = (bf16[1536,128]{1,0:T(8,128)(2,1)S(1)}, bf16[1536,128]{1,0:T(8,128)(2,1)S(1)}, u32[]{:S(2)}, u32[]{:S(2)}) collective-permute-start(bf16[1536,128]{1,0:T(8,128)(2,1)S(1)} %pad_maximum_fusion.6), channel_id=1, source_target_pairs={{0,4},{1,5},{2,6},{3,7},{4,0},{5,1},{6,2},{7,3},{8,12},{9,13},{10,... | collective-permute-start | bytes 1179656 | tf_op jit(solution)/shard_map/ppermute | solution.py:1043
  289.2 13.9 %collective-permute-start.73 = (bf16[1408,128]{1,0:T(8,128)(2,1)S(1)}, bf16[1408,128]{1,0:T(8,128)(2,1)S(1)}, u32[]{:S(2)}, u32[]{:S(2)}) collective-permute-start(bf16[1408,128]{1,0:T(8,128)(2,1)S(1)} %get-tuple-element.268), channel_id=1, source_target_pairs={{0,4},{1,5},{2,6},{3,7},{4,0},{5,1},{6,2},{7,3},{8,12},{9,13},{10,... | collective-permute-start | bytes 1081352 | tf_op jit(solution)/shard_map/ppermute | solution.py:1043
  304.6 34.8 %collective-permute-start.83 = (bf16[4,256,1024]{2,1,0:T(8,128)(2,1)S(1)}, bf16[4,256,1024]{2,1,0:T(8,128)(2,1)S(1)}, u32[]{:S(2)}, u32[]{:S(2)}) collective-permute-start(bf16[4,256,1024]{2,1,0:T(8,128)(2,1)S(1)} %get-tuple-element.243.x_ref), channel_id=1, source_target_pairs={{16,0},{17,1},{18,2},{19,3},{20,4},{21,5},{22,6},{23,7},{24,8},{25... | collective-permute-start | bytes 6291464 | tf_op jit(solution)/shard_map/ppermute | solution.py:1430
  333.3 19.6 %collective-permute-start.85 = (bf16[2816,128]{1,0:T(8,128)(2,1)S(1)}, bf16[2816,128]{1,0:T(8,128)(2,1)S(1)}, u32[]{:S(2)}, u32[]{:S(2)}) collective-permute-start(bf16[2816,128]{1,0:T(8,128)(2,1)S(1)} %pad_maximum_fusion.4), channel_id=1, source_target_pairs={{0,2},{1,3},{2,0},{3,1},{4,6},{5,7},{6,4},{7,5},{8,10},{9,11},{10,... | collective-permute-start | bytes 2162696 | tf_op jit(solution)/shard_map/ppermute | solution.py:1056
  336.0 22.8 %collective-permute-start.98 = (f32[2,5120]{1,0:T(2,128)S(1)}, f32[2,5120]{1,0:T(2,128)S(1)}, u32[]{:S(2)}, u32[]{:S(2)}) collective-permute-start(f32[2,5120]{1,0:T(2,128)S(1)} %select_add_fusion), channel_id=1, source_target_pairs={{0,4},{1,5},{2,6},{3,7},{4,0},{5,1},{6,2},{7,3},{8,12},{9,13},{10,... | collective-permute-start | bytes 122888 | tf_op jit(solution)/shard_map/ppermute | solution.py:1043
  336.1 24.8 %collective-permute-start.89 = (bf16[6144,128]{1,0:T(8,128)(2,1)S(1)}, bf16[6144,128]{1,0:T(8,128)(2,1)S(1)}, u32[]{:S(2)}, u32[]{:S(2)}) collective-permute-start(bf16[6144,128]{1,0:T(8,128)(2,1)S(1)} %pad_maximum_fusion.refs_0_), channel_id=1, source_target_pairs={{16,18},{17,19},{18,16},{19,17},{20,22},{21,23},{22,20},{23,21},{2... | collective-permute-start | bytes 4718600 | tf_op jit(solution)/shard_map/ppermute | solution.py:1094
  336.9 24.1 %collective-permute-start.88 = (bf16[6144,128]{1,0:T(8,128)(2,1)S(1)}, bf16[6144,128]{1,0:T(8,128)(2,1)S(1)}, u32[]{:S(2)}, u32[]{:S(2)}) collective-permute-start(bf16[6144,128]{1,0:T(8,128)(2,1)S(1)} %pad_maximum_fusion.refs_0_), channel_id=1, source_target_pairs={{0,17},{1,16},{2,19},{3,18},{4,21},{5,20},{6,23},{7,22},{8,25},{9,... | collective-permute-start | bytes 4718600 | tf_op jit(solution)/shard_map/ppermute | solution.py:1094
  339.4 25.5 %collective-permute-start.87 = (bf16[6144,128]{1,0:T(8,128)(2,1)S(1)}, bf16[6144,128]{1,0:T(8,128)(2,1)S(1)}, u32[]{:S(2)}, u32[]{:S(2)}) collective-permute-start(bf16[6144,128]{1,0:T(8,128)(2,1)S(1)} %pad_maximum_fusion.refs_0_), channel_id=1, source_target_pairs={{0,16},{1,17},{2,18},{3,19},{4,20},{5,21},{6,22},{7,23},{8,24},{9,... | collective-permute-start | bytes 4718600 | tf_op jit(solution)/shard_map/ppermute | solution.py:1094
  358.0 19.8 %collective-permute-start.93 = (bf16[5632,128]{1,0:T(8,128)(2,1)S(1)}, bf16[5632,128]{1,0:T(8,128)(2,1)S(1)}, u32[]{:S(2)}, u32[]{:S(2)}) collective-permute-start(bf16[5632,128]{1,0:T(8,128)(2,1)S(1)} %pad_maximum_fusion.1.refs_1_), channel_id=1, source_target_pairs={{16,18},{17,19},{18,16},{19,17},{20,22},{21,23},{22,20},{23,21},{2... | collective-permute-start | bytes 4325384 | tf_op jit(solution)/shard_map/ppermute | solution.py:1094
  358.8 15.5 %collective-permute-start.90 = (bf16[1088,128]{1,0:T(8,128)(2,1)S(1)}, bf16[1088,128]{1,0:T(8,128)(2,1)S(1)}, u32[]{:S(2)}, u32[]{:S(2)}) collective-permute-start(bf16[1088,128]{1,0:T(8,128)(2,1)S(1)} %pad_maximum_fusion.8), channel_id=1, source_target_pairs={{0,2},{1,3},{2,0},{3,1},{4,6},{5,7},{6,4},{7,5},{8,10},{9,11},{10,... | collective-permute-start | bytes 835592 | tf_op jit(solution)/shard_map/ppermute | solution.py:1056
  360.9 15.6 %collective-permute-start.99 = (f32[2,5120]{1,0:T(2,128)S(1)}, f32[2,5120]{1,0:T(2,128)S(1)}, u32[]{:S(2)}, u32[]{:S(2)}) collective-permute-start(f32[2,5120]{1,0:T(2,128)S(1)} %fusion.8), channel_id=1, source_target_pairs={{0,8},{1,9},{2,10},{3,11},{4,12},{5,13},{6,14},{7,15},{8,0},{9,1},... | collective-permute-start | bytes 122888 | tf_op jit(solution)/shard_map/ppermute | solution.py:1043
  361.0 20.3 %collective-permute-start.92 = (bf16[5632,128]{1,0:T(8,128)(2,1)S(1)}, bf16[5632,128]{1,0:T(8,128)(2,1)S(1)}, u32[]{:S(2)}, u32[]{:S(2)}) collective-permute-start(bf16[5632,128]{1,0:T(8,128)(2,1)S(1)} %pad_maximum_fusion.1.refs_1_), channel_id=1, source_target_pairs={{0,17},{1,16},{2,19},{3,18},{4,21},{5,20},{6,23},{7,22},{8,25},{9,... | collective-permute-start | bytes 4325384 | tf_op jit(solution)/shard_map/ppermute | solution.py:1094
  364.9 16.4 %collective-permute-start.91 = (bf16[5632,128]{1,0:T(8,128)(2,1)S(1)}, bf16[5632,128]{1,0:T(8,128)(2,1)S(1)}, u32[]{:S(2)}, u32[]{:S(2)}) collective-permute-start(bf16[5632,128]{1,0:T(8,128)(2,1)S(1)} %pad_maximum_fusion.1.refs_1_), channel_id=1, source_target_pairs={{0,16},{1,17},{2,18},{3,19},{4,20},{5,21},{6,22},{7,23},{8,24},{9,... | collective-permute-start | bytes 4325384 | tf_op jit(solution)/shard_map/ppermute | solution.py:1094
  (83 other events, 567.8 us)

commit v3 on v2

--- a/solution.py
+++ b/solution.py
@@ -778,30 +778,17 @@
     put_shards(out_ref, MIDDLE, 9 * M1 // 8, meta[CORE], False, first)
 
 
-def front_grad_two(meta, a1_ref, d2_ref, a2_ref, d3_ref, out_ref, acc2_ref, acc3_ref):
-    slot = pl.program_id(0)
-    conv = dot_tn(a1_ref[0], nine_shifts(d2_ref[0].astype(F32), HB, WB))
-    last = dot_tn(a2_ref[0], d3_ref[0])
-
-    @pl.when(slot == 0)
-    def _():
-        acc2_ref[...] = conv
-        acc3_ref[...] = last
-
-    @pl.when(slot > 0)
-    def _():
-        acc2_ref[...] += conv
-        acc3_ref[...] += last
-
-    @pl.when(slot == WORK - 1)
-    def _():
-        for tap in range(9):
-            for tile in range(2):
-                start = 2 * C0 + tile * 9 * M0 + tap * M0
-                lanes = tap * M0 + tile * 128
-                out_ref[start : start + M0, :] = acc2_ref[:, lanes : lanes + 128].astype(BF16)
-        out_ref[0 : 2 * C0, :] = jnp.zeros((2 * C0, 128), BF16)
-        put_tiles(out_ref, 2 * C0 + 2 * 9 * M0, acc3_ref[...])
+def front_grad_two(meta, a1_ref, d2_ref, a2_ref, d3_ref, out_ref):
+    last = dot_tn(a2_ref[...].reshape(ROWS0, M0), d3_ref[...].reshape(ROWS0, C0))
+    put_tiles(out_ref, 2 * C0 + 2 * 9 * M0, last)
+    shifted = nine_shifts(d2_ref[...].reshape(ROWS0, M0).astype(F32), HB, WB)
+    left = a1_ref[...].reshape(ROWS0, M0)
+    out_ref[0 : 2 * C0, :] = jnp.zeros((2 * C0, 128), BF16)
+    for tap in range(9):
+        conv = dot_tn(left, shifted[:, tap * M0 : (tap + 1) * M0])
+        for tile in range(2):
+            start = 2 * C0 + tile * 9 * M0 + tap * M0
+            out_ref[start : start + M0, :] = conv[:, tile * 128 : (tile + 1) * 128].astype(BF16)
 
 
 def unpack_kernel(jobs, chunk, meta, raw_ref, out_ref, *refs):
@@ -1369,10 +1356,10 @@
     front = call(
         front_grad_two,
         hbm_of((2 * C0 + 2 * 9 * M0 + 8 * M0, 128), BF16),
-        (WORK,),
-        [per_image(PIX0, M0)] * 3 + [per_image(PIX0, C0)],
+        (1,),
+        [full(WORK, PIX0, M0)] * 3 + [full(WORK, PIX0, C0)],
         full(2 * C0 + 2 * 9 * M0 + 8 * M0, 128),
-        [pltpu.VMEM((M0, 9 * M0), F32), pltpu.VMEM((M0, C0), F32)],
+        limit=40,
     )(meta, in_hbm(a1), in_hbm(d2), in_hbm(a2b), in_hbm(d3))
     one, two = place >> 1, place & 1
     kept, sent = part_at(middle, one, 2), part_at(middle, 1 - one, 2)

time: 401 us -> 401 us (level)
  no operation moved by 1% of the time
where the time goes in v3:
time: 401 us; the launch traced here: 393 us
  starting transfers between devices  127 us (32%)
  waiting for transfers between devices  126 us (31%)
  Pallas kernels  124 us (31%)
  local copies, waits for them, and re-layouts  8.26 us (2%)
  other arithmetic  5.21 us (1%)
    ppermute x48, waiting for transfers between devices, plane_turn(): return lax.ppermute(value, ('pipe', 'dp'), pairs)  58.1 us
    ppermute x29, waiting for transfers between devices, xor_permute(): return lax.ppermute(value, 'dp', [(i, i ^ mask) for i in range(count)])  56.3 us
    ppermute x48, starting transfers between devices, plane_turn(): return lax.ppermute(value, ('pipe', 'dp'), pairs)  54.4 us
    pallas_call x11, Pallas kernels, single(): return made(meta, *[array for array, _ in ins])  44.8 us
    ppermute x29, starting transfers between devices, xor_permute(): return lax.ppermute(value, 'dp', [(i, i ^ mask) for i in range(count)])  39.6 us
    ppermute x9, starting transfers between devices, to_core(): arrived.append(lax.ppermute(both, ('pipe', 'dp'), pairs))  15.4 us
    pallas_call x1, Pallas kernels, on_device(): call(rows_out, shape_of((2 * WORK, HB * WB * C0), BF16), (HB,), [pl.Block...  8.88 us
    pallas_call x3, Pallas kernels, unpack(): call(functools.partial(unpack_kernel, jobs, chunk), pltpu.HBM((rows, 256)...  8.29 us
  transfers between devices with their start and end apart: 100, of which 40 were waited for; matrix products, arithmetic and copies ran while one was open for 2% of the time, Pallas kernels for 24%

profile of v3, /device:TPU:0, one launch (start us, length us, event | category | flops | bytes accessed | tf_op | source)
XLA Modules:
  0.0 392.9 jit_solution(12139053907358316586)
XLA Ops:
  9.0 5.4 %shard_map.86 = (bf16[272,256]{1,0:T(8,128)(2,1)S(1)}, bf16[272,256]{1,0:T(8,128)(2,1)S(1)}, bf16[272,256]{1,0:T(8,128)(2,1)S(1)}, bf16[272,256]{1,0:T(8,128)(2,...) custom-call(s32[15]{0:T(128)S(1)} %concatenate.57.meta, ...), custom_call_target="tpu_custom_call" | custom-call | bytes 18000000 | tf_op jit(solution)/shard_map/pallas_call | solution.py:1109
  20.1 4.8 %shard_map.87.refs_7_.refs_8_.refs_12_.refs_14_.refs_11_ = bf16[10240,256]{1,0:T(8,128)(2,1)} custom-call(s32[15]{0:T(128)S(1)} %concatenate.57.meta, bf16[1,6029312]{1,0:T(2,128)(2,1)} %raw_ref.3), custom_call_target="tpu_custom_call" | custom-call | bytes 28800000 | tf_op jit(solution)/shard_map/pallas_call | solution.py:841
  25.0 4.1 %collective-permute-start.5 = (bf16[10240,256]{1,0:T(8,128)(2,1)}, bf16[10240,256]{1,0:T(8,128)(2,1)}, u32[]{:S(2)}, u32[]{:S(2)}) collective-permute-start(bf16[10240,256]{1,0:T(8,128)(2,1)} %shard_map.87.refs_7_.refs_8_.refs_12_.refs_14_.refs_11_), channel_id=1, source_target_pairs={{0,16},{16,0},{1,17},{17,1},{2,18},{18,2},{3,19},{19,3},{4,20},{20... | collective-permute-start | bytes 15728648 | tf_op jit(solution)/shard_map/ppermute | solution.py:1025
  29.2 5.7 %collective-permute-done.1 = f32[2,5120]{1,0:T(2,128)S(1)} collective-permute-done((f32[2,5120]{1,0:T(2,128)S(1)}, f32[2,5120]{1,0:T(2,128)S(1)}, u32[]{:S(2)}, u32[]{:S(2)}) %collective-permute-start.1) | collective-permute-done | bytes 40992 | tf_op jit(solution)/shard_map/ppermute | solution.py:1025
  37.5 8.3 %collective-permute-start.18 = (bf16[13312,256]{1,0:T(8,128)(2,1)}, bf16[13312,256]{1,0:T(8,128)(2,1)}, u32[]{:S(2)}, u32[]{:S(2)}) collective-permute-start(bf16[13312,256]{1,0:T(8,128)(2,1)} %shard_map.89.refs_8_.refs_14_.refs_12_), channel_id=1, source_target_pairs={{16,0},{17,1},{18,2},{19,3},{20,4},{21,5},{22,6},{23,7},{24,8},{25... | collective-permute-start | bytes 20447240 | tf_op jit(solution)/shard_map/ppermute | solution.py:1160
  59.5 4.5 %shard_map.90 = (f32[2,384]{1,0:T(2,128)S(1)}, bf16[4,256,256]{2,1,0:T(8,128)(2,1)}, f32[4,256,256]{2,1,0:T(8,128)S(1)}, f32[4,256,256]{2,1,0:T(8,128)}, f32[2,256]{1,0:T(2,128)S(1)}) custom-call(s32[15]{0:T(128)S(1)} %concatenate.57.meta, f32[2,384]{1,0:T(2,128)S(1)} %get-tuple-element.137.refs_0_, f32[2,384]{1,0:T(2,128)S(1)} %collective-permute-done.7.refs_1_, ...), custom_call_target="tpu_custom_call" | custom-call | bytes 18000000 | tf_op jit(solution)/shard_map/pallas_call | solution.py:198
  79.7 7.4 %shard_map.92 = (f32[2,1024]{1,0:T(2,128)S(1)}, bf16[256,1024]{1,0:T(8,128)(2,1)}, f32[256,1024]{1,0:T(8,128)}, f32[256,1024]{1,0:T(8,128)}, f32[256,512]{1,0:T(...) custom-call(s32[15]{0:T(128)S(1)} %concatenate.57.meta, ...), custom_call_target="tpu_custom_call" | custom-call | bytes 18000000 | tf_op jit(solution)/shard_map/pallas_call | solution.py:1179
  94.0 4.5 %shard_map.93 = (f32[2,512]{1,0:T(2,128)S(1)}, bf16[256,512]{1,0:T(8,128)(2,1)}, f32[256,512]{1,0:T(8,128)S(1)}, f32[256,512]{1,0:T(8,128)}, f32[2,512]{1,0:T(2,128)S(1)}) custom-call(s32[15]{0:T(128)S(1)} %concatenate.57.meta, f32[2,512]{1,0:T(2,128)S(1)} %get-tuple-element.152.refs_0_, f32[2,512]{1,0:T(2,128)S(1)} %collective-permute-done.20.refs_1_, ...), custom_call_target="tpu_custom_call" | custom-call | bytes 18000000 | tf_op jit(solution)/shard_map/pallas_call | solution.py:198
  114.9 8.6 %collective-permute-done.31.refs_15_ = bf16[64,2048]{1,0:T(8,128)(2,1)S(1)} collective-permute-done((bf16[64,2048]{1,0:T(8,128)(2,1)S(1)}, bf16[64,2048]{1,0:T(8,128)(2,1)S(1)}, u32[]{:S(2)}, u32[]{:S(2)}) %collective-permute-start.31) | collective-permute-done | bytes 262176 | tf_op jit(solution)/shard_map/ppermute | solution.py:1030
  127.2 5.8 %shard_map.95 = (f32[2,2048]{1,0:T(2,128)S(1)}, f32[2,2048]{1,0:T(2,128)S(1)}, bf16[64,2048]{1,0:T(8,128)(2,1)S(1)}, bf16[64,2048]{1,0:T(8,128)(2,1)S(1)}, bf16[...) custom-call(s32[15]{0:T(128)S(1)} %concatenate.57.meta, ...), custom_call_target="tpu_custom_call" | custom-call | bytes 18000000 | tf_op jit(solution)/shard_map/pallas_call | solution.py:1240
  139.1 5.8 %shard_map.96 = (f32[3,2048]{1,0:T(4,128)S(1)}, bf16[2,256,2048]{2,1,0:T(8,128)(2,1)S(1)}, bf16[256,2048]{1,0:T(8,128)(2,1)S(1)}, f32[256,512]{1,0:T(8,128)S(1)}, f32[2,512]{1,0:T(2,128)S(1)}) custom-call(s32[15]{0:T(128)S(1)} %concatenate.57.meta, f32[3,2048]{1,0:T(4,128)S(1)} %get-tuple-element.168.refs_0_, f32[3,2048]{1,0:T(4,128)S(1)} %collective-permute-done.37.refs_1_, ...), custom_call_target="tpu_custom_call" | custom-call | bytes 18000000 | tf_op jit(solution)/shard_map/pallas_call | solution.py:198
  151.7 5.3 %shard_map.97 = (f32[2,512]{1,0:T(2,128)S(1)}, bf16[2,256,256]{2,1,0:T(8,128)(2,1)S(1)}, f32[256,512]{1,0:T(8,128)S(1)}, f32[2,512]{1,0:T(2,128)S(1)}) custom-call(s32[15]{0:T(128)S(1)} %concatenate.57.meta, f32[2,512]{1,0:T(2,128)S(1)} %get-tuple-element.176.refs_0_, f32[2,512]{1,0:T(2,128)S(1)} %collective-permute-done.41.refs_1_, ...), custom_call_target="tpu_custom_call" | custom-call | bytes 18000000 | tf_op jit(solution)/shard_map/pallas_call | solution.py:198
  165.7 6.7 %shard_map.99 = (f32[2,512]{1,0:T(2,128)S(1)}, bf16[2,256,256]{2,1,0:T(8,128)(2,1)S(1)}, f32[256,1024]{1,0:T(8,128)S(1)}, f32[2,1024]{1,0:T(2,128)S(1)}) custom-call(s32[15]{0:T(128)S(1)} %concatenate.57.meta, f32[2,512]{1,0:T(2,128)S(1)} %get-tuple-element.183.refs_0_, f32[2,512]{1,0:T(2,128)S(1)} %collective-permute-done.45.refs_1_, ...), custom_call_target="tpu_custom_call" | custom-call | bytes 18000000 | tf_op jit(solution)/shard_map/pallas_call | solution.py:198
  178.2 7.3 %shard_map.100 = (f32[2,1024]{1,0:T(2,128)S(1)}, bf16[4,256,1024]{2,1,0:T(8,128)(2,1)}, f32[4,256,256]{2,1,0:T(8,128)S(1)}, f32[2,256]{1,0:T(2,128)S(1)}) custom-call(s32[15]{0:T(128)S(1)} %concatenate.57.meta, f32[2,1024]{1,0:T(2,128)S(1)} %get-tuple-element.192.refs_0_, f32[2,1024]{1,0:T(2,128)S(1)} %collective-permute-done.50.refs_1_, ...), custom_call_target="tpu_custom_call" | custom-call | bytes 18000000 | tf_op jit(solution)/shard_map/pallas_call | solution.py:1309
  192.8 6.8 %shard_map.102 = (f32[2,256]{1,0:T(2,128)S(1)}, bf16[4,256,256]{2,1,0:T(8,128)(2,1)}, f32[4,256,256]{2,1,0:T(8,128)S(1)}, f32[2,256]{1,0:T(2,128)S(1)}) custom-call(s32[15]{0:T(128)S(1)} %concatenate.57.meta, f32[2,256]{1,0:T(2,128)S(1)} %get-tuple-element.200.refs_0_, f32[2,256]{1,0:T(2,128)S(1)} %collective-permute-done.54.refs_1_, ...), custom_call_target="tpu_custom_call" | custom-call | bytes 18000000 | tf_op jit(solution)/shard_map/pallas_call | solution.py:1339
  213.9 6.0 %shard_map.103.refs_4_ = bf16[8704,128]{1,0:T(8,128)(2,1)} custom-call(s32[15]{0:T(128)S(1)} %concatenate.57.meta, bf16[4,256,256]{2,1,0:T(8,128)(2,1)} %get-tuple-element.204.a1_ref, bf16[4,256,256]{2,1,0:T(8,128)(2,1)} %get-tuple-element.205.d2_ref, bf16[4,256,256]{2,1,0:T(8,128)(2,1)} %get-tuple-element.194.refs_7_.a2_ref, ...), custom_call_target="tpu_custom_call" | custom-call | bytes 18000000 | tf_op jit(solution)/shard_map/pallas_call | solution.py:1356
  222.6 8.4 %collective-permute-done.61 = bf16[6144,128]{1,0:T(8,128)(2,1)S(1)} collective-permute-done((bf16[6144,128]{1,0:T(8,128)(2,1)}, bf16[6144,128]{1,0:T(8,128)(2,1)S(1)}, u32[]{:S(2)}, u32[]{:S(2)}) %collective-permute-start.61) | collective-permute-done | bytes 1572896 | tf_op jit(solution)/shard_map/ppermute | solution.py:1043
  237.7 14.4 %collective-permute-done.62 = bf16[3072,128]{1,0:T(8,128)(2,1)S(1)} collective-permute-done((bf16[3072,128]{1,0:T(8,128)(2,1)S(1)}, bf16[3072,128]{1,0:T(8,128)(2,1)S(1)}, u32[]{:S(2)}, u32[]{:S(2)}) %collective-permute-start.62) | collective-permute-done | bytes 786464 | tf_op jit(solution)/shard_map/ppermute | solution.py:1043
  252.5 6.5 %shard_map.105 = (bf16[4,256,1024]{2,1,0:T(8,128)(2,1)S(1)}, bf16[8704,128]{1,0:T(8,128)(2,1)}) custom-call(s32[15]{0:T(128)S(1)} %concatenate.57.meta, bf16[8,16,16,1024]{3,2,1,0:T(8,128)(2,1)} %x_ref.3, bf16[1024,256]{1,0:T(8,128)(2,1)} %shard_map.85.wa_ref, bf16[1024,256]{1,0:T(8,128)(2,1)} %copy-done.6, ...), custom_call_target="tpu_custom_call", output_to_operand_aliasing={{1}: (8, {})} | custom-call | bytes 18000000 | tf_op jit(solution)/shard_map/pallas_call | solution.py:1404
  261.1 5.7 %collective-permute-done.66 = bf16[1536,128]{1,0:T(8,128)(2,1)S(1)} collective-permute-done((bf16[1536,128]{1,0:T(8,128)(2,1)S(1)}, bf16[1536,128]{1,0:T(8,128)(2,1)S(1)}, u32[]{:S(2)}, u32[]{:S(2)}) %collective-permute-start.66) | collective-permute-done | bytes 393248 | tf_op jit(solution)/shard_map/ppermute | solution.py:1030
  266.9 4.5 %collective-permute-start.69 = (bf16[768,128]{1,0:T(8,128)(2,1)S(1)}, bf16[768,128]{1,0:T(8,128)(2,1)S(1)}, u32[]{:S(2)}, u32[]{:S(2)}) collective-permute-start(bf16[768,128]{1,0:T(8,128)(2,1)S(1)} %get-tuple-element.272), channel_id=1, source_target_pairs={{0,8},{1,9},{2,10},{3,11},{4,12},{5,13},{6,14},{7,15},{8,0},{9,1},... | collective-permute-start | bytes 589832 | tf_op jit(solution)/shard_map/ppermute | solution.py:1030
  272.4 7.3 %collective-permute-done.69 = bf16[768,128]{1,0:T(8,128)(2,1)S(1)} collective-permute-done((bf16[768,128]{1,0:T(8,128)(2,1)S(1)}, bf16[768,128]{1,0:T(8,128)(2,1)S(1)}, u32[]{:S(2)}, u32[]{:S(2)}) %collective-permute-start.69) | collective-permute-done | bytes 196640 | tf_op jit(solution)/shard_map/ppermute | solution.py:1030
  280.6 8.1 %collective-permute-done.70 = bf16[2816,128]{1,0:T(8,128)(2,1)S(1)} collective-permute-done((bf16[2816,128]{1,0:T(8,128)(2,1)S(1)}, bf16[2816,128]{1,0:T(8,128)(2,1)S(1)}, u32[]{:S(2)}, u32[]{:S(2)}) %collective-permute-start.70) | collective-permute-done | bytes 720928 | tf_op jit(solution)/shard_map/ppermute | solution.py:1043
  291.7 11.5 %collective-permute-done.73 = bf16[1408,128]{1,0:T(8,128)(2,1)S(1)} collective-permute-done((bf16[1408,128]{1,0:T(8,128)(2,1)S(1)}, bf16[1408,128]{1,0:T(8,128)(2,1)S(1)}, u32[]{:S(2)}, u32[]{:S(2)}) %collective-permute-start.73) | collective-permute-done | bytes 360480 | tf_op jit(solution)/shard_map/ppermute | solution.py:1030
  316.7 6.3 %collective-permute-done.79 = bf16[704,128]{1,0:T(8,128)(2,1)S(1)} collective-permute-done((bf16[704,128]{1,0:T(8,128)(2,1)S(1)}, bf16[704,128]{1,0:T(8,128)(2,1)S(1)}, u32[]{:S(2)}, u32[]{:S(2)}) %collective-permute-start.79) | collective-permute-done | bytes 180256 | tf_op jit(solution)/shard_map/ppermute | solution.py:1030
  328.3 5.0 %collective-permute-done.81 = bf16[1408,128]{1,0:T(8,128)(2,1)S(1)} collective-permute-done((bf16[1408,128]{1,0:T(8,128)(2,1)S(1)}, bf16[1408,128]{1,0:T(8,128)(2,1)S(1)}, u32[]{:S(2)}, u32[]{:S(2)}) %collective-permute-start.81) | collective-permute-done | bytes 360480 | tf_op jit(solution)/shard_map/ppermute | solution.py:1030
  340.8 8.9 %shard_map.106 = bf16[8,262144]{1,0:T(8,128)(2,1)} custom-call(s32[15]{0:T(128)S(1)} %concatenate.57.meta, bf16[4,256,1024]{2,1,0:T(8,128)(2,1)S(1)} %get-tuple-element.243.x_ref, bf16[4,256,1024]{2,1,0:T(8,128)(2,1)S(1)} %collective-permute-done.83.xg_ref, bf16[4,64,2048]{2,1,0:T(8,128)(2,1)S(1)} %pad_maximum_fusion.2.y_ref, ...), custom_call_target="tpu_custom_call" | custom-call | bytes 32400000 | tf_op jit(solution)/shard_map/pallas_call | solution.py:1453
  353.0 5.0 %collective-permute-done.86 = bf16[544,128]{1,0:T(8,128)(2,1)S(1)} collective-permute-done((bf16[544,128]{1,0:T(8,128)(2,1)S(1)}, bf16[544,128]{1,0:T(8,128)(2,1)S(1)}, u32[]{:S(2)}, u32[]{:S(2)}) %collective-permute-start.86) | collective-permute-done | bytes 139296 | tf_op jit(solution)/shard_map/ppermute | solution.py:1030
  361.0 3.9 collective-permute-start.92
  366.3 8.0 %shard_map.107.refs_0_ = f32[47104,128]{1,0:T(8,128)} custom-call(s32[15]{0:T(128)S(1)} %concatenate.57.meta, bf16[6144,128]{1,0:T(8,128)(2,1)S(1)} %pad_maximum_fusion.refs_0_, bf16[6144,128]{1,0:T(8,128)(2,1)S(1)} %collective-permute-done.87.refs_1_, bf16[6144,128]{1,0:T(8,128)(2,1)S(1)} %collective-permute-done.88.refs_2_, ...), custom_call_target="tpu_custom_call" | custom-call | bytes 28800000 | tf_op jit(solution)/shard_map/pallas_call | solution.py:1472
  381.3 4.5 %shard_map.108.refs_0_ = f32[47104,128]{1,0:T(8,128)} custom-call(s32[15]{0:T(128)S(1)} %concatenate.57.meta, f32[47104,128]{1,0:T(8,128)} %shard_map.107.refs_0_, bf16[5632,128]{1,0:T(8,128)(2,1)S(1)} %pad_maximum_fusion.1.refs_1_, bf16[5632,128]{1,0:T(8,128)(2,1)S(1)} %collective-permute-done.91.refs_2_, ...), custom_call_target="tpu_custom_call", output_to_operand_aliasing={{}: (1, {})} | custom-call | bytes 18000000 | tf_op jit(solution)/shard_map/pallas_call | solution.py:1476
  388.0 4.4 %shard_map.109 = f32[47104,128]{1,0:T(8,128)} custom-call(s32[15]{0:T(128)S(1)} %concatenate.57.meta, f32[47104,128]{1,0:T(8,128)} %shard_map.108.refs_0_, bf16[5632,128]{1,0:T(8,128)(2,1)S(1)} %pad_maximum_fusion.1.refs_1_, bf16[5632,128]{1,0:T(8,128)(2,1)S(1)} %collective-permute-done.91.refs_2_, ...), custom_call_target="tpu_custom_call", output_to_operand_aliasing={{}: (1, {})} | custom-call | bytes 18000000 | tf_op jit(solution)/shard_map/pallas_call | solution.py:1480
  (282 shorter events, 181.4 us)
Async XLA Ops:
  14.4 20.5 %collective-permute-start.2 = (bf16[272,256]{1,0:T(8,128)(2,1)S(1)}, bf16[272,256]{1,0:T(8,128)(2,1)S(1)}, u32[]{:S(2)}, u32[]{:S(2)}) collective-permute-start(bf16[272,256]{1,0:T(8,128)(2,1)S(1)} %get-tuple-element.131), channel_id=1, source_target_pairs={{0,4},{1,5},{2,6},{3,7},{4,0},{5,1},{6,2},{7,3},{8,12},{9,13},{10,... | collective-permute-start | bytes 417800 | tf_op jit(solution)/shard_map/ppermute | solution.py:1030
  17.5 17.4 %collective-permute-start.3 = (bf16[272,256]{1,0:T(8,128)(2,1)S(1)}, bf16[272,256]{1,0:T(8,128)(2,1)S(1)}, u32[]{:S(2)}, u32[]{:S(2)}) collective-permute-start(bf16[272,256]{1,0:T(8,128)(2,1)S(1)} %get-tuple-element.132), channel_id=1, source_target_pairs={{0,8},{1,9},{2,10},{3,11},{4,12},{5,13},{6,14},{7,15},{8,0},{9,1},... | collective-permute-start | bytes 417800 | tf_op jit(solution)/shard_map/ppermute | solution.py:1030
  20.1 14.8 %collective-permute-start.4 = (bf16[272,256]{1,0:T(8,128)(2,1)S(1)}, bf16[272,256]{1,0:T(8,128)(2,1)S(1)}, u32[]{:S(2)}, u32[]{:S(2)}) collective-permute-start(bf16[272,256]{1,0:T(8,128)(2,1)S(1)} %get-tuple-element.133), channel_id=1, source_target_pairs={{0,12},{1,13},{2,14},{3,15},{4,8},{5,9},{6,10},{7,11},{8,4},{9,5},... | collective-permute-start | bytes 417800 | tf_op jit(solution)/shard_map/ppermute | solution.py:1030
  25.0 31.0 %collective-permute-start.5 = (bf16[10240,256]{1,0:T(8,128)(2,1)}, bf16[10240,256]{1,0:T(8,128)(2,1)}, u32[]{:S(2)}, u32[]{:S(2)}) collective-permute-start(bf16[10240,256]{1,0:T(8,128)(2,1)} %shard_map.87.refs_7_.refs_8_.refs_12_.refs_14_.refs_11_), channel_id=1, source_target_pairs={{0,16},{16,0},{1,17},{17,1},{2,18},{18,2},{3,19},{19,3},{4,20},{20... | collective-permute-start | bytes 15728648 | tf_op jit(solution)/shard_map/ppermute | solution.py:1025
  37.5 53.4 %collective-permute-start.18 = (bf16[13312,256]{1,0:T(8,128)(2,1)}, bf16[13312,256]{1,0:T(8,128)(2,1)}, u32[]{:S(2)}, u32[]{:S(2)}) collective-permute-start(bf16[13312,256]{1,0:T(8,128)(2,1)} %shard_map.89.refs_8_.refs_14_.refs_12_), channel_id=1, source_target_pairs={{16,0},{17,1},{18,2},{19,3},{20,4},{21,5},{22,6},{23,7},{24,8},{25... | collective-permute-start | bytes 20447240 | tf_op jit(solution)/shard_map/ppermute | solution.py:1160
  49.0 18.1 %collective-permute-start.10 = (bf16[64,1024]{1,0:T(8,128)(2,1)S(1)}, bf16[64,1024]{1,0:T(8,128)(2,1)S(1)}, u32[]{:S(2)}, u32[]{:S(2)}) collective-permute-start(bf16[64,1024]{1,0:T(8,128)(2,1)S(1)} %get-tuple-element.141), channel_id=1, source_target_pairs={{0,8},{1,9},{2,10},{3,11},{4,12},{5,13},{6,14},{7,15},{8,0},{9,1},... | collective-permute-start | bytes 393224 | tf_op jit(solution)/shard_map/ppermute | solution.py:1030
  52.4 25.1 %collective-permute-start.14 = (bf16[64,1024]{1,0:T(8,128)(2,1)S(1)}, bf16[64,1024]{1,0:T(8,128)(2,1)S(1)}, u32[]{:S(2)}, u32[]{:S(2)}) collective-permute-start(bf16[64,1024]{1,0:T(8,128)(2,1)S(1)} %get-tuple-element.146), channel_id=1, source_target_pairs={{0,12},{1,13},{2,14},{3,15},{4,8},{5,9},{6,10},{7,11},{8,4},{9,5},... | collective-permute-start | bytes 393224 | tf_op jit(solution)/shard_map/ppermute | solution.py:1030
  87.2 14.9 %collective-permute-start.23 = (bf16[64,2048]{1,0:T(8,128)(2,1)S(1)}, bf16[64,2048]{1,0:T(8,128)(2,1)S(1)}, u32[]{:S(2)}, u32[]{:S(2)}) collective-permute-start(bf16[64,2048]{1,0:T(8,128)(2,1)S(1)} %get-tuple-element.155), channel_id=1, source_target_pairs={{0,4},{1,5},{2,6},{3,7},{4,0},{5,1},{6,2},{7,3},{8,12},{9,13},{10,... | collective-permute-start | bytes 786440 | tf_op jit(solution)/shard_map/ppermute | solution.py:1030
  102.1 21.4 %collective-permute-start.31 = (bf16[64,2048]{1,0:T(8,128)(2,1)S(1)}, bf16[64,2048]{1,0:T(8,128)(2,1)S(1)}, u32[]{:S(2)}, u32[]{:S(2)}) collective-permute-start(bf16[64,2048]{1,0:T(8,128)(2,1)S(1)} %get-tuple-element.161), channel_id=1, source_target_pairs={{0,8},{1,9},{2,10},{3,11},{4,12},{5,13},{6,14},{7,15},{8,0},{9,1},... | collective-permute-start | bytes 786440 | tf_op jit(solution)/shard_map/ppermute | solution.py:1030
  106.9 17.1 %collective-permute-start.32 = (bf16[64,2048]{1,0:T(8,128)(2,1)S(1)}, bf16[64,2048]{1,0:T(8,128)(2,1)S(1)}, u32[]{:S(2)}, u32[]{:S(2)}) collective-permute-start(bf16[64,2048]{1,0:T(8,128)(2,1)S(1)} %get-tuple-element.162), channel_id=1, source_target_pairs={{0,12},{1,13},{2,14},{3,15},{4,8},{5,9},{6,10},{7,11},{8,4},{9,5},... | collective-permute-start | bytes 786440 | tf_op jit(solution)/shard_map/ppermute | solution.py:1030
  148.6 25.9 %collective-permute-start.49 = (bf16[64,2048]{1,0:T(8,128)(2,1)S(1)}, bf16[64,2048]{1,0:T(8,128)(2,1)S(1)}, u32[]{:S(2)}, u32[]{:S(2)}) collective-permute-start(bf16[64,2048]{1,0:T(8,128)(2,1)S(1)} %get-tuple-element.191), channel_id=1, source_target_pairs={{0,4},{1,5},{2,6},{3,7},{4,0},{5,1},{6,2},{7,3},{8,12},{9,13},{10,... | collective-permute-start | bytes 786440 | tf_op jit(solution)/shard_map/ppermute | solution.py:1030
  157.1 35.7 %collective-permute-start.53 = (bf16[64,2048]{1,0:T(8,128)(2,1)S(1)}, bf16[64,2048]{1,0:T(8,128)(2,1)S(1)}, u32[]{:S(2)}, u32[]{:S(2)}) collective-permute-start(bf16[64,2048]{1,0:T(8,128)(2,1)S(1)} %get-tuple-element.199), channel_id=1, source_target_pairs={{0,8},{1,9},{2,10},{3,11},{4,12},{5,13},{6,14},{7,15},{8,0},{9,1},... | collective-permute-start | bytes 786440 | tf_op jit(solution)/shard_map/ppermute | solution.py:1030
  209.1 22.0 %collective-permute-start.61 = (bf16[6144,128]{1,0:T(8,128)(2,1)}, bf16[6144,128]{1,0:T(8,128)(2,1)S(1)}, u32[]{:S(2)}, u32[]{:S(2)}) collective-permute-start(bf16[6144,128]{1,0:T(8,128)(2,1)} %get-tuple-element.254), channel_id=1, source_target_pairs={{0,1},{1,0},{2,3},{3,2},{4,5},{5,4},{6,7},{7,6},{8,9},{9,8},{10,11... | collective-permute-start | bytes 4718600 | tf_op jit(solution)/shard_map/ppermute | solution.py:1043
  231.6 20.5 %collective-permute-start.62 = (bf16[3072,128]{1,0:T(8,128)(2,1)S(1)}, bf16[3072,128]{1,0:T(8,128)(2,1)S(1)}, u32[]{:S(2)}, u32[]{:S(2)}) collective-permute-start(bf16[3072,128]{1,0:T(8,128)(2,1)S(1)} %get-tuple-element.260), channel_id=1, source_target_pairs={{0,2},{1,3},{2,0},{3,1},{4,6},{5,7},{6,4},{7,5},{8,10},{9,11},{10,... | collective-permute-start | bytes 2359304 | tf_op jit(solution)/shard_map/ppermute | solution.py:1043
  231.9 20.5 %collective-permute-start.63 = (bf16[512,256]{1,0:T(8,128)(2,1)S(1)}, bf16[512,256]{1,0:T(8,128)(2,1)S(1)}, u32[]{:S(2)}, u32[]{:S(2)}) collective-permute-start(bf16[512,256]{1,0:T(8,128)(2,1)S(1)} %get-tuple-element.220), channel_id=1, source_target_pairs={{0,4},{1,5},{2,6},{3,7},{4,0},{5,1},{6,2},{7,3},{8,12},{9,13},{10,... | collective-permute-start | bytes 786440 | tf_op jit(solution)/shard_map/ppermute | solution.py:1030
  232.7 19.8 %collective-permute-start.64 = (bf16[512,256]{1,0:T(8,128)(2,1)S(1)}, bf16[512,256]{1,0:T(8,128)(2,1)S(1)}, u32[]{:S(2)}, u32[]{:S(2)}) collective-permute-start(bf16[512,256]{1,0:T(8,128)(2,1)S(1)} %get-tuple-element.221), channel_id=1, source_target_pairs={{0,8},{1,9},{2,10},{3,11},{4,12},{5,13},{6,14},{7,15},{8,0},{9,1},... | collective-permute-start | bytes 786440 | tf_op jit(solution)/shard_map/ppermute | solution.py:1030
  234.7 17.8 %collective-permute-start.65 = (bf16[512,256]{1,0:T(8,128)(2,1)S(1)}, bf16[512,256]{1,0:T(8,128)(2,1)S(1)}, u32[]{:S(2)}, u32[]{:S(2)}) collective-permute-start(bf16[512,256]{1,0:T(8,128)(2,1)S(1)} %get-tuple-element.222), channel_id=1, source_target_pairs={{0,12},{1,13},{2,14},{3,15},{4,8},{5,9},{6,10},{7,11},{8,4},{9,5},... | collective-permute-start | bytes 786440 | tf_op jit(solution)/shard_map/ppermute | solution.py:1030
  236.5 35.0 %collective-permute-start.67 = (bf16[5632,128]{1,0:T(8,128)(2,1)S(1)}, bf16[5632,128]{1,0:T(8,128)(2,1)S(1)}, u32[]{:S(2)}, u32[]{:S(2)}) collective-permute-start(bf16[5632,128]{1,0:T(8,128)(2,1)S(1)} %get-tuple-element.227), channel_id=1, source_target_pairs={{0,1},{1,0},{2,3},{3,2},{4,5},{5,4},{6,7},{7,6},{8,9},{9,8},{10,11... | collective-permute-start | bytes 4325384 | tf_op jit(solution)/shard_map/ppermute | solution.py:1043
  272.0 16.7 %collective-permute-start.70 = (bf16[2816,128]{1,0:T(8,128)(2,1)S(1)}, bf16[2816,128]{1,0:T(8,128)(2,1)S(1)}, u32[]{:S(2)}, u32[]{:S(2)}) collective-permute-start(bf16[2816,128]{1,0:T(8,128)(2,1)S(1)} %get-tuple-element.262), channel_id=1, source_target_pairs={{0,2},{1,3},{2,0},{3,1},{4,6},{5,7},{6,4},{7,5},{8,10},{9,11},{10,... | collective-permute-start | bytes 2162696 | tf_op jit(solution)/shard_map/ppermute | solution.py:1043
  288.9 15.6 %collective-permute-start.75 = (bf16[1536,128]{1,0:T(8,128)(2,1)S(1)}, bf16[1536,128]{1,0:T(8,128)(2,1)S(1)}, u32[]{:S(2)}, u32[]{:S(2)}) collective-permute-start(bf16[1536,128]{1,0:T(8,128)(2,1)S(1)} %pad_maximum_fusion.6), channel_id=1, source_target_pairs={{0,4},{1,5},{2,6},{3,7},{4,0},{5,1},{6,2},{7,3},{8,12},{9,13},{10,... | collective-permute-start | bytes 1179656 | tf_op jit(solution)/shard_map/ppermute | solution.py:1030
  289.2 13.9 %collective-permute-start.73 = (bf16[1408,128]{1,0:T(8,128)(2,1)S(1)}, bf16[1408,128]{1,0:T(8,128)(2,1)S(1)}, u32[]{:S(2)}, u32[]{:S(2)}) collective-permute-start(bf16[1408,128]{1,0:T(8,128)(2,1)S(1)} %get-tuple-element.268), channel_id=1, source_target_pairs={{0,4},{1,5},{2,6},{3,7},{4,0},{5,1},{6,2},{7,3},{8,12},{9,13},{10,... | collective-permute-start | bytes 1081352 | tf_op jit(solution)/shard_map/ppermute | solution.py:1030
  304.6 34.8 %collective-permute-start.83 = (bf16[4,256,1024]{2,1,0:T(8,128)(2,1)S(1)}, bf16[4,256,1024]{2,1,0:T(8,128)(2,1)S(1)}, u32[]{:S(2)}, u32[]{:S(2)}) collective-permute-start(bf16[4,256,1024]{2,1,0:T(8,128)(2,1)S(1)} %get-tuple-element.243.x_ref), channel_id=1, source_target_pairs={{16,0},{17,1},{18,2},{19,3},{20,4},{21,5},{22,6},{23,7},{24,8},{25... | collective-permute-start | bytes 6291464 | tf_op jit(solution)/shard_map/ppermute | solution.py:1417
  333.3 19.6 %collective-permute-start.85 = (bf16[2816,128]{1,0:T(8,128)(2,1)S(1)}, bf16[2816,128]{1,0:T(8,128)(2,1)S(1)}, u32[]{:S(2)}, u32[]{:S(2)}) collective-permute-start(bf16[2816,128]{1,0:T(8,128)(2,1)S(1)} %pad_maximum_fusion.4), channel_id=1, source_target_pairs={{0,2},{1,3},{2,0},{3,1},{4,6},{5,7},{6,4},{7,5},{8,10},{9,11},{10,... | collective-permute-start | bytes 2162696 | tf_op jit(solution)/shard_map/ppermute | solution.py:1043
  336.0 22.8 %collective-permute-start.98 = (f32[2,5120]{1,0:T(2,128)S(1)}, f32[2,5120]{1,0:T(2,128)S(1)}, u32[]{:S(2)}, u32[]{:S(2)}) collective-permute-start(f32[2,5120]{1,0:T(2,128)S(1)} %select_add_fusion), channel_id=1, source_target_pairs={{0,4},{1,5},{2,6},{3,7},{4,0},{5,1},{6,2},{7,3},{8,12},{9,13},{10,... | collective-permute-start | bytes 122888 | tf_op jit(solution)/shard_map/ppermute | solution.py:1030
  336.1 24.8 %collective-permute-start.89 = (bf16[6144,128]{1,0:T(8,128)(2,1)S(1)}, bf16[6144,128]{1,0:T(8,128)(2,1)S(1)}, u32[]{:S(2)}, u32[]{:S(2)}) collective-permute-start(bf16[6144,128]{1,0:T(8,128)(2,1)S(1)} %pad_maximum_fusion.refs_0_), channel_id=1, source_target_pairs={{16,18},{17,19},{18,16},{19,17},{20,22},{21,23},{22,20},{23,21},{2... | collective-permute-start | bytes 4718600 | tf_op jit(solution)/shard_map/ppermute | solution.py:1081
  336.9 24.1 %collective-permute-start.88 = (bf16[6144,128]{1,0:T(8,128)(2,1)S(1)}, bf16[6144,128]{1,0:T(8,128)(2,1)S(1)}, u32[]{:S(2)}, u32[]{:S(2)}) collective-permute-start(bf16[6144,128]{1,0:T(8,128)(2,1)S(1)} %pad_maximum_fusion.refs_0_), channel_id=1, source_target_pairs={{0,17},{1,16},{2,19},{3,18},{4,21},{5,20},{6,23},{7,22},{8,25},{9,... | collective-permute-start | bytes 4718600 | tf_op jit(solution)/shard_map/ppermute | solution.py:1081
  339.4 25.5 %collective-permute-start.87 = (bf16[6144,128]{1,0:T(8,128)(2,1)S(1)}, bf16[6144,128]{1,0:T(8,128)(2,1)S(1)}, u32[]{:S(2)}, u32[]{:S(2)}) collective-permute-start(bf16[6144,128]{1,0:T(8,128)(2,1)S(1)} %pad_maximum_fusion.refs_0_), channel_id=1, source_target_pairs={{0,16},{1,17},{2,18},{3,19},{4,20},{5,21},{6,22},{7,23},{8,24},{9,... | collective-permute-start | bytes 4718600 | tf_op jit(solution)/shard_map/ppermute | solution.py:1081
  358.0 19.8 %collective-permute-start.93 = (bf16[5632,128]{1,0:T(8,128)(2,1)S(1)}, bf16[5632,128]{1,0:T(8,128)(2,1)S(1)}, u32[]{:S(2)}, u32[]{:S(2)}) collective-permute-start(bf16[5632,128]{1,0:T(8,128)(2,1)S(1)} %pad_maximum_fusion.1.refs_1_), channel_id=1, source_target_pairs={{16,18},{17,19},{18,16},{19,17},{20,22},{21,23},{22,20},{23,21},{2... | collective-permute-start | bytes 4325384 | tf_op jit(solution)/shard_map/ppermute | solution.py:1081
  358.8 15.4 %collective-permute-start.90 = (bf16[1088,128]{1,0:T(8,128)(2,1)S(1)}, bf16[1088,128]{1,0:T(8,128)(2,1)S(1)}, u32[]{:S(2)}, u32[]{:S(2)}) collective-permute-start(bf16[1088,128]{1,0:T(8,128)(2,1)S(1)} %pad_maximum_fusion.8), channel_id=1, source_target_pairs={{0,2},{1,3},{2,0},{3,1},{4,6},{5,7},{6,4},{7,5},{8,10},{9,11},{10,... | collective-permute-start | bytes 835592 | tf_op jit(solution)/shard_map/ppermute | solution.py:1043
  360.9 15.6 %collective-permute-start.99 = (f32[2,5120]{1,0:T(2,128)S(1)}, f32[2,5120]{1,0:T(2,128)S(1)}, u32[]{:S(2)}, u32[]{:S(2)}) collective-permute-start(f32[2,5120]{1,0:T(2,128)S(1)} %fusion.8), channel_id=1, source_target_pairs={{0,8},{1,9},{2,10},{3,11},{4,12},{5,13},{6,14},{7,15},{8,0},{9,1},... | collective-permute-start | bytes 122888 | tf_op jit(solution)/shard_map/ppermute | solution.py:1030
  361.0 20.3 %collective-permute-start.92 = (bf16[5632,128]{1,0:T(8,128)(2,1)S(1)}, bf16[5632,128]{1,0:T(8,128)(2,1)S(1)}, u32[]{:S(2)}, u32[]{:S(2)}) collective-permute-start(bf16[5632,128]{1,0:T(8,128)(2,1)S(1)} %pad_maximum_fusion.1.refs_1_), channel_id=1, source_target_pairs={{0,17},{1,16},{2,19},{3,18},{4,21},{5,20},{6,23},{7,22},{8,25},{9,... | collective-permute-start | bytes 4325384 | tf_op jit(solution)/shard_map/ppermute | solution.py:1081
  364.9 16.4 %collective-permute-start.91 = (bf16[5632,128]{1,0:T(8,128)(2,1)S(1)}, bf16[5632,128]{1,0:T(8,128)(2,1)S(1)}, u32[]{:S(2)}, u32[]{:S(2)}) collective-permute-start(bf16[5632,128]{1,0:T(8,128)(2,1)S(1)} %pad_maximum_fusion.1.refs_1_), channel_id=1, source_target_pairs={{0,16},{1,17},{2,18},{3,19},{4,20},{5,21},{6,22},{7,23},{8,24},{9,... | collective-permute-start | bytes 4325384 | tf_op jit(solution)/shard_map/ppermute | solution.py:1081
  (83 other events, 566.3 us)
